TPU v7x, 32 devices: a whole 2x2x4 slice. The times are simulated.
32 devices in a mesh: row: 4 (over z), col: 8 (over y, x, core).
Axes of the slice: x: 2, y: 2, z: 4, core: 2. Of those that a mesh axis runs over, the one named last changes fastest.
Arguments:
- pair: bfloat16 [256, 256, 128], P('row', 'col'), may hold values from -24 to 24
- token_mask: int32 [256], replicated, may hold values 0 or 1
- ln_gain: float32 [128], replicated, may hold values from 0.5 to 1.5
- ln_shift: float32 [128], replicated, may hold values from -3 to 3
- w_qkv: bfloat16 [128, 384], replicated, may hold values from -1 to 1
- w_bias: bfloat16 [128, 4], replicated, may hold values from -12 to 12
- w_gate: bfloat16 [128, 128], replicated, may hold values from -0.5 to 0.5
- gate_bias: float32 [128], replicated, may hold values from -4 to 4
- w_out: bfloat16 [128, 128], replicated, may hold values from -0.5 to 0.5
- out_bias: float32 [128], replicated, may hold values from -3 to 3
Outputs:
- update: bfloat16 [256, 256, 128], P('row', 'col')
All inputs are finite; a program needn't handle non-finite values.
Results may differ from a plain program's by a relative error of at most 0.001.
The roundings to bfloat16 on the way count: a program that leaves them out, or rounds other values in their place, can miss the bound.
Values may be sent and summed in bfloat16 or wider, within the bound.
No kernel may reach another device: no remote copies, remote signals or barrier semaphores. Data moves between devices by JAX's collectives and lax.ppermute only.
A program may use at most 192 MiB of HBM per device.

v0:
```python
import jax
import jax.numpy as jnp
from jax import lax
from jax.sharding import PartitionSpec as P


def layer_norm(pair, ln_gain, ln_shift):
    values = pair.astype(jnp.float32)
    mean = jnp.mean(values, -1, keepdims=True)
    centred = values - mean
    var = jnp.mean(centred * centred, -1, keepdims=True)
    return (centred * lax.rsqrt(var + 1e-05) * ln_gain + ln_shift).astype(jnp.bfloat16)


def softmax_rounded(scores):
    top = jnp.max(scores, -1, keepdims=True)
    expo = jnp.exp(scores - top)
    return (expo / jnp.sum(expo, -1, keepdims=True)).astype(jnp.bfloat16)


def per_device(
    pair, token_mask, ln_gain, ln_shift, w_qkv, w_bias, w_gate, gate_bias, w_out, out_bias
):
    rows, cols, chans = pair.shape
    heads = w_bias.shape[1]
    inner = w_gate.shape[1]
    head = inner // heads
    row_count = lax.axis_size("row")
    col_count = lax.axis_size("col")
    count = rows * row_count
    normed = layer_norm(pair, ln_gain, ln_shift).reshape(rows * cols, chans)
    mixed = jnp.dot(normed, w_qkv, preferred_element_type=jnp.float32)
    qscale = jnp.where(jnp.arange(3 * inner) < inner, head ** (-0.5), 1.0).astype(jnp.float32)
    qkv = (mixed * qscale).astype(jnp.bfloat16).reshape(rows, cols, 3 * inner)
    bias_tile = jnp.dot(normed, w_bias, preferred_element_type=jnp.float32).astype(jnp.bfloat16)
    gate = jax.nn.sigmoid(jnp.dot(normed, w_gate, preferred_element_type=jnp.float32) + gate_bias)
    gathered = lax.all_gather(
        bias_tile.reshape(1, rows * cols * heads), ("row", "col"), axis=0, tiled=True
    )
    bias_t = (
        gathered.reshape(row_count, col_count, rows, cols, heads)
        .transpose(4, 1, 3, 0, 2)
        .reshape(heads, count, count)
    )
    key_bias = jnp.where(token_mask == 1, 0.0, -1000000000.0).astype(jnp.float32)
    width = cols // row_count
    packed = qkv.reshape(rows, row_count, width * 3 * inner)
    moved = lax.all_to_all(packed, "row", split_axis=1, concat_axis=0, tiled=True).reshape(
        count, width, 3, heads, head
    )

    def one_column(index):
        column_index = index // heads
        head_index = index % heads
        column = lax.dynamic_index_in_dim(moved, column_index, 1, keepdims=False)
        column = lax.dynamic_index_in_dim(column, head_index, 2, keepdims=False)
        query = column[:, 0]
        keys = column[:, 1]
        vals = column[:, 2]
        scores = jnp.einsum("ad,kd->ak", query, keys, preferred_element_type=jnp.float32)
        head_bias = lax.dynamic_index_in_dim(bias_t, head_index, 0, keepdims=False)
        scores = scores + head_bias.astype(jnp.float32) + key_bias
        weights = softmax_rounded(scores)
        return jnp.dot(weights, vals, preferred_element_type=jnp.float32).astype(jnp.bfloat16)

    outputs = lax.map(one_column, jnp.arange(width * heads, dtype=jnp.int32))
    outgoing = (
        outputs.reshape(width, heads, count, head)
        .transpose(2, 0, 1, 3)
        .reshape(count, 1, width * inner)
    )
    returned = lax.all_to_all(outgoing, "row", split_axis=0, concat_axis=1, tiled=True)
    attended = returned.reshape(rows * cols, inner)
    gated = (gate * attended.astype(jnp.float32)).astype(jnp.bfloat16)
    update = jnp.dot(gated, w_out, preferred_element_type=jnp.float32) + out_bias
    return update.astype(jnp.bfloat16).reshape(rows, cols, chans)


def solution(mesh):
    in_specs = (P("row", "col", None), P(), P(), P(), P(), P(), P(), P(), P(), P())
    out_specs = P("row", "col", None)
    return jax.shard_map(
        per_device, mesh=mesh, in_specs=in_specs, out_specs=out_specs, check_vma=False
    )
```

profile of v0, /device:TPU:0, one launch (start us, length us, event | category | flops | bytes accessed | tf_op | source)
XLA Modules:
  0.0 326.7 jit_solution(15556335744917127674)
XLA Ops:
  0.0 1.4 convert_reduce_fusion
  1.5 1.7 fusion.15
  3.2 1.3 fusion.18
  6.2 1.6 copy.26
  7.9 6.5 %all-to-all-start = ((bf16[64,4,3072]{2,0,1:T(8,128)(2,1)}), bf16[64,4,3072]{2,0,1:T(8,128)(2,1)}, u32[]{:S(2)}, u32[]{:S(2)}) async-start(bf16[64,4,3072]{2,0,1:T(8,128)(2,1)} %copy.26), calls=%async_computation | async-start | bytes 3145728 | tf_op jit(solution)/shard_map/all_to_all | solution.py:48
  15.7 62.2 %all-gather = bf16[32,1,8192]{2,1,0:T(2,128)(2,1)S(1)} all-gather(bf16[1,1,8192]{2,1,0:T(2,128)(2,1)S(1)} %reshape.70), channel_id=1, replica_groups=mesh['row'=4,'col'=8] {'row','col'}, dimensions={0}, use_global_device_ids=true | all-gather | bytes 540672 | tf_op jit(solution)/shard_map/all_gather | solution.py:37
  77.9 1.4 copy.29
  79.4 6.1 %reshape.62 = bf16[4,8,64,32,4]{1,0,4,3,2:T(4,128)(2,1)} reshape(bf16[32,1,8192]{0,2,1:T(8,128)(2,1)S(1)} %copy.29) | data formatting | bytes 1048576 | tf_op jit(solution)/shard_map/reshape | solution.py:41
  85.5 11.7 %copy.30 = bf16[4,8,32,4,64]{4,3,2,1,0:T(4,128)(2,1)S(1)} copy(bf16[4,8,32,4,64]{1,3,0,2,4:T(4,128)(2,1)} %bitcast.63) | data formatting | bytes 1048576 | tf_op jit(solution)/shard_map/transpose | solution.py:42
  97.2 1.5 reshape.63
  98.7 4.2 %copy.27 = bf16[4,64,1,3072]{1,0,3,2:T(4,128)(2,1)S(1)} copy(bf16[4,64,1,3072]{3,1,0,2:T(8,128)(2,1)} %bitcast.9) | data formatting | bytes 3145728 | tf_op jit(solution)/shard_map/all_to_all | solution.py:48
  102.9 3.0 reshape.60
  105.8 194.2 %while.13 = (s32[]{:T(128)}, bf16[32,256,32]{1,2,0:T(8,128)(2,1)}, s32[32]{0:T(128)S(1)}, bf16[256,8,3,4,32]{0,4,3,2,1:T(8,128)(2,1)}, bf16[4,256,256]{2,1,0:T(8...) while((s32[]{:T(128)}, bf16[32,256,32]{1,2,0:T(8,128)(2,1)}, ...), condition=%wide.region_5.6_spmd, body=%wide.region_2.5_spmd.sunk | while | flops 8986141 | bytes 1612732 | solution.py:66
  108.3 0.9 constant_dynamic-slice_fusion.2
  114.4 0.9 constant_dynamic-slice_fusion.2
  120.5 0.9 constant_dynamic-slice_fusion.2
  132.6 0.9 constant_dynamic-slice_fusion.2
  138.7 0.9 constant_dynamic-slice_fusion.2
  144.7 0.9 constant_dynamic-slice_fusion.2
  156.9 0.9 constant_dynamic-slice_fusion.2
  162.9 0.9 constant_dynamic-slice_fusion.2
  300.6 2.0 reduce
  303.1 19.6 %all_to_all.24 = bf16[4,2,32768]{2,1,0:T(2,128)(2,1)S(1)} all-to-all(bf16[4,2,32768]{2,1,0:T(2,128)(2,1)S(1)} %reshape.74), channel_id=1, replica_groups=mesh['row'=4,'col'=8] {'row'}, dimensions={0} | all-to-all | bytes 1048576 | tf_op jit(solution)/shard_map/all_to_all | solution.py:72
  325.3 1.3 fusion.12
  (258 shorter events, 112.2 us)
Async XLA Ops:
  0.0 5.3 %copy-start = (bf16[128,384]{1,0:T(8,128)(2,1)S(1)}, bf16[128,384]{1,0:T(8,128)(2,1)}, u32[]{:S(2)}) copy-start(bf16[128,384]{1,0:T(8,128)(2,1)} %param.16) | copy-start | bytes 294916
  0.0 3.2 copy-start.1
  4.5 0.8 copy-start.2
  7.9 6.5 %copy-start.3 = (bf16[64,32,128]{2,1,0:T(8,128)(2,1)S(1)}, bf16[64,32,128]{2,1,0:T(8,128)(2,1)}, u32[]{:S(2)}) copy-start(bf16[64,32,128]{2,1,0:T(8,128)(2,1)} %copy-done.2) | copy-start | bytes 1572868
  7.9 6.5 %copy-start.5 = (bf16[128,4]{0,1:T(4,128)(2,1)S(1)}, bf16[128,4]{0,1:T(4,128)(2,1)}, u32[]{:S(2)}) copy-start(bf16[128,4]{0,1:T(4,128)(2,1)} %param.17) | copy-start | bytes 3076
  7.9 90.8 %all-to-all-start = ((bf16[64,4,3072]{2,0,1:T(8,128)(2,1)}), bf16[64,4,3072]{2,0,1:T(8,128)(2,1)}, u32[]{:S(2)}, u32[]{:S(2)}) async-start(bf16[64,4,3072]{2,0,1:T(8,128)(2,1)} %copy.26), calls=%async_computation | async-start | bytes 3145728 | tf_op jit(solution)/shard_map/all_to_all | solution.py:48
  97.2 1.5 copy-start.6
  324.3 1.0 copy-start.4
  324.3 1.0 copy-start.7
  324.3 1.0 copy-start.8
  324.3 1.0 copy-start.9
  324.3 1.0 copy-start.10
where the time goes:
time: 331 us; the launch traced here: 327 us
  local copies, waits for them, and re-layouts  113 us (34%)
  blocking collectives  81.8 us (25%)
  loops' own time  81.4 us (25%)
  matrix products  35.2 us (11%)
  other arithmetic  8.84 us (3%)
  starting transfers between devices  6.45 us (2%)
    another operation x1, loops' own time, per_device(): outputs = lax.map(one_column, jnp.arange(width * heads, dtype=jnp.int32))  81.4 us
    all_gather x1, blocking collectives, per_device(): lax.all_gather(bias_tile.reshape(1, rows * cols * heads), ('row', 'col'),...  62.2 us
    dynamic_slice x64, local copies, waits for them, and re-layouts, one_column(): head_bias = lax.dynamic_index_in_dim(bias_t, head_index, 0, keepdims=False)  32.5 us
    squeeze x32, local copies, waits for them, and re-layouts, one_column(): column = lax.dynamic_index_in_dim(column, head_index, 2, keepdims=False)  26 us
    dot_general x32, matrix products, one_column(): jnp.dot(weights, vals, preferred_element_type=jnp.float32)  24.8 us
    all_to_all x1, blocking collectives, per_device(): lax.all_to_all(outgoing, 'row', split_axis=0, concat_axis=1, tiled=True)  19.6 us
    dynamic_slice x32, local copies, waits for them, and re-layouts, per_device(): outputs = lax.map(one_column, jnp.arange(width * heads, dtype=jnp.int32))  18.9 us
    transpose x1, local copies, waits for them, and re-layouts, per_device(): bias_t = gathered.reshape(row_count, col_count, rows, cols, heads).transp...  11.7 us
  transfers between devices with their start and end apart: 1, of which 0 were waited for; matrix products, arithmetic and copies ran while one was open for 7% of the time, Pallas kernels for 0%

commit v1 on v0

v1 whole, which is shorter than its diff:
```python
import functools

import jax
import jax.numpy as jnp
from jax import lax
from jax.experimental import pallas as pl
from jax.experimental.pallas import tpu as pltpu
from jax.sharding import PartitionSpec as P

BF = jnp.bfloat16
F32 = jnp.float32
VMEM_LIMIT = 52 * 1024 * 1024


def dot(a, b):
    return jnp.dot(a, b, preferred_element_type=F32)


def dot_t(a, b):
    return lax.dot_general(a, b, (((1,), (1,)), ((), ())), preferred_element_type=F32)


def transposed(a):
    return a.astype(F32).T.astype(BF)


def column_of(row, width):
    return jnp.broadcast_to(row, (width, row.shape[1])).T


def split_sum(a, ones):
    first = a.astype(BF)
    rest = a - first.astype(F32)
    second = rest.astype(BF)
    third = (rest - second.astype(F32)).astype(BF)
    return dot(first, ones) + dot(second, ones) + dot(third, ones)


def prep_kernel(pair_ref, gain_ref, shift_ref, wb_ref, *refs):
    chunks, tile_ref, wide = refs[:-2], refs[-2], refs[-1]
    rows, cols, chans = pair_ref.shape
    heads = wb_ref.shape[0]
    lanes = heads * cols
    parts = len(chunks)
    width = cols // parts
    me = lax.axis_index("row")
    ones = jnp.ones((chans, chans), BF)
    head_of = lax.broadcasted_iota(jnp.int32, (lanes, heads), 0) // cols
    spread = (head_of == lax.broadcasted_iota(jnp.int32, (lanes, heads), 1)).astype(BF)
    wb = dot(spread, wb_ref[...]).astype(BF)
    lane_col = lax.broadcasted_iota(jnp.int32, (cols, lanes), 1) % cols
    keep = lane_col == lax.broadcasted_iota(jnp.int32, (cols, lanes), 0)
    gain = gain_ref[...]
    shift = shift_ref[...]
    step = min(rows, 16)

    def body(index, carry):
        start = pl.multiple_of(index * step, step)
        raw = pair_ref[pl.ds(start, step)].reshape(step * cols, chans)
        mean = dot(raw, ones) * (1.0 / chans)
        centred = raw.astype(F32) - mean
        var = split_sum(centred * centred, ones) * (1.0 / chans)
        normed = (centred * lax.rsqrt(var + 1e-05) * gain + shift).astype(BF)
        wide[pl.ds(pl.multiple_of(index * step * cols, step * cols), step * cols), :] = normed.astype(F32)
        every = dot_t(normed, wb).reshape(step, cols, lanes)
        tile = jnp.sum(jnp.where(keep[None], every, 0.0), axis=1)
        tile_ref[pl.ds(start, step), :] = tile.astype(BF)
        return carry

    lax.fori_loop(0, rows // step, body, 0)
    for s in range(parts):
        first = (me ^ s) * width
        for j in range(width):
            chunks[s][j] = wide[pl.ds(first + j, rows, stride=cols), :].astype(BF)


def attend_kernel(parts, *refs):
    pieces = refs[:parts]
    bias_a, bias_b, mask_ref, wqkv_ref, wg_ref, gb_ref, wo_ref, ob_ref = refs[parts : parts + 8]
    outs = refs[parts + 8 : 2 * parts + 8]
    normed, update, tiles, bias, key_bias, wt, queries, keys, vals, heard, gates, sem_p, sem_b, sem_o = refs[2 * parts + 8 :]
    width, rows, chans = pieces[0].shape
    pairs, _, _, lanes = bias_a.shape
    heads = bias.shape[0]
    count = bias.shape[1]
    cols = lanes // heads
    inner = wg_ref.shape[1]
    head = inner // heads
    me = lax.axis_index("row")
    col = lax.axis_index("col")

    bias_copies = []
    for k, source in enumerate((bias_a, bias_b)):
        for t in range(pairs):
            copy = pltpu.make_async_copy(
                source.at[t], tiles.at[col ^ (2 * t + k)], sem_b.at[k * pairs + t]
            )
            copy.start()
            bias_copies.append(copy)
    piece_copies = []
    for s in range(parts):
        copy = pltpu.make_async_copy(pieces[s], normed.at[me ^ s], sem_p.at[s])
        copy.start()
        piece_copies.append(copy)

    wt[0:inner] = transposed(wqkv_ref[:, 2 * inner : 3 * inner])
    wt[inner : 2 * inner] = transposed(wg_ref[...])
    wt[2 * inner : 2 * inner + chans] = transposed(wo_ref[...])
    gate_bias = column_of(gb_ref[...], 128)[:, 0:1]
    out_bias = column_of(ob_ref[...], 128)[:, 0:1]
    key_bias[...] = jnp.where(column_of(mask_ref[...], 128) == 1, 0.0, -1000000000.0).astype(F32)

    for copy in bias_copies:
        copy.wait()
    group = 128 // cols
    span = group * lanes
    source_lane = lax.broadcasted_iota(jnp.int32, (span, span), 0)
    target_lane = lax.broadcasted_iota(jnp.int32, (span, span), 1)
    tile_of, rest = source_lane // lanes, source_lane % lanes
    wanted = (rest // cols) * 128 + tile_of * cols + rest % cols
    order = (wanted == target_lane).astype(BF)
    groups = count // 128

    batch = max(1, min(count, 256) // rows)

    def one_block(index, carry):
        g, b = index // (parts // batch), index % (parts // batch)
        block = jnp.concatenate(
            [
                tiles[g * group + t, pl.ds(b * batch, batch)].reshape(batch * rows, lanes)
                for t in range(group)
            ],
            axis=1,
        )
        ordered = dot(block, order)
        across = pl.ds(pl.multiple_of(g * 128, 128), 128)
        for s in range(batch):
            at = pl.ds(pl.multiple_of((me ^ (b * batch + s)) * rows, rows), rows)
            for h in range(heads):
                bias[h, at, across] = (
                    ordered[s * rows : (s + 1) * rows, h * 128 : (h + 1) * 128] + key_bias[at, :]
                )
        return carry

    blocks = groups * (parts // batch)
    lax.fori_loop(0, blocks, one_block, 0, unroll=blocks <= 2)

    for copy in piece_copies:
        copy.wait()
    lane_head = lax.broadcasted_iota(jnp.int32, (1, inner), 1) // head
    wide = heard.shape[1]

    def one_column(j, carry):
        tokens = normed[:, j].reshape(count, chans)
        mixed = dot(tokens, wqkv_ref[:, 0 : 2 * inner])
        query = (mixed[:, 0:inner] * (head ** (-0.5))).astype(BF)
        keys[...] = mixed[:, inner : 2 * inner].astype(BF)
        vals_gate = dot_t(wt[0 : 2 * inner], tokens)
        vals[...] = vals_gate[0:inner].astype(BF)
        queries[...] = query
        gates[...] = jax.nn.sigmoid(vals_gate[inner : 2 * inner] + gate_bias)

        def one_part(g, inside):
            lo = pl.multiple_of(g * wide, wide)
            some = queries[pl.ds(lo, wide), :]

            def one_head(h, within):
                at = pl.ds(pl.multiple_of(h * head, head), head)
                head_keys = jnp.where(lane_head == h, keys[...], jnp.zeros_like(keys))
                scores = dot_t(head_keys, some) + bias[h, :, pl.ds(lo, wide)]
                top = jnp.max(scores, axis=0, keepdims=True)
                expo = jnp.exp(scores - top)
                total = jnp.sum(expo, axis=0, keepdims=True)
                weights = (expo * (1.0 / total)).astype(BF)
                heard[at, :] = dot(vals[at, :], weights)
                return within

            lax.fori_loop(0, heads, one_head, 0, unroll=count == wide)
            attended = heard[...].astype(BF).astype(F32)
            gated = (gates[:, pl.ds(lo, wide)] * attended).astype(BF)
            result = dot(wt[2 * inner : 2 * inner + chans], gated) + out_bias
            result = result.T.astype(BF)
            for p in range(wide // rows):
                update[g * (wide // rows) + p, j] = result[p * rows : (p + 1) * rows]
            return inside

        lax.fori_loop(0, count // wide, one_part, 0, unroll=count == wide)
        return carry

    lax.fori_loop(0, width, one_column, 0)
    out_copies = []
    for s in range(parts):
        copy = pltpu.make_async_copy(update.at[me ^ s], outs[s], sem_o.at[s])
        copy.start()
        out_copies.append(copy)
    for copy in out_copies:
        copy.wait()


def place_kernel(*refs):
    pieces, out_ref, wide = refs[:-2], refs[-2], refs[-1]
    rows, cols, chans = out_ref.shape
    width = cols // len(pieces)
    me = lax.axis_index("row")
    for s, piece in enumerate(pieces):
        first = (me ^ s) * width

        def one_column(j, carry, first=first, piece=piece):
            wide[pl.ds(first + j, rows, stride=cols), :] = piece[j].astype(F32)
            return carry

        lax.fori_loop(0, width, one_column, 0, unroll=rows <= 64)
    step = min(rows, 16)

    def body(index, carry):
        lines = wide[pl.ds(pl.multiple_of(index * step * cols, step * cols), step * cols), :]
        out_ref[pl.ds(index * step, step)] = lines.astype(BF).reshape(step, cols, chans)
        return carry

    lax.fori_loop(0, rows // step, body, 0)


def per_device(
    pair, token_mask, ln_gain, ln_shift, w_qkv, w_bias, w_gate, gate_bias, w_out, out_bias
):
    rows, cols, chans = pair.shape
    heads = w_bias.shape[1]
    inner = w_gate.shape[1]
    parts = lax.axis_size("row")
    col_count = lax.axis_size("col")
    count = rows * parts
    width = cols // parts
    lanes = heads * cols
    lane_part = 256 if count <= 256 else 128
    chunk = jax.ShapeDtypeStruct((width, rows, chans), BF)
    vmem = pl.BlockSpec(memory_space=pltpu.VMEM)
    anywhere = pl.BlockSpec(memory_space=pl.ANY)
    params = pltpu.CompilerParams(vmem_limit_bytes=VMEM_LIMIT)

    def swap(x, axis, offset):
        size = lax.axis_size(axis)
        return lax.ppermute(x, axis, [(i, i ^ offset) for i in range(size)])

    *chunks, tile = pl.pallas_call(
        prep_kernel,
        out_shape=[chunk] * parts + [jax.ShapeDtypeStruct((rows, lanes), BF)],
        in_specs=[vmem] * 4,
        out_specs=[vmem] * (parts + 1),
        scratch_shapes=[pltpu.VMEM((rows * cols, chans), F32)],
        compiler_params=params,
        name="prep",
    )(pair, ln_gain.reshape(1, chans), ln_shift.reshape(1, chans), w_bias.T)

    by_row = jnp.stack([tile] + [swap(tile, "row", s) for s in range(1, parts)])
    pieces = [chunks[0]] + [swap(chunks[s], "row", s) for s in range(1, parts)]
    by_chip = jnp.stack([by_row] + [swap(by_row, "col", 2 * t) for t in range(1, col_count // 2)])
    other = swap(by_chip, "col", 1)

    returned = pl.pallas_call(
        functools.partial(attend_kernel, parts),
        out_shape=[chunk] * parts,
        in_specs=[anywhere] * (parts + 2) + [vmem] * 6,
        out_specs=[anywhere] * parts,
        scratch_shapes=[
            pltpu.VMEM((parts, width, rows, chans), BF),
            pltpu.VMEM((parts, width, rows, chans), BF),
            pltpu.VMEM((col_count, parts, rows, lanes), BF),
            pltpu.VMEM((heads, count, count), F32),
            pltpu.VMEM((count, 128), F32),
            pltpu.VMEM((2 * inner + chans, chans), BF),
            pltpu.VMEM((count, inner), BF),
            pltpu.VMEM((count, inner), BF),
            pltpu.VMEM((inner, count), BF),
            pltpu.VMEM((inner, lane_part), F32),
            pltpu.VMEM((inner, count), F32),
            pltpu.SemaphoreType.DMA((parts,)),
            pltpu.SemaphoreType.DMA((col_count,)),
            pltpu.SemaphoreType.DMA((parts,)),
        ],
        compiler_params=params,
        name="attend",
    )(
        *pieces,
        by_chip,
        other,
        token_mask.reshape(1, count),
        w_qkv,
        w_gate,
        gate_bias.reshape(1, inner),
        w_out,
        out_bias.reshape(1, chans),
    )
    back = [returned[0]] + [swap(returned[s], "row", s) for s in range(1, parts)]
    return pl.pallas_call(
        place_kernel,
        out_shape=jax.ShapeDtypeStruct((rows, cols, chans), BF),
        in_specs=[vmem] * parts,
        out_specs=vmem,
        scratch_shapes=[pltpu.VMEM((rows * cols, chans), F32)],
        compiler_params=params,
        name="place",
    )(*back)


def solution(mesh):
    in_specs = (P("row", "col", None), P(), P(), P(), P(), P(), P(), P(), P(), P())
    out_specs = P("row", "col", None)
    return jax.shard_map(
        per_device, mesh=mesh, in_specs=in_specs, out_specs=out_specs, check_vma=False
    )
```

time: 331 us -> 72.1 us (0.22); the launches traced: 327 us -> 72 us
  local copies, waits for them, and re-layouts: 113 us -> 2.4 us
  blocking collectives: 81.8 us -> 0 us
  loops' own time: 81.4 us -> 0 us
  matrix products: 35.2 us -> 0 us
  waiting for transfers between devices: 0.01 us -> 26.8 us
  Pallas kernels: 0 us -> 22.8 us
  starting transfers between devices: 6.45 us -> 19.8 us
  other arithmetic: 8.84 us -> 0.05 us
    another operation x1 -> x0, loops' own time: 81.4 us -> none  [per_device(): outputs = lax.map(one_column, jnp.arange(width * heads, dtype=jnp.int32))]
    all_gather x1 -> x0, blocking collectives: 62.2 us -> none  [per_device(): lax.all_gather(bias_tile.reshape(1, rows * cols * heads), ('row', 'col'),...]
    dynamic_slice x96 -> x0, local copies, waits for them, and re-layouts: 51.4 us -> none  [the longest x64 32.5 us: one_column(): head_bias = lax.dynamic_index_in_dim(bias_t, head_index, 0, keepdims=False)]
    dot_general x67 -> x0, matrix products: 35.2 us -> none  [the longest x32 24.8 us: one_column(): jnp.dot(weights, vals, preferred_element_type=jnp.float32)]
    ppermute x0 -> x13, waiting for transfers between devices: none -> 26.8 us  [swap(): return lax.ppermute(x, axis, [(i, i ^ offset) for i in range(size)])]
    squeeze x32 -> x0, local copies, waits for them, and re-layouts: 26 us -> none  [one_column(): column = lax.dynamic_index_in_dim(column, head_index, 2, keepdims=False)]
    pallas_call x0 -> x3, Pallas kernels: none -> 22.8 us  [the longest x1 17.8 us: per_device(): pl.pallas_call(functools.partial(attend_kernel, parts), out_shape=[chunk]...]
    ppermute x0 -> x13, starting transfers between devices: none -> 19.8 us  [swap(): return lax.ppermute(x, axis, [(i, i ^ offset) for i in range(size)])]
  transfers between devices with their start and end apart: 1 -> 13, of which waited for: 0 -> 9; matrix products, arithmetic and copies ran while one was open for 7% -> 0% of each run, Pallas kernels for 0% -> 0%
where the time goes in v1:
time: 72.1 us; the launch traced here: 72 us
  waiting for transfers between devices  26.8 us (37%)
  Pallas kernels  22.8 us (32%)
  starting transfers between devices  19.8 us (27%)
  local copies, waits for them, and re-layouts  2.4 us (3%)
    ppermute x13, waiting for transfers between devices, swap(): return lax.ppermute(x, axis, [(i, i ^ offset) for i in range(size)])  26.8 us
    ppermute x13, starting transfers between devices, swap(): return lax.ppermute(x, axis, [(i, i ^ offset) for i in range(size)])  19.8 us
    pallas_call x1, Pallas kernels, per_device(): pl.pallas_call(functools.partial(attend_kernel, parts), out_shape=[chunk]...  17.8 us
    pallas_call x1, Pallas kernels, per_device(): pl.pallas_call(prep_kernel, out_shape=[chunk] * parts + [jax.ShapeDtypeSt...  3.14 us
    unnamed x20, local copies, waits for them, and re-layouts  2.4 us
    pallas_call x1, Pallas kernels, per_device(): pl.pallas_call(place_kernel, out_shape=jax.ShapeDtypeStruct((rows, cols,...  1.8 us
  transfers between devices with their start and end apart: 13, of which 9 were waited for; matrix products, arithmetic and copies ran while one was open for 0% of the time, Pallas kernels for 0%

profile of v1, /device:TPU:0, one launch (start us, length us, event | category | flops | bytes accessed | tf_op | source)
XLA Modules:
  0.0 72.0 jit_solution(6357196584237247210)
XLA Ops:
  0.0 0.6 copy-done.9
  0.7 1.0 %copy-done = bf16[64,32,128]{2,1,0:T(8,128)(2,1)S(1)} copy-done((bf16[64,32,128]{2,1,0:T(8,128)(2,1)S(1)}, bf16[64,32,128]{2,1,0:T(8,128)(2,1)}, u32[]{:S(2)}) %copy-start) | copy-done | bytes 524312
  1.7 3.1 %prep.1 = (bf16[8,64,128]{2,1,0:T(8,128)(2,1)S(1)}, bf16[8,64,128]{2,1,0:T(8,128)(2,1)S(1)}, bf16[8,64,128]{2,1,0:T(8,128)(2,1)S(1)}, bf16[8,64,128]{2,1,0:T(8,128)(2,1)S(1)}, bf16[64,128]{1,0:T(8,128)(2,1)S(1)}) custom-call(bf16[64,32,128]{2,1,0:T(8,128)(2,1)S(1)} %copy-done, f32[1,128]{1,0:T(1,128)S(1)} %bitcast.20, f32[1,128]{1,0:T(1,128)S(1)} %bitcast.21, ...), custom_call_target="tpu_custom_call" | custom-call | tf_op jit(solution)/shard_map/prep/pallas_call | solution.py:244
  4.9 5.1 %collective-permute-start.5 = (bf16[64,128]{1,0:T(8,128)(2,1)S(1)}, bf16[64,128]{1,0:T(8,128)(2,1)S(1)}, u32[]{:S(2)}, u32[]{:S(2)}) collective-permute-start(bf16[64,128]{1,0:T(8,128)(2,1)S(1)} %get-tuple-element.18), channel_id=1, source_target_pairs={{0,24},{8,16},{16,8},{24,0},{1,25},{9,17},{17,9},{25,1},{2,26},{10... | collective-permute-start | bytes 49160 | tf_op jit(solution)/shard_map/ppermute | solution.py:242
  10.0 0.6 collective-permute-start.3
  10.6 1.1 %collective-permute-done.5 = bf16[64,128]{1,0:T(8,128)(2,1)S(1)} collective-permute-done((bf16[64,128]{1,0:T(8,128)(2,1)S(1)}, bf16[64,128]{1,0:T(8,128)(2,1)S(1)}, u32[]{:S(2)}, u32[]{:S(2)}) %collective-permute-start.5) | collective-permute-done | bytes 16416 | tf_op jit(solution)/shard_map/ppermute | solution.py:242
  11.7 2.9 %collective-permute-done.4 = bf16[64,128]{1,0:T(8,128)(2,1)S(1)} collective-permute-done((bf16[64,128]{1,0:T(8,128)(2,1)S(1)}, bf16[64,128]{1,0:T(8,128)(2,1)S(1)}, u32[]{:S(2)}, u32[]{:S(2)}) %collective-permute-start.4) | collective-permute-done | bytes 16416 | tf_op jit(solution)/shard_map/ppermute | solution.py:242
  14.7 1.6 %collective-permute-start.7 = (bf16[4,64,128]{2,1,0:T(8,128)(2,1)S(1)}, bf16[4,64,128]{2,1,0:T(8,128)(2,1)S(1)}, u32[]{:S(2)}, u32[]{:S(2)}) collective-permute-start(bf16[4,64,128]{2,1,0:T(8,128)(2,1)S(1)} %get-tuple-element.24), channel_id=1, source_target_pairs={{0,4},{1,5},{2,6},{3,7},{4,0},{5,1},{6,2},{7,3},{8,12},{9,13},{10,... | collective-permute-start | bytes 196616 | tf_op jit(solution)/shard_map/ppermute | solution.py:242
  16.2 1.5 %collective-permute-start.6 = (bf16[4,64,128]{2,1,0:T(8,128)(2,1)S(1)}, bf16[4,64,128]{2,1,0:T(8,128)(2,1)S(1)}, u32[]{:S(2)}, u32[]{:S(2)}) collective-permute-start(bf16[4,64,128]{2,1,0:T(8,128)(2,1)S(1)} %get-tuple-element.24), channel_id=1, source_target_pairs={{0,2},{1,3},{2,0},{3,1},{4,6},{5,7},{6,4},{7,5},{8,10},{9,11},{10,... | collective-permute-start | bytes 196616 | tf_op jit(solution)/shard_map/ppermute | solution.py:242
  18.2 0.8 %collective-permute-done.7 = bf16[4,64,128]{2,1,0:T(8,128)(2,1)S(1)} collective-permute-done((bf16[4,64,128]{2,1,0:T(8,128)(2,1)S(1)}, bf16[4,64,128]{2,1,0:T(8,128)(2,1)S(1)}, u32[]{:S(2)}, u32[]{:S(2)}) %collective-permute-start.7) | collective-permute-done | bytes 65568 | tf_op jit(solution)/shard_map/ppermute | solution.py:242
  19.0 1.5 %collective-permute-done.6 = bf16[4,64,128]{2,1,0:T(8,128)(2,1)S(1)} collective-permute-done((bf16[4,64,128]{2,1,0:T(8,128)(2,1)S(1)}, bf16[4,64,128]{2,1,0:T(8,128)(2,1)S(1)}, u32[]{:S(2)}, u32[]{:S(2)}) %collective-permute-start.6) | collective-permute-done | bytes 65568 | tf_op jit(solution)/shard_map/ppermute | solution.py:242
  20.5 2.4 %collective-permute-done.8 = bf16[4,64,128]{2,1,0:T(8,128)(2,1)S(1)} collective-permute-done((bf16[4,64,128]{2,1,0:T(8,128)(2,1)S(1)}, bf16[4,64,128]{2,1,0:T(8,128)(2,1)S(1)}, u32[]{:S(2)}, u32[]{:S(2)}) %collective-permute-start.8) | collective-permute-done | bytes 65568 | tf_op jit(solution)/shard_map/ppermute | solution.py:242
  23.1 2.1 %collective-permute-start.1 = (bf16[8,64,128]{2,1,0:T(8,128)(2,1)S(1)}, bf16[8,64,128]{2,1,0:T(8,128)(2,1)S(1)}, u32[]{:S(2)}, u32[]{:S(2)}) collective-permute-start(bf16[8,64,128]{2,1,0:T(8,128)(2,1)S(1)} %get-tuple-element.16), channel_id=1, source_target_pairs={{0,16},{8,24},{16,0},{24,8},{1,17},{9,25},{17,1},{25,9},{2,18},{10... | collective-permute-start | bytes 393224 | tf_op jit(solution)/shard_map/ppermute | solution.py:242
  25.2 2.3 %collective-permute-start.2 = (bf16[8,64,128]{2,1,0:T(8,128)(2,1)S(1)}, bf16[8,64,128]{2,1,0:T(8,128)(2,1)S(1)}, u32[]{:S(2)}, u32[]{:S(2)}) collective-permute-start(bf16[8,64,128]{2,1,0:T(8,128)(2,1)S(1)} %get-tuple-element.17), channel_id=1, source_target_pairs={{0,24},{8,16},{16,8},{24,0},{1,25},{9,17},{17,9},{25,1},{2,26},{10... | collective-permute-start | bytes 393224 | tf_op jit(solution)/shard_map/ppermute | solution.py:242
  27.5 4.3 %collective-permute-done.refs_1_ = bf16[8,64,128]{2,1,0:T(8,128)(2,1)S(1)} collective-permute-done((bf16[8,64,128]{2,1,0:T(8,128)(2,1)S(1)}, bf16[8,64,128]{2,1,0:T(8,128)(2,1)S(1)}, u32[]{:S(2)}, u32[]{:S(2)}) %collective-permute-start) | collective-permute-done | bytes 131104 | tf_op jit(solution)/shard_map/ppermute | solution.py:242
  31.8 4.4 %collective-permute-done.2.refs_3_ = bf16[8,64,128]{2,1,0:T(8,128)(2,1)S(1)} collective-permute-done((bf16[8,64,128]{2,1,0:T(8,128)(2,1)S(1)}, bf16[8,64,128]{2,1,0:T(8,128)(2,1)S(1)}, u32[]{:S(2)}, u32[]{:S(2)}) %collective-permute-start.2) | collective-permute-done | bytes 131104 | tf_op jit(solution)/shard_map/ppermute | solution.py:242
  36.2 0.6 copy-done.5
  36.8 17.8 %attend.1 = (bf16[8,64,128]{2,1,0:T(8,128)(2,1)S(1)}, bf16[8,64,128]{2,1,0:T(8,128)(2,1)S(1)}, bf16[8,64,128]{2,1,0:T(8,128)(2,1)S(1)}, bf16[8,64,128]{2,1,0:T(8,128)(2,1)S(1)}) custom-call(bf16[8,64,128]{2,1,0:T(8,128)(2,1)S(1)} %get-tuple-element.14.refs_0_, bf16[8,64,128]{2,1,0:T(8,128)(2,1)S(1)} %collective-permute-done.refs_1_, ...), custom_call_target="tpu_custom_call" | custom-call | tf_op jit(solution)/shard_map/attend/pallas_call | solution.py:259
  54.7 2.8 %collective-permute-start.10 = (bf16[8,64,128]{2,1,0:T(8,128)(2,1)S(1)}, bf16[8,64,128]{2,1,0:T(8,128)(2,1)S(1)}, u32[]{:S(2)}, u32[]{:S(2)}) collective-permute-start(bf16[8,64,128]{2,1,0:T(8,128)(2,1)S(1)} %get-tuple-element.20), channel_id=1, source_target_pairs={{0,8},{8,0},{16,24},{24,16},{1,9},{9,1},{17,25},{25,17},{2,10},{10... | collective-permute-start | bytes 393224 | tf_op jit(solution)/shard_map/ppermute | solution.py:242
  57.5 1.8 %collective-permute-start.11 = (bf16[8,64,128]{2,1,0:T(8,128)(2,1)S(1)}, bf16[8,64,128]{2,1,0:T(8,128)(2,1)S(1)}, u32[]{:S(2)}, u32[]{:S(2)}) collective-permute-start(bf16[8,64,128]{2,1,0:T(8,128)(2,1)S(1)} %get-tuple-element.21), channel_id=1, source_target_pairs={{0,16},{8,24},{16,0},{24,8},{1,17},{9,25},{17,1},{25,9},{2,18},{10... | collective-permute-start | bytes 393224 | tf_op jit(solution)/shard_map/ppermute | solution.py:242
  59.3 1.4 %collective-permute-start.12 = (bf16[8,64,128]{2,1,0:T(8,128)(2,1)S(1)}, bf16[8,64,128]{2,1,0:T(8,128)(2,1)S(1)}, u32[]{:S(2)}, u32[]{:S(2)}) collective-permute-start(bf16[8,64,128]{2,1,0:T(8,128)(2,1)S(1)} %get-tuple-element.22), channel_id=1, source_target_pairs={{0,24},{8,16},{16,8},{24,0},{1,25},{9,17},{17,9},{25,1},{2,26},{10... | collective-permute-start | bytes 393224 | tf_op jit(solution)/shard_map/ppermute | solution.py:242
  60.7 1.7 %collective-permute-done.10.refs_1_ = bf16[8,64,128]{2,1,0:T(8,128)(2,1)S(1)} collective-permute-done((bf16[8,64,128]{2,1,0:T(8,128)(2,1)S(1)}, bf16[8,64,128]{2,1,0:T(8,128)(2,1)S(1)}, u32[]{:S(2)}, u32[]{:S(2)}) %collective-permute-start.10) | collective-permute-done | bytes 131104 | tf_op jit(solution)/shard_map/ppermute | solution.py:242
  62.3 7.8 %collective-permute-done.11.refs_2_ = bf16[8,64,128]{2,1,0:T(8,128)(2,1)S(1)} collective-permute-done((bf16[8,64,128]{2,1,0:T(8,128)(2,1)S(1)}, bf16[8,64,128]{2,1,0:T(8,128)(2,1)S(1)}, u32[]{:S(2)}, u32[]{:S(2)}) %collective-permute-start.11) | collective-permute-done | bytes 131104 | tf_op jit(solution)/shard_map/ppermute | solution.py:242
  70.2 1.8 %place.1 = bf16[64,32,128]{2,1,0:T(8,128)(2,1)} custom-call(bf16[8,64,128]{2,1,0:T(8,128)(2,1)S(1)} %get-tuple-element.19.refs_0_, bf16[8,64,128]{2,1,0:T(8,128)(2,1)S(1)} %collective-permute-done.10.refs_1_, bf16[8,64,128]{2,1,0:T(8,128)(2,1)S(1)} %collective-permute-done.11.refs_2_, bf16[8,64,128]{2,1,0:T(8,128)(2,1)S(1)} %collective-permute-done.12.refs_3_), custom_call_target="tpu_custom_call" | custom-call | tf_op jit(solution)/shard_map/place/pallas_call | solution.py:294
  (27 shorter events, 0.7 us)
Async XLA Ops:
  0.0 0.7 copy-start.9
  0.0 0.7 copy-start.4
  0.0 0.7 copy-start.8
  0.7 1.0 %copy-start = (bf16[64,32,128]{2,1,0:T(8,128)(2,1)S(1)}, bf16[64,32,128]{2,1,0:T(8,128)(2,1)}, u32[]{:S(2)}) copy-start(bf16[64,32,128]{2,1,0:T(8,128)(2,1)} %pair_ref.1) | copy-start | bytes 1572868
  4.9 6.8 %collective-permute-start.5 = (bf16[64,128]{1,0:T(8,128)(2,1)S(1)}, bf16[64,128]{1,0:T(8,128)(2,1)S(1)}, u32[]{:S(2)}, u32[]{:S(2)}) collective-permute-start(bf16[64,128]{1,0:T(8,128)(2,1)S(1)} %get-tuple-element.18), channel_id=1, source_target_pairs={{0,24},{8,16},{16,8},{24,0},{1,25},{9,17},{17,9},{25,1},{2,26},{10... | collective-permute-start | bytes 49160 | tf_op jit(solution)/shard_map/ppermute | solution.py:242
  10.0 4.6 %collective-permute-start.4 = (bf16[64,128]{1,0:T(8,128)(2,1)S(1)}, bf16[64,128]{1,0:T(8,128)(2,1)S(1)}, u32[]{:S(2)}, u32[]{:S(2)}) collective-permute-start(bf16[64,128]{1,0:T(8,128)(2,1)S(1)} %get-tuple-element.18), channel_id=1, source_target_pairs={{0,16},{8,24},{16,0},{24,8},{1,17},{9,25},{17,1},{25,9},{2,18},{10... | collective-permute-start | bytes 49160 | tf_op jit(solution)/shard_map/ppermute | solution.py:242
  10.0 4.6 %collective-permute-start.3 = (bf16[64,128]{1,0:T(8,128)(2,1)S(1)}, bf16[64,128]{1,0:T(8,128)(2,1)S(1)}, u32[]{:S(2)}, u32[]{:S(2)}) collective-permute-start(bf16[64,128]{1,0:T(8,128)(2,1)S(1)} %get-tuple-element.18), channel_id=1, source_target_pairs={{0,8},{8,0},{16,24},{24,16},{1,9},{9,1},{17,25},{25,17},{2,10},{10... | collective-permute-start | bytes 49160 | tf_op jit(solution)/shard_map/ppermute | solution.py:242
  14.7 4.3 %collective-permute-start.7 = (bf16[4,64,128]{2,1,0:T(8,128)(2,1)S(1)}, bf16[4,64,128]{2,1,0:T(8,128)(2,1)S(1)}, u32[]{:S(2)}, u32[]{:S(2)}) collective-permute-start(bf16[4,64,128]{2,1,0:T(8,128)(2,1)S(1)} %get-tuple-element.24), channel_id=1, source_target_pairs={{0,4},{1,5},{2,6},{3,7},{4,0},{5,1},{6,2},{7,3},{8,12},{9,13},{10,... | collective-permute-start | bytes 196616 | tf_op jit(solution)/shard_map/ppermute | solution.py:242
  16.2 4.3 %collective-permute-start.6 = (bf16[4,64,128]{2,1,0:T(8,128)(2,1)S(1)}, bf16[4,64,128]{2,1,0:T(8,128)(2,1)S(1)}, u32[]{:S(2)}, u32[]{:S(2)}) collective-permute-start(bf16[4,64,128]{2,1,0:T(8,128)(2,1)S(1)} %get-tuple-element.24), channel_id=1, source_target_pairs={{0,2},{1,3},{2,0},{3,1},{4,6},{5,7},{6,4},{7,5},{8,10},{9,11},{10,... | collective-permute-start | bytes 196616 | tf_op jit(solution)/shard_map/ppermute | solution.py:242
  17.7 5.2 %collective-permute-start.8 = (bf16[4,64,128]{2,1,0:T(8,128)(2,1)S(1)}, bf16[4,64,128]{2,1,0:T(8,128)(2,1)S(1)}, u32[]{:S(2)}, u32[]{:S(2)}) collective-permute-start(bf16[4,64,128]{2,1,0:T(8,128)(2,1)S(1)} %get-tuple-element.24), channel_id=1, source_target_pairs={{0,6},{1,7},{2,4},{3,5},{4,2},{5,3},{6,0},{7,1},{8,14},{9,15},{10,... | collective-permute-start | bytes 196616 | tf_op jit(solution)/shard_map/ppermute | solution.py:242
  22.9 13.2 %copy-start.1 = (bf16[128,384]{1,0:T(8,128)(2,1)S(1)}, bf16[128,384]{1,0:T(8,128)(2,1)}, u32[]{:S(2)}) copy-start(bf16[128,384]{1,0:T(8,128)(2,1)} %refs_7_.1) | copy-start | bytes 294916
  22.9 13.2 %copy-start.2 = (bf16[128,128]{1,0:T(8,128)(2,1)S(1)}, bf16[128,128]{1,0:T(8,128)(2,1)}, u32[]{:S(2)}) copy-start(bf16[128,128]{1,0:T(8,128)(2,1)} %refs_8_.1) | copy-start | bytes 98308
  22.9 13.2 %copy-start.3 = (bf16[128,128]{1,0:T(8,128)(2,1)S(1)}, bf16[128,128]{1,0:T(8,128)(2,1)}, u32[]{:S(2)}) copy-start(bf16[128,128]{1,0:T(8,128)(2,1)} %refs_10_.1) | copy-start | bytes 98308
  22.9 13.3 %copy-start.7 = (f32[128]{0:T(128)S(1)}, f32[128]{0:T(128)}, u32[]{:S(2)}) copy-start(f32[128]{0:T(128)} %param.19) | copy-start | bytes 1540
  23.0 13.2 %collective-permute-start.9 = (bf16[4,4,64,128]{3,2,1,0:T(8,128)(2,1)S(1)}, bf16[4,4,64,128]{3,2,1,0:T(8,128)(2,1)S(1)}, u32[]{:S(2)}, u32[]{:S(2)}) collective-permute-start(bf16[4,4,64,128]{3,2,1,0:T(8,128)(2,1)S(1)} %pad_maximum_fusion.refs_4_), channel_id=1, source_target_pairs={{0,1},{1,0},{2,3},{3,2},{4,5},{5,4},{6,7},{7,6},{8,9},{9,8},{10,11... | collective-permute-start | bytes 786440 | tf_op jit(solution)/shard_map/ppermute | solution.py:242
  23.0 8.7 %collective-permute-start = (bf16[8,64,128]{2,1,0:T(8,128)(2,1)S(1)}, bf16[8,64,128]{2,1,0:T(8,128)(2,1)S(1)}, u32[]{:S(2)}, u32[]{:S(2)}) collective-permute-start(bf16[8,64,128]{2,1,0:T(8,128)(2,1)S(1)} %get-tuple-element.15), channel_id=1, source_target_pairs={{0,8},{8,0},{16,24},{24,16},{1,9},{9,1},{17,25},{25,17},{2,10},{10... | collective-permute-start | bytes 393224 | tf_op jit(solution)/shard_map/ppermute | solution.py:242
  23.1 8.6 %collective-permute-start.1 = (bf16[8,64,128]{2,1,0:T(8,128)(2,1)S(1)}, bf16[8,64,128]{2,1,0:T(8,128)(2,1)S(1)}, u32[]{:S(2)}, u32[]{:S(2)}) collective-permute-start(bf16[8,64,128]{2,1,0:T(8,128)(2,1)S(1)} %get-tuple-element.16), channel_id=1, source_target_pairs={{0,16},{8,24},{16,0},{24,8},{1,17},{9,25},{17,1},{25,9},{2,18},{10... | collective-permute-start | bytes 393224 | tf_op jit(solution)/shard_map/ppermute | solution.py:242
  25.2 10.9 %collective-permute-start.2 = (bf16[8,64,128]{2,1,0:T(8,128)(2,1)S(1)}, bf16[8,64,128]{2,1,0:T(8,128)(2,1)S(1)}, u32[]{:S(2)}, u32[]{:S(2)}) collective-permute-start(bf16[8,64,128]{2,1,0:T(8,128)(2,1)S(1)} %get-tuple-element.17), channel_id=1, source_target_pairs={{0,24},{8,16},{16,8},{24,0},{1,25},{9,17},{17,9},{25,1},{2,26},{10... | collective-permute-start | bytes 393224 | tf_op jit(solution)/shard_map/ppermute | solution.py:242
  36.1 0.7 copy-start.5
  36.1 0.7 copy-start.6
  54.7 7.7 %collective-permute-start.10 = (bf16[8,64,128]{2,1,0:T(8,128)(2,1)S(1)}, bf16[8,64,128]{2,1,0:T(8,128)(2,1)S(1)}, u32[]{:S(2)}, u32[]{:S(2)}) collective-permute-start(bf16[8,64,128]{2,1,0:T(8,128)(2,1)S(1)} %get-tuple-element.20), channel_id=1, source_target_pairs={{0,8},{8,0},{16,24},{24,16},{1,9},{9,1},{17,25},{25,17},{2,10},{10... | collective-permute-start | bytes 393224 | tf_op jit(solution)/shard_map/ppermute | solution.py:242
  57.5 12.7 %collective-permute-start.11 = (bf16[8,64,128]{2,1,0:T(8,128)(2,1)S(1)}, bf16[8,64,128]{2,1,0:T(8,128)(2,1)S(1)}, u32[]{:S(2)}, u32[]{:S(2)}) collective-permute-start(bf16[8,64,128]{2,1,0:T(8,128)(2,1)S(1)} %get-tuple-element.21), channel_id=1, source_target_pairs={{0,16},{8,24},{16,0},{24,8},{1,17},{9,25},{17,1},{25,9},{2,18},{10... | collective-permute-start | bytes 393224 | tf_op jit(solution)/shard_map/ppermute | solution.py:242
  59.3 10.9 %collective-permute-start.12 = (bf16[8,64,128]{2,1,0:T(8,128)(2,1)S(1)}, bf16[8,64,128]{2,1,0:T(8,128)(2,1)S(1)}, u32[]{:S(2)}, u32[]{:S(2)}) collective-permute-start(bf16[8,64,128]{2,1,0:T(8,128)(2,1)S(1)} %get-tuple-element.22), channel_id=1, source_target_pairs={{0,24},{8,16},{16,8},{24,0},{1,25},{9,17},{17,9},{25,1},{2,26},{10... | collective-permute-start | bytes 393224 | tf_op jit(solution)/shard_map/ppermute | solution.py:242

commit v2 on v1

v2 whole, which is shorter than its diff:
```python
import functools

import jax
import jax.numpy as jnp
from jax import lax
from jax.experimental import pallas as pl
from jax.experimental.pallas import tpu as pltpu
from jax.sharding import PartitionSpec as P

BF = jnp.bfloat16
F32 = jnp.float32
VMEM_LIMIT = 52 * 1024 * 1024
VMEM_ALONE = 62 * 1024 * 1024


def dot(a, b):
    return jnp.dot(a, b, preferred_element_type=F32)


def dot_t(a, b):
    return lax.dot_general(a, b, (((1,), (1,)), ((), ())), preferred_element_type=F32)


def dot_l(a, b):
    return lax.dot_general(a, b, (((0,), (0,)), ((), ())), preferred_element_type=F32)


def over(a, size):
    return lax.shift_right_logical(a, jnp.full_like(a, size.bit_length() - 1))


def below(a, size):
    return a & (size - 1)


def column_of(row, width):
    return jnp.broadcast_to(row, (width, row.shape[1])).T


def split_sum(a, ones):
    first = a.astype(BF)
    rest = a - first.astype(F32)
    second = rest.astype(BF)
    third = (rest - second.astype(F32)).astype(BF)
    return dot(first, ones) + dot(second, ones) + dot(third, ones)


def prep_kernel(pair_ref, gain_ref, shift_ref, wb_ref, *refs):
    parcels, (raw, gain, shift, wbt, wide, sem) = refs[:-6], refs[-6:]
    rows, cols, chans = pair_ref.shape
    heads = wb_ref.shape[0]
    lanes = heads * cols
    parts = len(parcels)
    width = cols // parts
    me = lax.axis_index("row")
    step = wide.shape[0]
    small = [
        pltpu.make_async_copy(source, target, sem.at[n])
        for n, (source, target) in enumerate(((wb_ref, wbt), (gain_ref, gain), (shift_ref, shift)))
    ]
    for copy in small:
        copy.start()

    half = rows // 2
    fetches = [
        pltpu.make_async_copy(
            pair_ref.at[pl.ds(n * half, half)], raw.at[pl.ds(n * half, half)], sem.at[3 + n]
        )
        for n in range(2)
    ]
    for copy in fetches:
        copy.start()
    ones = jnp.ones((chans, chans), BF)
    lane_col = below(lax.broadcasted_iota(jnp.int32, (cols, lanes), 1), cols)
    keep = lane_col == lax.broadcasted_iota(jnp.int32, (cols, lanes), 0)
    head_of = over(lax.broadcasted_iota(jnp.int32, (lanes, heads), 0), cols)
    spread = (head_of == lax.broadcasted_iota(jnp.int32, (lanes, heads), 1)).astype(BF)
    for copy in small:
        copy.wait()
    wb = dot(spread, wbt[...]).astype(BF)

    def body(index, carry):
        start = pl.multiple_of(index * step, step)
        values = raw[pl.ds(start, step)].reshape(step * cols, chans)
        mean = dot(values, ones) * (1.0 / chans)
        centred = values.astype(F32) - mean
        var = split_sum(centred * centred, ones) * (1.0 / chans)
        normed = (centred * lax.rsqrt(var + 1e-05) * gain[...] + shift[...]).astype(BF)
        every = dot_t(normed, wb).reshape(step, cols, lanes)
        tile = jnp.sum(jnp.where(keep[None], every, 0.0), axis=1).astype(BF)
        wide[...] = normed.astype(F32).reshape(step, cols, chans)
        to = pl.ds(pl.multiple_of(start * width, step * width), step * width)
        for s in range(parts):
            first = pl.multiple_of((me ^ s) * width, width)
            chunk = wide[:, pl.ds(first, width), :].reshape(step * width, chans)
            parcels[s][to, :] = chunk.astype(BF)
            for n in range(lanes // chans):
                row = pl.multiple_of(rows * (width + n) + start, step)
                parcels[s][pl.ds(row, step), :] = tile[:, n * chans : (n + 1) * chans]
        return carry

    for n in range(2):
        fetches[n].wait()
        lax.fori_loop(n * half // step, (n + 1) * half // step, body, 0, unroll=rows <= 64)


def project_kernel(parts, scale, rows, width, offset, *refs):
    parcels = refs[:parts]
    wqkv_ref, wg_ref, gb_ref, q_ref, k_ref, v_ref, gate_ref = refs[parts : parts + 7]
    wide, tokens, weight, gate_bias, sem = refs[parts + 7 :]
    some, count, inner = q_ref.shape
    me = lax.axis_index("row")
    copies = [
        pltpu.make_async_copy(wqkv_ref, weight.at[:, pl.ds(0, 3 * inner)], sem.at[0]),
        pltpu.make_async_copy(wg_ref, weight.at[:, pl.ds(3 * inner, inner)], sem.at[1]),
        pltpu.make_async_copy(gb_ref, gate_bias, sem.at[2]),
    ]
    for copy in copies:
        copy.start()
    for s in range(parts):
        wide[s] = parcels[s][0 : rows * width, :].astype(F32)
    for copy in copies:
        copy.wait()

    def one_column(j, carry):
        for s in range(parts):
            at = pl.ds(pl.multiple_of((me ^ s) * rows, rows), rows)
            tokens[at, :] = wide[s, pl.ds(offset + j, rows, stride=width), :].astype(BF)
        mixed = dot(tokens[...], weight[...])
        q_ref[j] = (mixed[:, 0:inner] * scale).astype(BF)
        k_ref[j] = mixed[:, inner : 2 * inner].astype(BF)
        v_ref[j] = mixed[:, 2 * inner : 3 * inner].astype(BF)
        gate_ref[j] = jax.nn.sigmoid(mixed[:, 3 * inner : 4 * inner] + gate_bias[...])
        return carry

    lax.fori_loop(0, some, one_column, 0, unroll=2)


def attend_kernel(parts, *refs):
    halves = refs[0:4], refs[4:8]
    bias_a, bias_b, mask_ref, wo_ref, ob_ref = refs[8:13]
    outs = refs[13 : parts + 13]
    update, tiles, bias, key_bias, heard, mask, out_weight, out_bias, sem = refs[parts + 13 :]
    part, count, inner = halves[0][0].shape
    width = 2 * part
    pairs, _, layers, rows, chans = bias_a.shape
    heads = bias.shape[0]
    lanes = layers * chans
    cols = lanes // heads
    head = inner // heads
    me = lax.axis_index("row")
    col = lax.axis_index("col")
    copies = [
        pltpu.make_async_copy(source, target, sem.at[n])
        for n, (source, target) in enumerate(
            ((mask_ref, mask), (wo_ref, out_weight), (ob_ref, out_bias))
        )
    ]
    for copy in copies:
        copy.start()
    for k, source in enumerate((bias_a, bias_b)):
        for t in range(pairs):
            tiles[col ^ (2 * t + k)] = source[t]

    group = 128 // cols
    span = group * lanes
    source_lane = lax.broadcasted_iota(jnp.int32, (span, span), 0)
    target_lane = lax.broadcasted_iota(jnp.int32, (span, span), 1)
    tile_of, rest = over(source_lane, lanes), below(source_lane, lanes)
    wanted = over(rest, cols) * 128 + tile_of * cols + below(rest, cols)
    order = (wanted == target_lane).astype(BF)
    batch = max(1, min(count, 256) // rows)
    for copy in copies:
        copy.wait()
    key_bias[...] = jnp.where(column_of(mask[...], 128) == 1, 0.0, -1000000000.0).astype(F32)

    def one_block(index, carry):
        g, b = index // (parts // batch), index % (parts // batch)
        block = jnp.concatenate(
            [
                tiles[g * group + t, pl.ds(b * batch, batch), n].reshape(batch * rows, chans)
                for t in range(group)
                for n in range(layers)
            ],
            axis=1,
        )
        ordered = dot(block, order)
        across = pl.ds(pl.multiple_of(g * 128, 128), 128)
        for s in range(batch):
            at = pl.ds(pl.multiple_of((me ^ (b * batch + s)) * rows, rows), rows)
            for h in range(heads):
                bias[h, at, across] = (
                    ordered[s * rows : (s + 1) * rows, h * 128 : (h + 1) * 128] + key_bias[at, :]
                )
        return carry

    blocks = (count // 128) * (parts // batch)
    lax.fori_loop(0, blocks, one_block, 0, unroll=blocks <= 2)

    lane_head = over(lax.broadcasted_iota(jnp.int32, (1, inner), 1), head)
    wide = heard.shape[0]

    def one_column(half, j, carry):
        q_ref, k_ref, v_ref, gate_ref = halves[half]

        def one_part(g, inside):
            at = pl.ds(pl.multiple_of(g * wide, wide), wide)
            some = q_ref[j, at, :]
            heard[...] = jnp.zeros_like(heard)

            def one_head(h, within):
                mine = lane_head == h
                head_keys = jnp.where(mine, k_ref[j], jnp.zeros((count, inner), BF))
                head_vals = jnp.where(mine, v_ref[j], jnp.zeros((count, inner), BF))
                scores = dot_t(head_keys, some) + bias[h, :, at]
                top = jnp.max(scores, axis=0, keepdims=True)
                expo = jnp.exp(scores - top)
                total = jnp.sum(expo, axis=0, keepdims=True)
                weights = (expo * (1.0 / total)).astype(BF)
                heard[...] += dot_l(weights, head_vals)
                return within

            lax.fori_loop(0, heads, one_head, 0, unroll=count == wide)
            attended = heard[...].astype(BF).astype(F32)
            gated = (gate_ref[j, at, :] * attended).astype(BF)
            result = dot(gated, out_weight[...]) + out_bias[...]
            update[pl.ds(g * wide * width + half * part + j, wide, stride=width), :] = result
            return inside

        lax.fori_loop(0, count // wide, one_part, 0, unroll=count == wide)
        return carry

    for half in range(2):
        body = functools.partial(one_column, half)
        lax.fori_loop(0, part, body, 0, unroll=part if count == wide else 1)
    for s in range(parts):
        at = pl.ds(pl.multiple_of((me ^ s) * rows * width, rows * width), rows * width)
        outs[s][...] = update[at, :].astype(BF).reshape(rows, width, chans)


def place_kernel(*refs):
    pieces, out_ref, wide = refs[:-2], refs[-2], refs[-1]
    rows, cols, chans = out_ref.shape
    width = cols // len(pieces)
    me = lax.axis_index("row")
    step = wide.shape[0]

    def body(index, carry):
        at = pl.ds(pl.multiple_of(index * step, step), step)
        for s, piece in enumerate(pieces):
            first = pl.multiple_of((me ^ s) * width, width)
            wide[:, pl.ds(first, width), :] = piece[at].astype(F32)
        out_ref[at] = wide[...].astype(BF)
        return carry

    lax.fori_loop(0, rows // step, body, 0, unroll=rows <= 64)


def per_device(
    pair, token_mask, ln_gain, ln_shift, w_qkv, w_bias, w_gate, gate_bias, w_out, out_bias
):
    rows, cols, chans = pair.shape
    heads = w_bias.shape[1]
    inner = w_gate.shape[1]
    parts = lax.axis_size("row")
    col_count = lax.axis_size("col")
    count = rows * parts
    width = cols // parts
    lanes = heads * cols
    lane_part = 256 if count <= 256 else 128
    chunk = jax.ShapeDtypeStruct((rows, width, chans), BF)
    vmem = pl.BlockSpec(memory_space=pltpu.VMEM)
    hbm = pl.BlockSpec(memory_space=pltpu.HBM)
    large = count > 256
    params = pltpu.CompilerParams(vmem_limit_bytes=VMEM_LIMIT if large else VMEM_LIMIT // 4)
    alone = pltpu.CompilerParams(vmem_limit_bytes=VMEM_ALONE)

    def swap(x, axis, offset):
        size = lax.axis_size(axis)
        return lax.ppermute(x, axis, [(i, i ^ offset) for i in range(size)])

    layers = lanes // chans
    step = min(rows, 16)
    parcels = pl.pallas_call(
        prep_kernel,
        out_shape=[jax.ShapeDtypeStruct((rows * (width + layers), chans), BF)] * parts,
        in_specs=[hbm] * 4,
        out_specs=[vmem] * parts,
        scratch_shapes=[
            pltpu.VMEM((rows, cols, chans), BF),
            pltpu.VMEM((1, chans), F32),
            pltpu.VMEM((1, chans), F32),
            pltpu.VMEM((heads, chans), BF),
            pltpu.VMEM((step, cols, chans), F32),
            pltpu.SemaphoreType.DMA((5,)),
        ],
        compiler_params=alone,
        name="prep",
    )(pair, ln_gain.reshape(1, chans), ln_shift.reshape(1, chans), w_bias.T)

    parcels = [parcels[0]] + [swap(parcels[s], "row", s) for s in range(1, parts)]
    by_row = jnp.stack([p[rows * width :].reshape(layers, rows, chans) for p in parcels])
    by_chip = jnp.stack([by_row] + [swap(by_row, "col", 2 * t) for t in range(1, col_count // 2)])
    part = width // 2

    def project(offset):
        return pl.pallas_call(
            functools.partial(
                project_kernel, parts, (inner // heads) ** (-0.5), rows, width, offset
            ),
            out_shape=[jax.ShapeDtypeStruct((part, count, inner), BF)] * 3
            + [jax.ShapeDtypeStruct((part, count, inner), F32)],
            in_specs=[vmem] * parts + [hbm] * 3,
            out_specs=[vmem] * 4,
            scratch_shapes=[
                pltpu.VMEM((parts, rows * width, chans), F32),
                pltpu.VMEM((count, chans), BF),
                pltpu.VMEM((chans, 4 * inner), BF),
                pltpu.VMEM((1, inner), F32),
                pltpu.SemaphoreType.DMA((3,)),
            ],
            cost_estimate=pl.CostEstimate(
                flops=8 * part * count * chans * inner,
                bytes_accessed=part * count * (2 * chans + 10 * inner),
                transcendentals=part * count * inner,
            ),
            compiler_params=params,
            name="project",
        )(*parcels, w_qkv, w_gate, gate_bias.reshape(1, inner))

    first = project(0)
    by_chip, first = lax.optimization_barrier((by_chip, first))
    other = swap(by_chip, "col", 1)
    second = project(part)

    returned = pl.pallas_call(
        functools.partial(attend_kernel, parts),
        out_shape=[chunk] * parts,
        in_specs=[vmem] * 10 + [hbm] * 3,
        out_specs=[vmem] * parts,
        scratch_shapes=[
            pltpu.VMEM((count * width, chans), F32),
            pltpu.VMEM((col_count, parts, layers, rows, chans), BF),
            pltpu.VMEM((heads, count, count), F32),
            pltpu.VMEM((count, 128), F32),
            pltpu.VMEM((lane_part, inner), F32),
            pltpu.VMEM((1, count), jnp.int32),
            pltpu.VMEM((inner, chans), BF),
            pltpu.VMEM((1, chans), F32),
            pltpu.SemaphoreType.DMA((3,)),
        ],
        cost_estimate=pl.CostEstimate(
            flops=8 * width * count * count * inner,
            bytes_accessed=width * count * 12 * inner,
            transcendentals=width * heads * count * count,
        ),
        compiler_params=params,
        name="attend",
    )(
        *first,
        *second,
        by_chip,
        other,
        token_mask.reshape(1, count),
        w_out,
        out_bias.reshape(1, chans),
    )
    back = [returned[0]] + [swap(returned[s], "row", s) for s in range(1, parts)]
    return pl.pallas_call(
        place_kernel,
        out_shape=jax.ShapeDtypeStruct((rows, cols, chans), BF),
        in_specs=[vmem] * parts,
        out_specs=vmem,
        scratch_shapes=[pltpu.VMEM((min(rows, 16), cols, chans), F32)],
        compiler_params=params,
        name="place",
    )(*back)


def solution(mesh):
    in_specs = (P("row", "col", None), P(), P(), P(), P(), P(), P(), P(), P(), P())
    out_specs = P("row", "col", None)
    return jax.shard_map(
        per_device, mesh=mesh, in_specs=in_specs, out_specs=out_specs, check_vma=False
    )
```

time: 72.1 us -> 54.3 us (0.75)
  Pallas kernels: 22.8 us -> 12.4 us
  starting transfers between devices: 19.8 us -> 14.1 us
  local copies, waits for them, and re-layouts: 2.4 us -> 1.43 us
  waiting for transfers between devices: 26.8 us -> 26 us
    pallas_call x1, Pallas kernels: 17.8 us -> 6.25 us  [per_device(): pl.pallas_call(functools.partial(attend_kernel, parts), out_shape=[chunk]...]
    ppermute x13 -> x10, starting transfers between devices: 19.8 us -> 14.1 us  [swap(): return lax.ppermute(x, axis, [(i, i ^ offset) for i in range(size)])]
    pallas_call x1 -> x3, Pallas kernels: 3.14 us -> 5.17 us  [the longest x1 3.64 us: per_device(): pl.pallas_call(prep_kernel, out_shape=[jax.ShapeDtypeStruct((rows * (widt...]
    unnamed x20 -> x14, local copies, waits for them, and re-layouts: 2.4 us -> 0.71 us
    ppermute x13 -> x10, waiting for transfers between devices: 26.8 us -> 26 us  [swap(): return lax.ppermute(x, axis, [(i, i ^ offset) for i in range(size)])]
    pallas_call x1, Pallas kernels: 1.8 us -> 1.01 us  [per_device(): pl.pallas_call(place_kernel, out_shape=jax.ShapeDtypeStruct((rows, cols,...]
    another operation x0 -> x4, local copies, waits for them, and re-layouts: none -> 0.73 us  [per_device(): jnp.stack([p[rows * width:].reshape(layers, rows, chans) for p in parcels])]
  transfers between devices with their start and end apart: 13 -> 10, of which waited for: 9 -> 8; matrix products, arithmetic and copies ran while one was open for 0% -> 1% of each run, Pallas kernels for 0% -> 3%
where the time goes in v2:
time: 54.3 us; the launch traced here: 54.1 us
  waiting for transfers between devices  26 us (48%)
  starting transfers between devices  14.1 us (26%)
  Pallas kernels  12.4 us (23%)
  local copies, waits for them, and re-layouts  1.43 us (3%)
    ppermute x10, waiting for transfers between devices, swap(): return lax.ppermute(x, axis, [(i, i ^ offset) for i in range(size)])  26 us
    ppermute x10, starting transfers between devices, swap(): return lax.ppermute(x, axis, [(i, i ^ offset) for i in range(size)])  14.1 us
    pallas_call x1, Pallas kernels, per_device(): pl.pallas_call(functools.partial(attend_kernel, parts), out_shape=[chunk]...  6.25 us
    pallas_call x1, Pallas kernels, per_device(): pl.pallas_call(prep_kernel, out_shape=[jax.ShapeDtypeStruct((rows * (widt...  3.64 us
    pallas_call x2, Pallas kernels, project(): pl.pallas_call(functools.partial(project_kernel, parts, (inner // heads)...  1.53 us
  transfers between devices with their start and end apart: 10, of which 8 were waited for; matrix products, arithmetic and copies ran while one was open for 1% of the time, Pallas kernels for 3%

profile of v2, /device:TPU:0, one launch (start us, length us, event | category | flops | bytes accessed | tf_op | source)
XLA Modules:
  0.0 54.1 jit_solution(2160298377408117248)
XLA Ops:
  0.0 3.6 %prep.1 = (bf16[576,128]{1,0:T(8,128)(2,1)}, bf16[576,128]{1,0:T(8,128)(2,1)}, bf16[576,128]{1,0:T(8,128)(2,1)}, bf16[576,128]{1,0:T(8,128)(2,1)}) custom-call(bf16[64,32,128]{2,1,0:T(8,128)(2,1)} %pair_ref.1, f32[1,128]{1,0:T(1,128)} %bitcast.33, f32[1,128]{1,0:T(1,128)} %bitcast.34, bf16[4,128]{1,0:T(4,128)(2,1)} %bitcast.32), custom_call_target="tpu_custom_call" | custom-call | tf_op jit(solution)/shard_map/prep/pallas_call | solution.py:284
  3.6 3.1 %collective-permute-start = (bf16[576,128]{1,0:T(8,128)(2,1)}, bf16[576,128]{1,0:T(8,128)(2,1)S(1)}, u32[]{:S(2)}, u32[]{:S(2)}) collective-permute-start(bf16[576,128]{1,0:T(8,128)(2,1)} %get-tuple-element.27), channel_id=1, source_target_pairs={{0,8},{8,0},{16,24},{24,16},{1,9},{9,1},{17,25},{25,17},{2,10},{10... | collective-permute-start | bytes 442376 | tf_op jit(solution)/shard_map/ppermute | solution.py:280
  6.7 2.6 %collective-permute-start.1 = (bf16[576,128]{1,0:T(8,128)(2,1)}, bf16[576,128]{1,0:T(8,128)(2,1)S(1)}, u32[]{:S(2)}, u32[]{:S(2)}) collective-permute-start(bf16[576,128]{1,0:T(8,128)(2,1)} %get-tuple-element.28), channel_id=1, source_target_pairs={{0,16},{8,24},{16,0},{24,8},{1,17},{9,25},{17,1},{25,9},{2,18},{10... | collective-permute-start | bytes 442376 | tf_op jit(solution)/shard_map/ppermute | solution.py:280
  9.3 0.7 %slice_bitcast_fusion.3 = bf16[1,1,64,128]{3,2,0,1:T(8,128)(2,1)S(1)} fusion(bf16[576,128]{1,0:T(8,128)(2,1)} %get-tuple-element.26.refs_0_), kind=kLoop, calls=%fused_computation.5 | loop fusion | bytes 32768 | tf_op jit(solution)/shard_map/stack;reshape | solution.py:302
  10.1 2.7 %collective-permute-done.refs_1_ = bf16[576,128]{1,0:T(8,128)(2,1)S(1)} collective-permute-done((bf16[576,128]{1,0:T(8,128)(2,1)}, bf16[576,128]{1,0:T(8,128)(2,1)S(1)}, u32[]{:S(2)}, u32[]{:S(2)}) %collective-permute-start) | collective-permute-done | bytes 147488 | tf_op jit(solution)/shard_map/ppermute | solution.py:280
  12.8 8.1 %collective-permute-done.1.refs_2_ = bf16[576,128]{1,0:T(8,128)(2,1)S(1)} collective-permute-done((bf16[576,128]{1,0:T(8,128)(2,1)}, bf16[576,128]{1,0:T(8,128)(2,1)S(1)}, u32[]{:S(2)}, u32[]{:S(2)}) %collective-permute-start.1) | collective-permute-done | bytes 147488 | tf_op jit(solution)/shard_map/ppermute | solution.py:280
  21.0 1.6 %collective-permute-start.4 = (bf16[4,1,64,128]{3,2,0,1:T(8,128)(2,1)S(1)}, bf16[4,1,64,128]{3,2,0,1:T(8,128)(2,1)S(1)}, u32[]{:S(2)}, u32[]{:S(2)}) collective-permute-start(bf16[4,1,64,128]{3,2,0,1:T(8,128)(2,1)S(1)} %get-tuple-element.48), channel_id=1, source_target_pairs={{0,4},{1,5},{2,6},{3,7},{4,0},{5,1},{6,2},{7,3},{8,12},{9,13},{10,... | collective-permute-start | bytes 196616 | tf_op jit(solution)/shard_map/ppermute | solution.py:280
  22.6 1.5 %collective-permute-start.3 = (bf16[4,1,64,128]{3,2,0,1:T(8,128)(2,1)S(1)}, bf16[4,1,64,128]{3,2,0,1:T(8,128)(2,1)S(1)}, u32[]{:S(2)}, u32[]{:S(2)}) collective-permute-start(bf16[4,1,64,128]{3,2,0,1:T(8,128)(2,1)S(1)} %get-tuple-element.48), channel_id=1, source_target_pairs={{0,2},{1,3},{2,0},{3,1},{4,6},{5,7},{6,4},{7,5},{8,10},{9,11},{10,... | collective-permute-start | bytes 196616 | tf_op jit(solution)/shard_map/ppermute | solution.py:280
  24.1 0.5 collective-permute-start.5
  24.6 0.8 %project.2 = (bf16[4,256,128]{2,1,0:T(8,128)(2,1)S(1)}, bf16[4,256,128]{2,1,0:T(8,128)(2,1)S(1)}, bf16[4,256,128]{2,1,0:T(8,128)(2,1)S(1)}, f32[4,256,128]{2,1,0:T(8,128)S(1)}) custom-call(bf16[576,128]{1,0:T(8,128)(2,1)S(1)} %copy-done, bf16[576,128]{1,0:T(8,128)(2,1)S(1)} %collective-permute-done.refs_1_, ...), custom_call_target="tpu_custom_call" | custom-call | flops 134217728 | bytes 1572864 | tf_op jit(solution)/shard_map/project/pallas_call | solution.py:307
  25.4 0.4 collective-permute-done.4
  25.8 1.1 %collective-permute-done.3 = bf16[4,1,64,128]{3,2,0,1:T(8,128)(2,1)S(1)} collective-permute-done((bf16[4,1,64,128]{3,2,0,1:T(8,128)(2,1)S(1)}, bf16[4,1,64,128]{3,2,0,1:T(8,128)(2,1)S(1)}, u32[]{:S(2)}, u32[]{:S(2)}) %collective-permute-start.3) | collective-permute-done | bytes 65568 | tf_op jit(solution)/shard_map/ppermute | solution.py:280
  26.9 2.4 %collective-permute-done.5 = bf16[4,1,64,128]{3,2,0,1:T(8,128)(2,1)S(1)} collective-permute-done((bf16[4,1,64,128]{3,2,0,1:T(8,128)(2,1)S(1)}, bf16[4,1,64,128]{3,2,0,1:T(8,128)(2,1)S(1)}, u32[]{:S(2)}, u32[]{:S(2)}) %collective-permute-start.5) | collective-permute-done | bytes 65568 | tf_op jit(solution)/shard_map/ppermute | solution.py:280
  29.3 0.1 collective-permute-start.6
  29.4 0.8 %project.3 = (bf16[4,256,128]{2,1,0:T(8,128)(2,1)S(1)}, bf16[4,256,128]{2,1,0:T(8,128)(2,1)S(1)}, bf16[4,256,128]{2,1,0:T(8,128)(2,1)S(1)}, f32[4,256,128]{2,1,0:T(8,128)S(1)}) custom-call(bf16[576,128]{1,0:T(8,128)(2,1)S(1)} %copy-done, bf16[576,128]{1,0:T(8,128)(2,1)S(1)} %collective-permute-done.refs_1_, ...), custom_call_target="tpu_custom_call" | custom-call | flops 134217728 | bytes 1572864 | tf_op jit(solution)/shard_map/project/pallas_call | solution.py:307
  30.2 0.8 %collective-permute-done.6.refs_9_ = bf16[4,4,1,64,128]{4,3,2,1,0:T(8,128)(2,1)S(1)} collective-permute-done((bf16[4,4,1,64,128]{4,3,2,1,0:T(8,128)(2,1)S(1)}, bf16[4,4,1,64,128]{4,3,2,1,0:T(8,128)(2,1)S(1)}, u32[]{:S(2)}, u32[]{:S(2)}) %collective-permute-start.6) | collective-permute-done | bytes 262176 | tf_op jit(solution)/shard_map/ppermute | solution.py:280
  30.9 0.7 %copy-done.5 = s32[256]{0:T(256)S(1)} copy-done((s32[256]{0:T(256)S(1)}, s32[256]{0:T(256)}, u32[]{:S(2)}) %copy-start.5) | copy-done | bytes 1048
  31.6 6.3 %attend.1 = (bf16[64,8,128]{2,1,0:T(8,128)(2,1)S(1)}, bf16[64,8,128]{2,1,0:T(8,128)(2,1)S(1)}, bf16[64,8,128]{2,1,0:T(8,128)(2,1)S(1)}, bf16[64,8,128]{2,1,0:T(8,128)(2,1)S(1)}) custom-call(bf16[4,256,128]{2,1,0:T(8,128)(2,1)S(1)} %get-tuple-element.34.refs_0_, bf16[4,256,128]{2,1,0:T(8,128)(2,1)S(1)} %get-tuple-element.35.refs_1_, ...), custom_call_target="tpu_custom_call" | custom-call | flops 536870912 | bytes 3145728 | tf_op jit(solution)/shard_map/attend/pallas_call | solution.py:336
  37.9 2.3 %collective-permute-start.7 = (bf16[64,8,128]{2,1,0:T(8,128)(2,1)S(1)}, bf16[64,8,128]{2,1,0:T(8,128)(2,1)S(1)}, u32[]{:S(2)}, u32[]{:S(2)}) collective-permute-start(bf16[64,8,128]{2,1,0:T(8,128)(2,1)S(1)} %get-tuple-element.44), channel_id=1, source_target_pairs={{0,8},{8,0},{16,24},{24,16},{1,9},{9,1},{17,25},{25,17},{2,10},{10... | collective-permute-start | bytes 393224 | tf_op jit(solution)/shard_map/ppermute | solution.py:280
  40.2 1.1 %collective-permute-start.8 = (bf16[64,8,128]{2,1,0:T(8,128)(2,1)S(1)}, bf16[64,8,128]{2,1,0:T(8,128)(2,1)S(1)}, u32[]{:S(2)}, u32[]{:S(2)}) collective-permute-start(bf16[64,8,128]{2,1,0:T(8,128)(2,1)S(1)} %get-tuple-element.45), channel_id=1, source_target_pairs={{0,16},{8,24},{16,0},{24,8},{1,17},{9,25},{17,1},{25,9},{2,18},{10... | collective-permute-start | bytes 393224 | tf_op jit(solution)/shard_map/ppermute | solution.py:280
  41.3 1.4 %collective-permute-start.9 = (bf16[64,8,128]{2,1,0:T(8,128)(2,1)S(1)}, bf16[64,8,128]{2,1,0:T(8,128)(2,1)S(1)}, u32[]{:S(2)}, u32[]{:S(2)}) collective-permute-start(bf16[64,8,128]{2,1,0:T(8,128)(2,1)S(1)} %get-tuple-element.46), channel_id=1, source_target_pairs={{0,24},{8,16},{16,8},{24,0},{1,25},{9,17},{17,9},{25,1},{2,26},{10... | collective-permute-start | bytes 393224 | tf_op jit(solution)/shard_map/ppermute | solution.py:280
  42.7 3.2 %collective-permute-done.7.refs_1_ = bf16[64,8,128]{2,1,0:T(8,128)(2,1)S(1)} collective-permute-done((bf16[64,8,128]{2,1,0:T(8,128)(2,1)S(1)}, bf16[64,8,128]{2,1,0:T(8,128)(2,1)S(1)}, u32[]{:S(2)}, u32[]{:S(2)}) %collective-permute-start.7) | collective-permute-done | bytes 131104 | tf_op jit(solution)/shard_map/ppermute | solution.py:280
  45.9 7.2 %collective-permute-done.8.refs_2_ = bf16[64,8,128]{2,1,0:T(8,128)(2,1)S(1)} collective-permute-done((bf16[64,8,128]{2,1,0:T(8,128)(2,1)S(1)}, bf16[64,8,128]{2,1,0:T(8,128)(2,1)S(1)}, u32[]{:S(2)}, u32[]{:S(2)}) %collective-permute-start.8) | collective-permute-done | bytes 131104 | tf_op jit(solution)/shard_map/ppermute | solution.py:280
  53.1 1.0 %place.1 = bf16[64,32,128]{2,1,0:T(8,128)(2,1)} custom-call(bf16[64,8,128]{2,1,0:T(8,128)(2,1)S(1)} %get-tuple-element.43.refs_0_, bf16[64,8,128]{2,1,0:T(8,128)(2,1)S(1)} %collective-permute-done.7.refs_1_, bf16[64,8,128]{2,1,0:T(8,128)(2,1)S(1)} %collective-permute-done.8.refs_2_, bf16[64,8,128]{2,1,0:T(8,128)(2,1)S(1)} %collective-permute-done.9.refs_3_), custom_call_target="tpu_custom_call" | custom-call | tf_op jit(solution)/shard_map/place/pallas_call | solution.py:369
  (21 shorter events, 0.1 us)
Async XLA Ops:
  3.6 9.2 %collective-permute-start = (bf16[576,128]{1,0:T(8,128)(2,1)}, bf16[576,128]{1,0:T(8,128)(2,1)S(1)}, u32[]{:S(2)}, u32[]{:S(2)}) collective-permute-start(bf16[576,128]{1,0:T(8,128)(2,1)} %get-tuple-element.27), channel_id=1, source_target_pairs={{0,8},{8,0},{16,24},{24,16},{1,9},{9,1},{17,25},{25,17},{2,10},{10... | collective-permute-start | bytes 442376 | tf_op jit(solution)/shard_map/ppermute | solution.py:280
  6.7 14.2 %collective-permute-start.1 = (bf16[576,128]{1,0:T(8,128)(2,1)}, bf16[576,128]{1,0:T(8,128)(2,1)S(1)}, u32[]{:S(2)}, u32[]{:S(2)}) collective-permute-start(bf16[576,128]{1,0:T(8,128)(2,1)} %get-tuple-element.28), channel_id=1, source_target_pairs={{0,16},{8,24},{16,0},{24,8},{1,17},{9,25},{17,1},{25,9},{2,18},{10... | collective-permute-start | bytes 442376 | tf_op jit(solution)/shard_map/ppermute | solution.py:280
  9.3 11.6 %collective-permute-start.2 = (bf16[576,128]{1,0:T(8,128)(2,1)}, bf16[576,128]{1,0:T(8,128)(2,1)S(1)}, u32[]{:S(2)}, u32[]{:S(2)}) collective-permute-start(bf16[576,128]{1,0:T(8,128)(2,1)} %get-tuple-element.29), channel_id=1, source_target_pairs={{0,24},{8,16},{16,8},{24,0},{1,25},{9,17},{17,9},{25,1},{2,26},{10... | collective-permute-start | bytes 442376 | tf_op jit(solution)/shard_map/ppermute | solution.py:280
  10.1 14.5 %copy-start = (bf16[576,128]{1,0:T(8,128)(2,1)S(1)}, bf16[576,128]{1,0:T(8,128)(2,1)}, u32[]{:S(2)}) copy-start(bf16[576,128]{1,0:T(8,128)(2,1)} %get-tuple-element.26.refs_0_) | copy-start | bytes 442372
  21.0 3.6 %copy-start.1 = (bf16[128,384]{1,0:T(8,128)(2,1)S(1)}, bf16[128,384]{1,0:T(8,128)(2,1)}, u32[]{:S(2)}) copy-start(bf16[128,384]{1,0:T(8,128)(2,1)} %refs_4_.3) | copy-start | bytes 294916
  21.0 3.6 %copy-start.2 = (bf16[128,128]{1,0:T(8,128)(2,1)S(1)}, bf16[128,128]{1,0:T(8,128)(2,1)}, u32[]{:S(2)}) copy-start(bf16[128,128]{1,0:T(8,128)(2,1)} %refs_5_.3) | copy-start | bytes 98308
  21.0 3.6 %copy-start.3 = (f32[128]{0:T(128)S(1)}, f32[128]{0:T(128)}, u32[]{:S(2)}) copy-start(f32[128]{0:T(128)} %param.17) | copy-start | bytes 1540
  21.0 4.7 %collective-permute-start.4 = (bf16[4,1,64,128]{3,2,0,1:T(8,128)(2,1)S(1)}, bf16[4,1,64,128]{3,2,0,1:T(8,128)(2,1)S(1)}, u32[]{:S(2)}, u32[]{:S(2)}) collective-permute-start(bf16[4,1,64,128]{3,2,0,1:T(8,128)(2,1)S(1)} %get-tuple-element.48), channel_id=1, source_target_pairs={{0,4},{1,5},{2,6},{3,7},{4,0},{5,1},{6,2},{7,3},{8,12},{9,13},{10,... | collective-permute-start | bytes 196616 | tf_op jit(solution)/shard_map/ppermute | solution.py:280
  22.6 4.3 %collective-permute-start.3 = (bf16[4,1,64,128]{3,2,0,1:T(8,128)(2,1)S(1)}, bf16[4,1,64,128]{3,2,0,1:T(8,128)(2,1)S(1)}, u32[]{:S(2)}, u32[]{:S(2)}) collective-permute-start(bf16[4,1,64,128]{3,2,0,1:T(8,128)(2,1)S(1)} %get-tuple-element.48), channel_id=1, source_target_pairs={{0,2},{1,3},{2,0},{3,1},{4,6},{5,7},{6,4},{7,5},{8,10},{9,11},{10,... | collective-permute-start | bytes 196616 | tf_op jit(solution)/shard_map/ppermute | solution.py:280
  24.1 5.2 %collective-permute-start.5 = (bf16[4,1,64,128]{3,2,0,1:T(8,128)(2,1)S(1)}, bf16[4,1,64,128]{3,2,0,1:T(8,128)(2,1)S(1)}, u32[]{:S(2)}, u32[]{:S(2)}) collective-permute-start(bf16[4,1,64,128]{3,2,0,1:T(8,128)(2,1)S(1)} %get-tuple-element.48), channel_id=1, source_target_pairs={{0,6},{1,7},{2,4},{3,5},{4,2},{5,3},{6,0},{7,1},{8,14},{9,15},{10,... | collective-permute-start | bytes 196616 | tf_op jit(solution)/shard_map/ppermute | solution.py:280
  29.3 1.6 %copy-start.4 = (bf16[128,128]{1,0:T(8,128)(2,1)S(1)}, bf16[128,128]{1,0:T(8,128)(2,1)}, u32[]{:S(2)}) copy-start(bf16[128,128]{1,0:T(8,128)(2,1)} %refs_11_.1) | copy-start | bytes 98308
  29.3 1.6 %collective-permute-start.6 = (bf16[4,4,1,64,128]{4,3,2,1,0:T(8,128)(2,1)S(1)}, bf16[4,4,1,64,128]{4,3,2,1,0:T(8,128)(2,1)S(1)}, u32[]{:S(2)}, u32[]{:S(2)}) collective-permute-start(bf16[4,4,1,64,128]{4,3,2,1,0:T(8,128)(2,1)S(1)} %pad_maximum_fusion.refs_8_), channel_id=1, source_target_pairs={{0,1},{1,0},{2,3},{3,2},{4,5},{5,4},{6,7},{7,6},{8,9},{9,8},{10,11... | collective-permute-start | bytes 786440 | tf_op jit(solution)/shard_map/ppermute | solution.py:280
  30.9 0.7 %copy-start.5 = (s32[256]{0:T(256)S(1)}, s32[256]{0:T(256)}, u32[]{:S(2)}) copy-start(s32[256]{0:T(256)} %param.11) | copy-start | bytes 3076
  30.9 0.7 %copy-start.6 = (f32[128]{0:T(128)S(1)}, f32[128]{0:T(128)}, u32[]{:S(2)}) copy-start(f32[128]{0:T(128)} %param.19) | copy-start | bytes 1540
  37.9 8.0 %collective-permute-start.7 = (bf16[64,8,128]{2,1,0:T(8,128)(2,1)S(1)}, bf16[64,8,128]{2,1,0:T(8,128)(2,1)S(1)}, u32[]{:S(2)}, u32[]{:S(2)}) collective-permute-start(bf16[64,8,128]{2,1,0:T(8,128)(2,1)S(1)} %get-tuple-element.44), channel_id=1, source_target_pairs={{0,8},{8,0},{16,24},{24,16},{1,9},{9,1},{17,25},{25,17},{2,10},{10... | collective-permute-start | bytes 393224 | tf_op jit(solution)/shard_map/ppermute | solution.py:280
  40.2 12.9 %collective-permute-start.8 = (bf16[64,8,128]{2,1,0:T(8,128)(2,1)S(1)}, bf16[64,8,128]{2,1,0:T(8,128)(2,1)S(1)}, u32[]{:S(2)}, u32[]{:S(2)}) collective-permute-start(bf16[64,8,128]{2,1,0:T(8,128)(2,1)S(1)} %get-tuple-element.45), channel_id=1, source_target_pairs={{0,16},{8,24},{16,0},{24,8},{1,17},{9,25},{17,1},{25,9},{2,18},{10... | collective-permute-start | bytes 393224 | tf_op jit(solution)/shard_map/ppermute | solution.py:280
  41.3 11.8 %collective-permute-start.9 = (bf16[64,8,128]{2,1,0:T(8,128)(2,1)S(1)}, bf16[64,8,128]{2,1,0:T(8,128)(2,1)S(1)}, u32[]{:S(2)}, u32[]{:S(2)}) collective-permute-start(bf16[64,8,128]{2,1,0:T(8,128)(2,1)S(1)} %get-tuple-element.46), channel_id=1, source_target_pairs={{0,24},{8,16},{16,8},{24,0},{1,25},{9,17},{17,9},{25,1},{2,26},{10... | collective-permute-start | bytes 393224 | tf_op jit(solution)/shard_map/ppermute | solution.py:280

commit v3 on v2

v3 whole, which is shorter than its diff:
```python
import functools

import jax
import jax.numpy as jnp
from jax import lax
from jax.experimental import pallas as pl
from jax.experimental.pallas import tpu as pltpu
from jax.sharding import PartitionSpec as P

BF = jnp.bfloat16
F32 = jnp.float32
VMEM_LIMIT = 52 * 1024 * 1024
VMEM_ALONE = 62 * 1024 * 1024


def dot(a, b):
    return jnp.dot(a, b, preferred_element_type=F32)


def dot_t(a, b):
    return lax.dot_general(a, b, (((1,), (1,)), ((), ())), preferred_element_type=F32)


def dot_l(a, b):
    return lax.dot_general(a, b, (((0,), (0,)), ((), ())), preferred_element_type=F32)


def over(a, size):
    return lax.shift_right_logical(a, jnp.full_like(a, size.bit_length() - 1))


def below(a, size):
    return a & (size - 1)


def hop(s, parts):
    return (parts - s) % parts


def column_of(row, width):
    return jnp.broadcast_to(row, (width, row.shape[1])).T


def split_sum(a, ones):
    first = a.astype(BF)
    rest = a - first.astype(F32)
    second = rest.astype(BF)
    third = (rest - second.astype(F32)).astype(BF)
    return dot(first, ones) + dot(second, ones) + dot(third, ones)


def prep_kernel(pair_ref, gain_ref, shift_ref, wb_ref, *refs):
    parcels, (raw, gain, shift, wbt, wide, sem) = refs[:-6], refs[-6:]
    parts = len(parcels) // 2
    rows, cols, chans = pair_ref.shape
    heads = wb_ref.shape[0]
    lanes = heads * cols
    width = cols // parts
    me = lax.axis_index("row")
    step = wide.shape[0]
    half = rows // 2
    small = [
        pltpu.make_async_copy(source, target, sem.at[n])
        for n, (source, target) in enumerate(((wb_ref, wbt), (gain_ref, gain), (shift_ref, shift)))
    ]
    for copy in small:
        copy.start()

    fetches = [
        pltpu.make_async_copy(
            pair_ref.at[pl.ds(n * half, half)], raw.at[pl.ds(n * half, half)], sem.at[3 + n]
        )
        for n in range(2)
    ]
    for copy in fetches:
        copy.start()
    ones = jnp.ones((chans, chans), BF)
    lane_col = below(lax.broadcasted_iota(jnp.int32, (cols, lanes), 1), cols)
    keep = lane_col == lax.broadcasted_iota(jnp.int32, (cols, lanes), 0)
    head_of = over(lax.broadcasted_iota(jnp.int32, (lanes, heads), 0), cols)
    spread = (head_of == lax.broadcasted_iota(jnp.int32, (lanes, heads), 1)).astype(BF)
    for copy in small:
        copy.wait()
    wb = dot(spread, wbt[...]).astype(BF)

    def body(n, index, carry):
        start = pl.multiple_of(n * half + index * step, step)
        values = raw[pl.ds(start, step)].reshape(step * cols, chans)
        mean = dot(values, ones) * (1.0 / chans)
        centred = values.astype(F32) - mean
        var = split_sum(centred * centred, ones) * (1.0 / chans)
        normed = (centred * lax.rsqrt(var + 1e-05) * gain[...] + shift[...]).astype(BF)
        every = dot_t(normed, wb).reshape(step, cols, lanes)
        tile = jnp.sum(jnp.where(keep[None], every, 0.0), axis=1).astype(BF)
        wide[...] = normed.astype(F32).reshape(step, cols, chans)
        to = pl.ds(pl.multiple_of(index * (step * width), step * width), step * width)
        for s in range(parts):
            first = pl.multiple_of((me ^ hop(s, parts)) * width, width)
            chunk = wide[:, pl.ds(first, width), :].reshape(step * width, chans)
            parcels[n * parts + s][to, :] = chunk.astype(BF)
            for layer in range(lanes // chans):
                row = pl.multiple_of(half * width + rows * layer + start, step)
                parcels[s][pl.ds(row, step), :] = tile[:, layer * chans : (layer + 1) * chans]
        return carry

    for n in range(2):
        fetches[n].wait()
        lax.fori_loop(0, half // step, functools.partial(body, n), 0, unroll=rows <= 64)


def project_kernel(parts, scale, half, *refs):
    parcels = refs[:parts]
    weight, gate_bias, q_ref, k_ref, v_ref, gate_ref, wide, tokens = refs[parts:]
    width, count, inner = q_ref.shape
    me = lax.axis_index("row")
    for s in range(parts):
        wide[s] = parcels[s][0 : half * width, :].astype(F32)

    def two_columns(j, carry):
        for k in range(2):
            for s in range(parts):
                at = pl.multiple_of(k * count + (me ^ hop(s, parts)) * half, half)
                line = wide[s, pl.ds(2 * j + k, half, stride=width), :]
                tokens[pl.ds(at, half), :] = line.astype(BF)
        mixed = dot(tokens[...], weight[...])
        query = (mixed[:, 0:inner] * scale).astype(BF)
        gate = jax.nn.sigmoid(mixed[:, 3 * inner : 4 * inner] + gate_bias[...])
        for k in range(2):
            at = slice(k * count, (k + 1) * count)
            q_ref[2 * j + k] = query[at]
            k_ref[2 * j + k] = mixed[at, inner : 2 * inner].astype(BF)
            v_ref[2 * j + k] = mixed[at, 2 * inner : 3 * inner].astype(BF)
            gate_ref[2 * j + k] = gate[at]
        return carry

    lax.fori_loop(0, width // 2, two_columns, 0, unroll=2 if half <= 32 else 1)


def constants_kernel(parts, cols, lanes, *refs):
    mask_ref, wqkv_ref, wg_ref, gb_ref, wo_ref, ob_ref = refs[:6]
    weight_ref, gate_ref, out_ref, base_ref, order_ref, key_ref, mask, scratch, sem = refs[6:]
    inner = wg_ref.shape[1]
    moves = (
        (mask_ref, mask),
        (wqkv_ref, weight_ref.at[:, pl.ds(0, 3 * inner)]),
        (wg_ref, weight_ref.at[:, pl.ds(3 * inner, inner)]),
        (gb_ref, gate_ref),
        (wo_ref, out_ref),
        (ob_ref, base_ref),
    )
    copies = [
        pltpu.make_async_copy(source, target, sem.at[n])
        for n, (source, target) in enumerate(moves)
    ]
    for copy in copies:
        copy.start()
    span = order_ref.shape[0]
    source_lane = lax.broadcasted_iota(jnp.int32, (span, span), 0)
    target_lane = lax.broadcasted_iota(jnp.int32, (span, span), 1)
    tile_of, rest = over(source_lane, lanes), below(source_lane, lanes)
    wanted = over(rest, cols) * 128 + tile_of * cols + below(rest, cols)
    order_ref[...] = (wanted == target_lane).astype(BF)
    for copy in copies:
        copy.wait()
    scratch[...] = jnp.where(column_of(mask[...], 128) == 1, 0.0, -1000000000.0).astype(F32)
    count = key_ref.shape[0]
    half = count // parts // 2
    for n in range(2):
        for p in range(parts):
            key_ref[(n * parts + p) * half : (n * parts + p + 1) * half] = scratch[
                (2 * p + n) * half : (2 * p + n + 1) * half
            ]


def attend_kernel(parts, side, *refs):
    halves = refs[0:4], refs[4:8]
    tiles, out_weight, out_bias, order_ref, key_ref = refs[8:13]
    outs = refs[13 : parts + 13]
    update, bias = refs[parts + 13 :]
    width, half, inner = halves[0][0].shape
    count = 2 * half
    pairs, _, layers, rows, chans = tiles.shape
    groups = bias.shape[0]
    heads = bias.shape[2] // 128
    lanes = layers * chans
    cols = lanes // heads
    head = inner // heads
    me = lax.axis_index("row")
    col = lax.axis_index("col")
    group = 128 // cols
    batch = max(1, min(count, 256) // rows)

    def one_block(index, carry):
        g, b = index // (parts // batch), index % (parts // batch)
        block = jnp.concatenate(
            [
                tiles[g * group + t, pl.ds(b * batch, batch), n].reshape(batch * rows, chans)
                for t in range(group)
                for n in range(layers)
            ],
            axis=1,
        )
        ordered = dot(block, order_ref[...])
        for s in range(batch):
            for n in range(2):
                at = n * half + (me ^ hop(b * batch + s, parts)) * cols
                at = pl.ds(pl.multiple_of(at, cols), cols)
                low = s * rows + n * cols
                for h in range(heads):
                    across = slice(h * 128, (h + 1) * 128)
                    bias[g, at, across] = ordered[low : low + cols, across] + key_ref[at, :]
        return carry

    blocks = groups * (parts // batch)
    lax.fori_loop(0, blocks, one_block, 0, unroll=blocks <= 2)

    lane_head = over(lax.broadcasted_iota(jnp.int32, (1, inner), 1), head)
    odd = (col & 1) ^ side

    def one_column(j, carry):
        keys = jnp.concatenate([halves[0][1][j], halves[1][1][j]], axis=0)
        vals = jnp.concatenate([halves[0][2][j], halves[1][2][j]], axis=0)

        def one_group(g, inside):
            places = [
                pl.ds(pl.multiple_of((over(col, 2) ^ (g * group + t)) * cols, cols), cols)
                for t in range(group)
            ]

            def gathered(n):
                both = [
                    jnp.concatenate([halves[k][n][j, at, :] for at in places], axis=0)
                    for k in range(2)
                ]
                return jnp.where(odd == 1, both[1], both[0])

            query = gathered(0)
            gate = gathered(3)
            blank = jnp.zeros_like(query)
            attended = jnp.zeros((128, inner), F32)
            for h in range(0, heads, 2):
                some = jnp.concatenate(
                    [jnp.where(lane_head == n, query, blank) for n in (h, h + 1)], axis=0
                )
                scores = dot_t(keys, some) + bias[g, :, h * 128 : (h + 2) * 128]
                top = jnp.max(scores, axis=0, keepdims=True)
                expo = jnp.exp(scores - top)
                total = jnp.sum(expo, axis=0, keepdims=True)
                weights = (expo * (1.0 / total)).astype(BF)
                heard = dot_l(weights, vals)
                attended = jnp.where(lane_head == h, heard[0:128], attended)
                attended = jnp.where(lane_head == h + 1, heard[128:256], attended)
            gated = (gate * attended.astype(BF).astype(F32)).astype(BF)
            result = dot(gated, out_weight[...]) + out_bias[...]
            update[pl.ds(g * 128 * width + j, 128, stride=width), :] = result
            return inside

        lax.fori_loop(0, groups, one_group, 0, unroll=groups == 1)
        return carry

    lax.fori_loop(0, width, one_column, 0, unroll=width if groups == 1 else 1)
    for s in range(parts):
        at = (hop(s, parts) ^ me ^ over(col, 2)) * (cols * width)
        at = pl.ds(pl.multiple_of(at, cols * width), cols * width)
        outs[s][...] = update[at, :].astype(BF).reshape(cols, width, chans)


def place_kernel(parts, *refs):
    out_ref, wide = refs[2 * parts :]
    rows, cols, chans = out_ref.shape
    width = cols // parts
    me = lax.axis_index("row")
    odd = lax.axis_index("col") & 1
    step = wide.shape[1]

    def body(index, carry):
        for side in range(2):
            for s in range(parts):
                first = pl.multiple_of((me ^ hop(s, parts)) * width, width)
                at = pl.ds(pl.multiple_of(index * step, step), step)
                wide[side, :, pl.ds(first, width), :] = refs[side * parts + s][at].astype(F32)
            at = pl.multiple_of((odd ^ side) * (rows // 2) + index * step, step)
            out_ref[pl.ds(at, step)] = wide[side].astype(BF)
        return carry

    lax.fori_loop(0, rows // 2 // step, body, 0, unroll=rows <= 64)


def per_device(
    pair, token_mask, ln_gain, ln_shift, w_qkv, w_bias, w_gate, gate_bias, w_out, out_bias
):
    rows, cols, chans = pair.shape
    heads = w_bias.shape[1]
    inner = w_gate.shape[1]
    parts = lax.axis_size("row")
    col_count = lax.axis_size("col")
    count = rows * parts
    width = cols // parts
    lanes = heads * cols
    vmem = pl.BlockSpec(memory_space=pltpu.VMEM)
    hbm = pl.BlockSpec(memory_space=pltpu.HBM)
    large = count > 256
    params = pltpu.CompilerParams(vmem_limit_bytes=VMEM_LIMIT if large else VMEM_LIMIT // 4)
    alone = pltpu.CompilerParams(vmem_limit_bytes=VMEM_ALONE)

    def swap(x, axis, offset):
        size = lax.axis_size(axis)
        return lax.ppermute(x, axis, [(i, i ^ offset) for i in range(size)])

    layers = lanes // chans
    step = min(rows, 16)
    half = rows // 2
    parcels = pl.pallas_call(
        prep_kernel,
        out_shape=[jax.ShapeDtypeStruct((half * width + rows * layers, chans), BF)] * parts
        + [jax.ShapeDtypeStruct((half * width, chans), BF)] * parts,
        in_specs=[hbm] * 4,
        out_specs=[vmem] * (2 * parts),
        scratch_shapes=[
            pltpu.VMEM((rows, cols, chans), BF),
            pltpu.VMEM((1, chans), F32),
            pltpu.VMEM((1, chans), F32),
            pltpu.VMEM((heads, chans), BF),
            pltpu.VMEM((step, cols, chans), F32),
            pltpu.SemaphoreType.DMA((5,)),
        ],
        compiler_params=alone,
        name="prep",
    )(pair, ln_gain.reshape(1, chans), ln_shift.reshape(1, chans), w_bias.T)

    span = (128 // cols) * lanes
    shared = pl.pallas_call(
        functools.partial(constants_kernel, parts, cols, lanes),
        out_shape=[
            jax.ShapeDtypeStruct((chans, 4 * inner), BF),
            jax.ShapeDtypeStruct((1, inner), F32),
            jax.ShapeDtypeStruct((inner, chans), BF),
            jax.ShapeDtypeStruct((1, chans), F32),
            jax.ShapeDtypeStruct((span, span), BF),
            jax.ShapeDtypeStruct((count, 128), F32),
        ],
        in_specs=[hbm] * 6,
        out_specs=[vmem] * 6,
        scratch_shapes=[
            pltpu.VMEM((1, count), jnp.int32),
            pltpu.VMEM((count, 128), F32),
            pltpu.SemaphoreType.DMA((6,)),
        ],
        cost_estimate=pl.CostEstimate(
            flops=span * span * 8, bytes_accessed=span * span * 2, transcendentals=0
        ),
        compiler_params=params,
        name="constants",
    )(
        token_mask.reshape(1, count),
        w_qkv,
        w_gate,
        gate_bias.reshape(1, inner),
        w_out,
        out_bias.reshape(1, chans),
    )

    def back(pieces):
        return [pieces[0]] + [swap(pieces[s], "row", hop(s, parts)) for s in range(1, parts)]

    early = back(parcels[:parts])
    shared, *waiting = lax.optimization_barrier((shared, *parcels[parts:]))
    late = back(waiting)

    def project(pieces):
        return pl.pallas_call(
            functools.partial(project_kernel, parts, (inner // heads) ** (-0.5), half),
            out_shape=[jax.ShapeDtypeStruct((width, count // 2, inner), BF)] * 3
            + [jax.ShapeDtypeStruct((width, count // 2, inner), F32)],
            in_specs=[vmem] * (parts + 2),
            out_specs=[vmem] * 4,
            scratch_shapes=[
                pltpu.VMEM((parts, half * width, chans), F32),
                pltpu.VMEM((count, chans), BF),
            ],
            cost_estimate=pl.CostEstimate(
                flops=4 * width * count * chans * inner,
                bytes_accessed=width * count * (chans + 5 * inner),
                transcendentals=width * count * inner // 2,
            ),
            compiler_params=params,
            name="project",
        )(*pieces, weight, gate_row)

    by_row = jnp.stack([p[half * width :].reshape(layers, rows, chans) for p in early])
    weight, gate_row, *shared = shared
    from_chips = [swap(by_row, "col", 2 * t) for t in range(1, col_count // 2)]
    first = project(early)
    second = project(late)
    from_chips, second = lax.optimization_barrier((from_chips, second))
    by_chip = jnp.stack([by_row] + from_chips)
    other = swap(by_chip, "col", 1)

    block = jax.ShapeDtypeStruct((cols, width, chans), BF)

    def attend(side, tiles):
        return pl.pallas_call(
            functools.partial(attend_kernel, parts, side),
            out_shape=[block] * parts,
            in_specs=[vmem] * 13,
            out_specs=[vmem] * parts,
            scratch_shapes=[
                pltpu.VMEM((count // 2 * width, chans), F32),
                pltpu.VMEM((count // 256, count, heads * 128), F32),
            ],
            cost_estimate=pl.CostEstimate(
                flops=4 * width * count * count * inner,
                bytes_accessed=width * count * 8 * inner,
                transcendentals=width * heads * count * count // 2,
            ),
            compiler_params=params,
            name="attend",
        )(*first, *second, tiles, *shared)

    same = back(attend(0, by_chip))
    crossed = back(attend(1, other))
    return pl.pallas_call(
        functools.partial(place_kernel, parts),
        out_shape=jax.ShapeDtypeStruct((rows, cols, chans), BF),
        in_specs=[vmem] * (2 * parts),
        out_specs=vmem,
        scratch_shapes=[pltpu.VMEM((2, min(rows // 2, 16), cols, chans), F32)],
        compiler_params=params,
        name="place",
    )(*same, *crossed)


def solution(mesh):
    in_specs = (P("row", "col", None), P(), P(), P(), P(), P(), P(), P(), P(), P())
    out_specs = P("row", "col", None)
    return jax.shard_map(
        per_device, mesh=mesh, in_specs=in_specs, out_specs=out_specs, check_vma=False
    )
```

time: 54.3 us -> 50.1 us (0.923)
  waiting for transfers between devices: 26 us -> 10.4 us
  starting transfers between devices: 14.1 us -> 24 us
  Pallas kernels: 12.4 us -> 14.7 us
  local copies, waits for them, and re-layouts: 1.43 us -> 0.69 us
    ppermute x10 -> x16, waiting for transfers between devices: 26 us -> 10.4 us  [swap(): return lax.ppermute(x, axis, [(i, i ^ offset) for i in range(size)])]
    ppermute x10 -> x16, starting transfers between devices: 14.1 us -> 24 us  [swap(): return lax.ppermute(x, axis, [(i, i ^ offset) for i in range(size)])]
    pallas_call x3 -> x5, Pallas kernels: 10.9 us -> 13.4 us  [the longest x2 8.44 us: attend(): pl.pallas_call(functools.partial(attend_kernel, parts, side), out_shape=[...]
    another operation x4, local copies, waits for them, and re-layouts: 0.73 us -> 0.01 us  [per_device(): jnp.stack([p[half * width:].reshape(layers, rows, chans) for p in early])]
  transfers between devices with their start and end apart: 10 -> 16, of which waited for: 8 -> 6; matrix products, arithmetic and copies ran while one was open for 1% -> 0% of each run, Pallas kernels for 3% -> 20%
where the time goes in v3:
time: 50.1 us; the launch traced here: 50 us
  starting transfers between devices  24 us (48%)
  Pallas kernels  14.7 us (29%)
  waiting for transfers between devices  10.4 us (21%)
  local copies, waits for them, and re-layouts  0.69 us (1%)
    ppermute x16, starting transfers between devices, swap(): return lax.ppermute(x, axis, [(i, i ^ offset) for i in range(size)])  24 us
    ppermute x16, waiting for transfers between devices, swap(): return lax.ppermute(x, axis, [(i, i ^ offset) for i in range(size)])  10.4 us
    pallas_call x2, Pallas kernels, attend(): pl.pallas_call(functools.partial(attend_kernel, parts, side), out_shape=[...  8.44 us
    pallas_call x1, Pallas kernels, per_device(): pl.pallas_call(prep_kernel, out_shape=[jax.ShapeDtypeStruct((half * width...  3.61 us
    pallas_call x2, Pallas kernels, project(): pl.pallas_call(functools.partial(project_kernel, parts, (inner // heads)...  1.3 us
  transfers between devices with their start and end apart: 16, of which 6 were waited for; matrix products, arithmetic and copies ran while one was open for 0% of the time, Pallas kernels for 20%

profile of v3, /device:TPU:0, one launch (start us, length us, event | category | flops | bytes accessed | tf_op | source)
XLA Modules:
  0.0 50.0 jit_solution(347359009139539121)
XLA Ops:
  0.0 3.6 %prep.1 = (bf16[320,128]{1,0:T(8,128)(2,1)}, bf16[320,128]{1,0:T(8,128)(2,1)}, bf16[320,128]{1,0:T(8,128)(2,1)}, bf16[320,128]{1,0:T(8,128)(2,1)}, bf16[256,128]...) custom-call(bf16[64,32,128]{2,1,0:T(8,128)(2,1)} %pair_ref.1, ...), custom_call_target="tpu_custom_call" | custom-call | tf_op jit(solution)/shard_map/prep/pallas_call | solution.py:313
  3.6 5.1 %collective-permute-start = (bf16[320,128]{1,0:T(8,128)(2,1)}, bf16[320,128]{1,0:T(8,128)(2,1)S(1)}, u32[]{:S(2)}, u32[]{:S(2)}) collective-permute-start(bf16[320,128]{1,0:T(8,128)(2,1)} %get-tuple-element.53), channel_id=1, source_target_pairs={{0,24},{8,16},{16,8},{24,0},{1,25},{9,17},{17,9},{25,1},{2,26},{10... | collective-permute-start | bytes 245768 | tf_op jit(solution)/shard_map/ppermute | solution.py:308
  8.8 0.6 %collective-permute-start.2 = (bf16[320,128]{1,0:T(8,128)(2,1)}, bf16[320,128]{1,0:T(8,128)(2,1)S(1)}, u32[]{:S(2)}, u32[]{:S(2)}) collective-permute-start(bf16[320,128]{1,0:T(8,128)(2,1)} %get-tuple-element.55), channel_id=1, source_target_pairs={{0,8},{8,0},{16,24},{24,16},{1,9},{9,1},{17,25},{25,17},{2,10},{10... | collective-permute-start | bytes 245768 | tf_op jit(solution)/shard_map/ppermute | solution.py:308
  9.4 0.6 %copy-done.4 = s32[256]{0:T(256)S(1)} copy-done((s32[256]{0:T(256)S(1)}, s32[256]{0:T(256)}, u32[]{:S(2)}) %copy-start.4) | copy-done | bytes 1048
  10.5 3.8 %collective-permute-start.6 = (bf16[256,128]{1,0:T(8,128)(2,1)}, bf16[256,128]{1,0:T(8,128)(2,1)S(1)}, u32[]{:S(2)}, u32[]{:S(2)}) collective-permute-start(bf16[256,128]{1,0:T(8,128)(2,1)} %get-tuple-element.73), channel_id=1, source_target_pairs={{0,24},{8,16},{16,8},{24,0},{1,25},{9,17},{17,9},{25,1},{2,26},{10... | collective-permute-start | bytes 196616 | tf_op jit(solution)/shard_map/ppermute | solution.py:308
  14.3 1.9 %collective-permute-start.8 = (bf16[256,128]{1,0:T(8,128)(2,1)S(1)}, bf16[256,128]{1,0:T(8,128)(2,1)S(1)}, u32[]{:S(2)}, u32[]{:S(2)}) collective-permute-start(bf16[256,128]{1,0:T(8,128)(2,1)S(1)} %copy-done.8), channel_id=1, source_target_pairs={{0,8},{8,0},{16,24},{24,16},{1,9},{9,1},{17,25},{25,17},{2,10},{10... | collective-permute-start | bytes 196616 | tf_op jit(solution)/shard_map/ppermute | solution.py:308
  16.2 3.2 %collective-permute-done.1.refs_2_ = bf16[320,128]{1,0:T(8,128)(2,1)S(1)} collective-permute-done((bf16[320,128]{1,0:T(8,128)(2,1)}, bf16[320,128]{1,0:T(8,128)(2,1)S(1)}, u32[]{:S(2)}, u32[]{:S(2)}) %collective-permute-start.1) | collective-permute-done | bytes 81952 | tf_op jit(solution)/shard_map/ppermute | solution.py:308
  19.5 2.4 %collective-permute-start.5 = (bf16[4,1,64,128]{3,2,0,1:T(8,128)(2,1)S(1)}, bf16[4,1,64,128]{3,2,0,1:T(8,128)(2,1)S(1)}, u32[]{:S(2)}, u32[]{:S(2)}) collective-permute-start(bf16[4,1,64,128]{3,2,0,1:T(8,128)(2,1)S(1)} %get-tuple-element.100), channel_id=1, source_target_pairs={{0,6},{1,7},{2,4},{3,5},{4,2},{5,3},{6,0},{7,1},{8,14},{9,15},{10,... | collective-permute-start | bytes 196616 | tf_op jit(solution)/shard_map/ppermute | solution.py:308
  21.8 0.5 %collective-permute-start.4 = (bf16[4,1,64,128]{3,2,0,1:T(8,128)(2,1)S(1)}, bf16[4,1,64,128]{3,2,0,1:T(8,128)(2,1)S(1)}, u32[]{:S(2)}, u32[]{:S(2)}) collective-permute-start(bf16[4,1,64,128]{3,2,0,1:T(8,128)(2,1)S(1)} %get-tuple-element.100), channel_id=1, source_target_pairs={{0,4},{1,5},{2,6},{3,7},{4,0},{5,1},{6,2},{7,3},{8,12},{9,13},{10,... | collective-permute-start | bytes 196616 | tf_op jit(solution)/shard_map/ppermute | solution.py:308
  22.4 0.7 %collective-permute-start.3 = (bf16[4,1,64,128]{3,2,0,1:T(8,128)(2,1)S(1)}, bf16[4,1,64,128]{3,2,0,1:T(8,128)(2,1)S(1)}, u32[]{:S(2)}, u32[]{:S(2)}) collective-permute-start(bf16[4,1,64,128]{3,2,0,1:T(8,128)(2,1)S(1)} %get-tuple-element.100), channel_id=1, source_target_pairs={{0,2},{1,3},{2,0},{3,1},{4,6},{5,7},{6,4},{7,5},{8,10},{9,11},{10,... | collective-permute-start | bytes 196616 | tf_op jit(solution)/shard_map/ppermute | solution.py:308
  23.0 0.6 %project.3 = (bf16[8,128,128]{2,1,0:T(8,128)(2,1)S(1)}, bf16[8,128,128]{2,1,0:T(8,128)(2,1)S(1)}, bf16[8,128,128]{2,1,0:T(8,128)(2,1)S(1)}, f32[8,128,128]{2,1,0:T(8,128)S(1)}) custom-call(bf16[256,128]{1,0:T(8,128)(2,1)S(1)} %copy-done.7, bf16[256,128]{1,0:T(8,128)(2,1)S(1)} %collective-permute-done.6.refs_1_, ...), custom_call_target="tpu_custom_call" | custom-call | flops 134217728 | bytes 1572864 | tf_op jit(solution)/shard_map/project/pallas_call | solution.py:371
  23.7 1.0 %collective-permute-done.5 = bf16[4,1,64,128]{3,2,0,1:T(8,128)(2,1)S(1)} collective-permute-done((bf16[4,1,64,128]{3,2,0,1:T(8,128)(2,1)S(1)}, bf16[4,1,64,128]{3,2,0,1:T(8,128)(2,1)S(1)}, u32[]{:S(2)}, u32[]{:S(2)}) %collective-permute-start.5) | collective-permute-done | bytes 65568 | tf_op jit(solution)/shard_map/ppermute | solution.py:308
  24.7 1.4 %collective-permute-done.4 = bf16[4,1,64,128]{3,2,0,1:T(8,128)(2,1)S(1)} collective-permute-done((bf16[4,1,64,128]{3,2,0,1:T(8,128)(2,1)S(1)}, bf16[4,1,64,128]{3,2,0,1:T(8,128)(2,1)S(1)}, u32[]{:S(2)}, u32[]{:S(2)}) %collective-permute-start.4) | collective-permute-done | bytes 65568 | tf_op jit(solution)/shard_map/ppermute | solution.py:308
  26.1 0.5 %collective-permute-done.3 = bf16[4,1,64,128]{3,2,0,1:T(8,128)(2,1)S(1)} collective-permute-done((bf16[4,1,64,128]{3,2,0,1:T(8,128)(2,1)S(1)}, bf16[4,1,64,128]{3,2,0,1:T(8,128)(2,1)S(1)}, u32[]{:S(2)}, u32[]{:S(2)}) %collective-permute-start.3) | collective-permute-done | bytes 65568 | tf_op jit(solution)/shard_map/ppermute | solution.py:308
  26.7 0.6 %project.2 = (bf16[8,128,128]{2,1,0:T(8,128)(2,1)S(1)}, bf16[8,128,128]{2,1,0:T(8,128)(2,1)S(1)}, bf16[8,128,128]{2,1,0:T(8,128)(2,1)S(1)}, f32[8,128,128]{2,1,0:T(8,128)S(1)}) custom-call(bf16[320,128]{1,0:T(8,128)(2,1)S(1)} %copy-done.3, bf16[320,128]{1,0:T(8,128)(2,1)S(1)} %collective-permute-done.refs_1_, ...), custom_call_target="tpu_custom_call" | custom-call | flops 134217728 | bytes 1572864 | tf_op jit(solution)/shard_map/project/pallas_call | solution.py:371
  27.4 4.2 %attend.2 = (bf16[32,8,128]{2,1,0:T(8,128)(2,1)S(1)}, bf16[32,8,128]{2,1,0:T(8,128)(2,1)S(1)}, bf16[32,8,128]{2,1,0:T(8,128)(2,1)S(1)}, bf16[32,8,128]{2,1,0:T(8,128)(2,1)S(1)}) custom-call(bf16[8,128,128]{2,1,0:T(8,128)(2,1)S(1)} %get-tuple-element.68.refs_0_, bf16[8,128,128]{2,1,0:T(8,128)(2,1)S(1)} %get-tuple-element.69.refs_1_, ...), custom_call_target="tpu_custom_call" | custom-call | flops 268435456 | bytes 2097152 | tf_op jit(solution)/shard_map/attend/pallas_call | solution.py:402
  31.6 3.0 %collective-permute-start.9 = (bf16[32,8,128]{2,1,0:T(8,128)(2,1)S(1)}, bf16[32,8,128]{2,1,0:T(8,128)(2,1)S(1)}, u32[]{:S(2)}, u32[]{:S(2)}) collective-permute-start(bf16[32,8,128]{2,1,0:T(8,128)(2,1)S(1)} %get-tuple-element.92), channel_id=1, source_target_pairs={{0,24},{8,16},{16,8},{24,0},{1,25},{9,17},{17,9},{25,1},{2,26},{10... | collective-permute-start | bytes 196616 | tf_op jit(solution)/shard_map/ppermute | solution.py:308
  34.6 1.4 %collective-permute-start.11 = (bf16[32,8,128]{2,1,0:T(8,128)(2,1)S(1)}, bf16[32,8,128]{2,1,0:T(8,128)(2,1)S(1)}, u32[]{:S(2)}, u32[]{:S(2)}) collective-permute-start(bf16[32,8,128]{2,1,0:T(8,128)(2,1)S(1)} %get-tuple-element.94), channel_id=1, source_target_pairs={{0,8},{8,0},{16,24},{24,16},{1,9},{9,1},{17,25},{25,17},{2,10},{10... | collective-permute-start | bytes 196616 | tf_op jit(solution)/shard_map/ppermute | solution.py:308
  36.1 4.2 %attend.3 = (bf16[32,8,128]{2,1,0:T(8,128)(2,1)S(1)}, bf16[32,8,128]{2,1,0:T(8,128)(2,1)S(1)}, bf16[32,8,128]{2,1,0:T(8,128)(2,1)S(1)}, bf16[32,8,128]{2,1,0:T(8,128)(2,1)S(1)}) custom-call(bf16[8,128,128]{2,1,0:T(8,128)(2,1)S(1)} %get-tuple-element.68.refs_0_, bf16[8,128,128]{2,1,0:T(8,128)(2,1)S(1)} %get-tuple-element.69.refs_1_, ...), custom_call_target="tpu_custom_call" | custom-call | flops 268435456 | bytes 2097152 | tf_op jit(solution)/shard_map/attend/pallas_call | solution.py:402
  40.3 3.0 %collective-permute-start.13 = (bf16[32,8,128]{2,1,0:T(8,128)(2,1)S(1)}, bf16[32,8,128]{2,1,0:T(8,128)(2,1)S(1)}, u32[]{:S(2)}, u32[]{:S(2)}) collective-permute-start(bf16[32,8,128]{2,1,0:T(8,128)(2,1)S(1)} %get-tuple-element.96), channel_id=1, source_target_pairs={{0,24},{8,16},{16,8},{24,0},{1,25},{9,17},{17,9},{25,1},{2,26},{10... | collective-permute-start | bytes 196616 | tf_op jit(solution)/shard_map/ppermute | solution.py:308
  43.3 1.4 %collective-permute-start.15 = (bf16[32,8,128]{2,1,0:T(8,128)(2,1)S(1)}, bf16[32,8,128]{2,1,0:T(8,128)(2,1)S(1)}, u32[]{:S(2)}, u32[]{:S(2)}) collective-permute-start(bf16[32,8,128]{2,1,0:T(8,128)(2,1)S(1)} %get-tuple-element.98), channel_id=1, source_target_pairs={{0,8},{8,0},{16,24},{24,16},{1,9},{9,1},{17,25},{25,17},{2,10},{10... | collective-permute-start | bytes 196616 | tf_op jit(solution)/shard_map/ppermute | solution.py:308
  44.8 1.9 %collective-permute-done.13.refs_5_ = bf16[32,8,128]{2,1,0:T(8,128)(2,1)S(1)} collective-permute-done((bf16[32,8,128]{2,1,0:T(8,128)(2,1)S(1)}, bf16[32,8,128]{2,1,0:T(8,128)(2,1)S(1)}, u32[]{:S(2)}, u32[]{:S(2)}) %collective-permute-start.13) | collective-permute-done | bytes 65568 | tf_op jit(solution)/shard_map/ppermute | solution.py:308
  46.7 2.3 %collective-permute-done.14.refs_6_ = bf16[32,8,128]{2,1,0:T(8,128)(2,1)S(1)} collective-permute-done((bf16[32,8,128]{2,1,0:T(8,128)(2,1)S(1)}, bf16[32,8,128]{2,1,0:T(8,128)(2,1)S(1)}, u32[]{:S(2)}, u32[]{:S(2)}) %collective-permute-start.14) | collective-permute-done | bytes 65568 | tf_op jit(solution)/shard_map/ppermute | solution.py:308
  49.0 1.0 %place.1 = bf16[64,32,128]{2,1,0:T(8,128)(2,1)} custom-call(bf16[32,8,128]{2,1,0:T(8,128)(2,1)S(1)} %get-tuple-element.91.refs_0_, bf16[32,8,128]{2,1,0:T(8,128)(2,1)S(1)} %collective-permute-done.9.refs_1_, bf16[32,8,128]{2,1,0:T(8,128)(2,1)S(1)} %collective-permute-done.10.refs_2_, bf16[32,8,128]{2,1,0:T(8,128)(2,1)S(1)} %collective-permute-done.11.refs_3_, ...), custom_call_target="tpu_custom_call" | custom-call | tf_op jit(solution)/shard_map/place/pallas_call | solution.py:422
  (39 shorter events, 0.6 us)
Async XLA Ops:
  0.0 9.4 %copy-start = (bf16[128,384]{1,0:T(8,128)(2,1)S(1)}, bf16[128,384]{1,0:T(8,128)(2,1)}, u32[]{:S(2)}) copy-start(bf16[128,384]{1,0:T(8,128)(2,1)} %refs_1_.1) | copy-start | bytes 294916
  0.0 9.4 %copy-start.1 = (bf16[128,128]{1,0:T(8,128)(2,1)S(1)}, bf16[128,128]{1,0:T(8,128)(2,1)}, u32[]{:S(2)}) copy-start(bf16[128,128]{1,0:T(8,128)(2,1)} %refs_2_.1) | copy-start | bytes 98308
  0.0 9.4 %copy-start.2 = (bf16[128,128]{1,0:T(8,128)(2,1)S(1)}, bf16[128,128]{1,0:T(8,128)(2,1)}, u32[]{:S(2)}) copy-start(bf16[128,128]{1,0:T(8,128)(2,1)} %refs_4_.1) | copy-start | bytes 98308
  3.6 10.7 %collective-permute-start = (bf16[320,128]{1,0:T(8,128)(2,1)}, bf16[320,128]{1,0:T(8,128)(2,1)S(1)}, u32[]{:S(2)}, u32[]{:S(2)}) collective-permute-start(bf16[320,128]{1,0:T(8,128)(2,1)} %get-tuple-element.53), channel_id=1, source_target_pairs={{0,24},{8,16},{16,8},{24,0},{1,25},{9,17},{17,9},{25,1},{2,26},{10... | collective-permute-start | bytes 245768 | tf_op jit(solution)/shard_map/ppermute | solution.py:308
  8.7 10.7 %collective-permute-start.1 = (bf16[320,128]{1,0:T(8,128)(2,1)}, bf16[320,128]{1,0:T(8,128)(2,1)S(1)}, u32[]{:S(2)}, u32[]{:S(2)}) collective-permute-start(bf16[320,128]{1,0:T(8,128)(2,1)} %get-tuple-element.54), channel_id=1, source_target_pairs={{0,16},{8,24},{16,0},{24,8},{1,17},{9,25},{17,1},{25,9},{2,18},{10... | collective-permute-start | bytes 245768 | tf_op jit(solution)/shard_map/ppermute | solution.py:308
  8.8 10.7 %collective-permute-start.2 = (bf16[320,128]{1,0:T(8,128)(2,1)}, bf16[320,128]{1,0:T(8,128)(2,1)S(1)}, u32[]{:S(2)}, u32[]{:S(2)}) collective-permute-start(bf16[320,128]{1,0:T(8,128)(2,1)} %get-tuple-element.55), channel_id=1, source_target_pairs={{0,8},{8,0},{16,24},{24,16},{1,9},{9,1},{17,25},{25,17},{2,10},{10... | collective-permute-start | bytes 245768 | tf_op jit(solution)/shard_map/ppermute | solution.py:308
  9.4 0.7 %copy-start.4 = (s32[256]{0:T(256)S(1)}, s32[256]{0:T(256)}, u32[]{:S(2)}) copy-start(s32[256]{0:T(256)} %param.11) | copy-start | bytes 3076
  9.4 0.7 %copy-start.5 = (f32[128]{0:T(128)S(1)}, f32[128]{0:T(128)}, u32[]{:S(2)}) copy-start(f32[128]{0:T(128)} %param.17) | copy-start | bytes 1540
  10.1 4.2 %copy-start.3 = (bf16[320,128]{1,0:T(8,128)(2,1)S(1)}, bf16[320,128]{1,0:T(8,128)(2,1)}, u32[]{:S(2)}) copy-start(bf16[320,128]{1,0:T(8,128)(2,1)} %get-tuple-element.52.refs_0_) | copy-start | bytes 245764
  10.1 4.2 %copy-start.8 = (bf16[256,128]{1,0:T(8,128)(2,1)S(1)}, bf16[256,128]{1,0:T(8,128)(2,1)}, u32[]{:S(2)}) copy-start(bf16[256,128]{1,0:T(8,128)(2,1)} %get-tuple-element.75) | copy-start | bytes 196612
  10.5 11.9 %collective-permute-start.6 = (bf16[256,128]{1,0:T(8,128)(2,1)}, bf16[256,128]{1,0:T(8,128)(2,1)S(1)}, u32[]{:S(2)}, u32[]{:S(2)}) collective-permute-start(bf16[256,128]{1,0:T(8,128)(2,1)} %get-tuple-element.73), channel_id=1, source_target_pairs={{0,24},{8,16},{16,8},{24,0},{1,25},{9,17},{17,9},{25,1},{2,26},{10... | collective-permute-start | bytes 196616 | tf_op jit(solution)/shard_map/ppermute | solution.py:308
  14.3 8.8 %collective-permute-start.7 = (bf16[256,128]{1,0:T(8,128)(2,1)}, bf16[256,128]{1,0:T(8,128)(2,1)S(1)}, u32[]{:S(2)}, u32[]{:S(2)}) collective-permute-start(bf16[256,128]{1,0:T(8,128)(2,1)} %get-tuple-element.74), channel_id=1, source_target_pairs={{0,16},{8,24},{16,0},{24,8},{1,17},{9,25},{17,1},{25,9},{2,18},{10... | collective-permute-start | bytes 196616 | tf_op jit(solution)/shard_map/ppermute | solution.py:308
  14.3 8.7 %collective-permute-start.8 = (bf16[256,128]{1,0:T(8,128)(2,1)S(1)}, bf16[256,128]{1,0:T(8,128)(2,1)S(1)}, u32[]{:S(2)}, u32[]{:S(2)}) collective-permute-start(bf16[256,128]{1,0:T(8,128)(2,1)S(1)} %copy-done.8), channel_id=1, source_target_pairs={{0,8},{8,0},{16,24},{24,16},{1,9},{9,1},{17,25},{25,17},{2,10},{10... | collective-permute-start | bytes 196616 | tf_op jit(solution)/shard_map/ppermute | solution.py:308
  19.4 3.6 %copy-start.7 = (bf16[256,128]{1,0:T(8,128)(2,1)S(1)}, bf16[256,128]{1,0:T(8,128)(2,1)}, u32[]{:S(2)}) copy-start(bf16[256,128]{1,0:T(8,128)(2,1)} %get-tuple-element.72.refs_0_) | copy-start | bytes 196612
  19.5 5.2 %collective-permute-start.5 = (bf16[4,1,64,128]{3,2,0,1:T(8,128)(2,1)S(1)}, bf16[4,1,64,128]{3,2,0,1:T(8,128)(2,1)S(1)}, u32[]{:S(2)}, u32[]{:S(2)}) collective-permute-start(bf16[4,1,64,128]{3,2,0,1:T(8,128)(2,1)S(1)} %get-tuple-element.100), channel_id=1, source_target_pairs={{0,6},{1,7},{2,4},{3,5},{4,2},{5,3},{6,0},{7,1},{8,14},{9,15},{10,... | collective-permute-start | bytes 196616 | tf_op jit(solution)/shard_map/ppermute | solution.py:308
  21.8 4.3 %collective-permute-start.4 = (bf16[4,1,64,128]{3,2,0,1:T(8,128)(2,1)S(1)}, bf16[4,1,64,128]{3,2,0,1:T(8,128)(2,1)S(1)}, u32[]{:S(2)}, u32[]{:S(2)}) collective-permute-start(bf16[4,1,64,128]{3,2,0,1:T(8,128)(2,1)S(1)} %get-tuple-element.100), channel_id=1, source_target_pairs={{0,4},{1,5},{2,6},{3,7},{4,0},{5,1},{6,2},{7,3},{8,12},{9,13},{10,... | collective-permute-start | bytes 196616 | tf_op jit(solution)/shard_map/ppermute | solution.py:308
  22.4 4.3 %collective-permute-start.3 = (bf16[4,1,64,128]{3,2,0,1:T(8,128)(2,1)S(1)}, bf16[4,1,64,128]{3,2,0,1:T(8,128)(2,1)S(1)}, u32[]{:S(2)}, u32[]{:S(2)}) collective-permute-start(bf16[4,1,64,128]{3,2,0,1:T(8,128)(2,1)S(1)} %get-tuple-element.100), channel_id=1, source_target_pairs={{0,2},{1,3},{2,0},{3,1},{4,6},{5,7},{6,4},{7,5},{8,10},{9,11},{10,... | collective-permute-start | bytes 196616 | tf_op jit(solution)/shard_map/ppermute | solution.py:308
  26.7 9.4 %collective-permute-start.12 = (bf16[4,4,1,64,128]{4,3,2,1,0:T(8,128)(2,1)S(1)}, bf16[4,4,1,64,128]{4,3,2,1,0:T(8,128)(2,1)S(1)}, u32[]{:S(2)}, u32[]{:S(2)}) collective-permute-start(bf16[4,4,1,64,128]{4,3,2,1,0:T(8,128)(2,1)S(1)} %pad_maximum_fusion.refs_8_), channel_id=1, source_target_pairs={{0,1},{1,0},{2,3},{3,2},{4,5},{5,4},{6,7},{7,6},{8,9},{9,8},{10,11... | collective-permute-start | bytes 786440 | tf_op jit(solution)/shard_map/ppermute | solution.py:308
  31.6 11.7 %collective-permute-start.9 = (bf16[32,8,128]{2,1,0:T(8,128)(2,1)S(1)}, bf16[32,8,128]{2,1,0:T(8,128)(2,1)S(1)}, u32[]{:S(2)}, u32[]{:S(2)}) collective-permute-start(bf16[32,8,128]{2,1,0:T(8,128)(2,1)S(1)} %get-tuple-element.92), channel_id=1, source_target_pairs={{0,24},{8,16},{16,8},{24,0},{1,25},{9,17},{17,9},{25,1},{2,26},{10... | collective-permute-start | bytes 196616 | tf_op jit(solution)/shard_map/ppermute | solution.py:308
  34.6 10.1 %collective-permute-start.10 = (bf16[32,8,128]{2,1,0:T(8,128)(2,1)S(1)}, bf16[32,8,128]{2,1,0:T(8,128)(2,1)S(1)}, u32[]{:S(2)}, u32[]{:S(2)}) collective-permute-start(bf16[32,8,128]{2,1,0:T(8,128)(2,1)S(1)} %get-tuple-element.93), channel_id=1, source_target_pairs={{0,16},{8,24},{16,0},{24,8},{1,17},{9,25},{17,1},{25,9},{2,18},{10... | collective-permute-start | bytes 196616 | tf_op jit(solution)/shard_map/ppermute | solution.py:308
  34.6 10.1 %collective-permute-start.11 = (bf16[32,8,128]{2,1,0:T(8,128)(2,1)S(1)}, bf16[32,8,128]{2,1,0:T(8,128)(2,1)S(1)}, u32[]{:S(2)}, u32[]{:S(2)}) collective-permute-start(bf16[32,8,128]{2,1,0:T(8,128)(2,1)S(1)} %get-tuple-element.94), channel_id=1, source_target_pairs={{0,8},{8,0},{16,24},{24,16},{1,9},{9,1},{17,25},{25,17},{2,10},{10... | collective-permute-start | bytes 196616 | tf_op jit(solution)/shard_map/ppermute | solution.py:308
  40.3 6.4 %collective-permute-start.13 = (bf16[32,8,128]{2,1,0:T(8,128)(2,1)S(1)}, bf16[32,8,128]{2,1,0:T(8,128)(2,1)S(1)}, u32[]{:S(2)}, u32[]{:S(2)}) collective-permute-start(bf16[32,8,128]{2,1,0:T(8,128)(2,1)S(1)} %get-tuple-element.96), channel_id=1, source_target_pairs={{0,24},{8,16},{16,8},{24,0},{1,25},{9,17},{17,9},{25,1},{2,26},{10... | collective-permute-start | bytes 196616 | tf_op jit(solution)/shard_map/ppermute | solution.py:308
  43.3 5.7 %collective-permute-start.14 = (bf16[32,8,128]{2,1,0:T(8,128)(2,1)S(1)}, bf16[32,8,128]{2,1,0:T(8,128)(2,1)S(1)}, u32[]{:S(2)}, u32[]{:S(2)}) collective-permute-start(bf16[32,8,128]{2,1,0:T(8,128)(2,1)S(1)} %get-tuple-element.97), channel_id=1, source_target_pairs={{0,16},{8,24},{16,0},{24,8},{1,17},{9,25},{17,1},{25,9},{2,18},{10... | collective-permute-start | bytes 196616 | tf_op jit(solution)/shard_map/ppermute | solution.py:308
  43.3 5.7 %collective-permute-start.15 = (bf16[32,8,128]{2,1,0:T(8,128)(2,1)S(1)}, bf16[32,8,128]{2,1,0:T(8,128)(2,1)S(1)}, u32[]{:S(2)}, u32[]{:S(2)}) collective-permute-start(bf16[32,8,128]{2,1,0:T(8,128)(2,1)S(1)} %get-tuple-element.98), channel_id=1, source_target_pairs={{0,8},{8,0},{16,24},{24,16},{1,9},{9,1},{17,25},{25,17},{2,10},{10... | collective-permute-start | bytes 196616 | tf_op jit(solution)/shard_map/ppermute | solution.py:308
  (1 other events, 0.7 us)

commit v4 on v3

--- a/solution.py
+++ b/solution.py
@@ -47,6 +47,15 @@
     second = rest.astype(BF)
     third = (rest - second.astype(F32)).astype(BF)
     return dot(first, ones) + dot(second, ones) + dot(third, ones)
+
+
+def pipelined(count, stages, lags):
+    kept = {}
+    for turn in range(count + max(lags)):
+        for k, (stage, lag) in enumerate(zip(stages, lags)):
+            if 0 <= turn - lag < count:
+                given = kept.pop((k - 1, turn - lag), ())
+                kept[k, turn - lag] = stage(turn - lag, *given)
 
 
 def prep_kernel(pair_ref, gain_ref, shift_ref, wb_ref, *refs):
@@ -57,8 +66,9 @@
     lanes = heads * cols
     width = cols // parts
     me = lax.axis_index("row")
-    step = wide.shape[0]
+    step = min(rows, 16)
     half = rows // 2
+    first_rows = rows // 4
     small = [
         pltpu.make_async_copy(source, target, sem.at[n])
         for n, (source, target) in enumerate(((wb_ref, wbt), (gain_ref, gain), (shift_ref, shift)))
@@ -83,57 +93,99 @@
         copy.wait()
     wb = dot(spread, wbt[...]).astype(BF)
 
-    def body(n, index, carry):
-        start = pl.multiple_of(n * half + index * step, step)
+    def centre(start):
         values = raw[pl.ds(start, step)].reshape(step * cols, chans)
         mean = dot(values, ones) * (1.0 / chans)
         centred = values.astype(F32) - mean
-        var = split_sum(centred * centred, ones) * (1.0 / chans)
+        return centred, split_sum(centred * centred, ones) * (1.0 / chans)
+
+    def scale(start, centred, var):
         normed = (centred * lax.rsqrt(var + 1e-05) * gain[...] + shift[...]).astype(BF)
-        every = dot_t(normed, wb).reshape(step, cols, lanes)
+        return normed, dot_t(normed, wb)
+
+    def store(start, which, normed, every):
+        every = every.reshape(step, cols, lanes)
         tile = jnp.sum(jnp.where(keep[None], every, 0.0), axis=1).astype(BF)
-        wide[...] = normed.astype(F32).reshape(step, cols, chans)
-        to = pl.ds(pl.multiple_of(index * (step * width), step * width), step * width)
+        wide[pl.ds(start, step)] = normed.astype(F32).reshape(step, cols, chans)
+        to = pl.multiple_of((start - which * first_rows) * width, step * width)
+        to = pl.ds(to, step * width)
         for s in range(parts):
             first = pl.multiple_of((me ^ hop(s, parts)) * width, width)
-            chunk = wide[:, pl.ds(first, width), :].reshape(step * width, chans)
-            parcels[n * parts + s][to, :] = chunk.astype(BF)
+            chunk = wide[pl.ds(start, step), pl.ds(first, width), :].reshape(step * width, chans)
+            parcels[which * parts + s][to, :] = chunk.astype(BF)
             for layer in range(lanes // chans):
-                row = pl.multiple_of(half * width + rows * layer + start, step)
+                row = pl.multiple_of(first_rows * width + rows * layer + start, step)
                 parcels[s][pl.ds(row, step), :] = tile[:, layer * chans : (layer + 1) * chans]
-        return carry
-
-    for n in range(2):
-        fetches[n].wait()
-        lax.fori_loop(0, half // step, functools.partial(body, n), 0, unroll=rows <= 64)
-
-
-def project_kernel(parts, scale, half, *refs):
+        return ()
+
+    if rows <= 64:
+
+        def first_stage(n):
+            if n * step in (0, half):
+                fetches[n * step // half].wait()
+            return centre(n * step)
+
+        def second_stage(n, centred, var):
+            return scale(n * step, centred, var)
+
+        def third_stage(n, normed, every):
+            return store(n * step, int(n * step >= first_rows), normed, every)
+
+        pipelined(rows // step, (first_stage, second_stage, third_stage), (0, 1, 2))
+    else:
+        for copy in fetches:
+            copy.wait()
+        for low, high, which in ((0, first_rows, 0), (first_rows, rows, 1)):
+
+            def one(index, carry, low=low, which=which):
+                start = pl.multiple_of(low + index * step, step)
+                store(start, which, *scale(start, *centre(start)))
+                return carry
+
+            lax.fori_loop(0, (high - low) // step, one, 0)
+
+
+def project_kernel(parts, scale, size, *refs):
     parcels = refs[:parts]
     weight, gate_bias, q_ref, k_ref, v_ref, gate_ref, wide, tokens = refs[parts:]
     width, count, inner = q_ref.shape
+    batch = tokens.shape[1] // count
     me = lax.axis_index("row")
     for s in range(parts):
-        wide[s] = parcels[s][0 : half * width, :].astype(F32)
-
-    def two_columns(j, carry):
-        for k in range(2):
+        wide[s] = parcels[s][0 : size * width, :].astype(F32)
+
+    def lay(j):
+        for k in range(batch):
             for s in range(parts):
-                at = pl.multiple_of(k * count + (me ^ hop(s, parts)) * half, half)
-                line = wide[s, pl.ds(2 * j + k, half, stride=width), :]
-                tokens[pl.ds(at, half), :] = line.astype(BF)
-        mixed = dot(tokens[...], weight[...])
+                at = pl.multiple_of(k * count + (me ^ hop(s, parts)) * size, size)
+                line = wide[s, pl.ds(batch * j + k, size, stride=width), :]
+                tokens[j, pl.ds(at, size), :] = line.astype(BF)
+        return ()
+
+    def multiply(j):
+        return (dot(tokens[j], weight[...]),)
+
+    def store(j, mixed):
         query = (mixed[:, 0:inner] * scale).astype(BF)
         gate = jax.nn.sigmoid(mixed[:, 3 * inner : 4 * inner] + gate_bias[...])
-        for k in range(2):
+        for k in range(batch):
             at = slice(k * count, (k + 1) * count)
-            q_ref[2 * j + k] = query[at]
-            k_ref[2 * j + k] = mixed[at, inner : 2 * inner].astype(BF)
-            v_ref[2 * j + k] = mixed[at, 2 * inner : 3 * inner].astype(BF)
-            gate_ref[2 * j + k] = gate[at]
-        return carry
-
-    lax.fori_loop(0, width // 2, two_columns, 0, unroll=2 if half <= 32 else 1)
+            q_ref[batch * j + k] = query[at]
+            k_ref[batch * j + k] = mixed[at, inner : 2 * inner].astype(BF)
+            v_ref[batch * j + k] = mixed[at, 2 * inner : 3 * inner].astype(BF)
+            gate_ref[batch * j + k] = gate[at]
+        return ()
+
+    if count <= 256:
+        pipelined(width // batch, (lay, multiply, store), (0, 1, 2))
+    else:
+
+        def one(j, carry):
+            lay(j)
+            store(j, *multiply(j))
+            return carry
+
+        lax.fori_loop(0, width // batch, one, 0)
 
 
 def constants_kernel(parts, cols, lanes, *refs):
@@ -163,13 +215,13 @@
     for copy in copies:
         copy.wait()
     scratch[...] = jnp.where(column_of(mask[...], 128) == 1, 0.0, -1000000000.0).astype(F32)
-    count = key_ref.shape[0]
-    half = count // parts // 2
-    for n in range(2):
+    rows = key_ref.shape[0] // parts
+    first_rows = rows // 4
+    to = 0
+    for low, high in ((0, first_rows), (first_rows, rows)):
         for p in range(parts):
-            key_ref[(n * parts + p) * half : (n * parts + p + 1) * half] = scratch[
-                (2 * p + n) * half : (2 * p + n + 1) * half
-            ]
+            key_ref[to : to + high - low] = scratch[p * rows + low : p * rows + high]
+            to += high - low
 
 
 def attend_kernel(parts, side, *refs):
@@ -177,8 +229,9 @@
     tiles, out_weight, out_bias, order_ref, key_ref = refs[8:13]
     outs = refs[13 : parts + 13]
     update, bias = refs[parts + 13 :]
-    width, half, inner = halves[0][0].shape
-    count = 2 * half
+    width, early, inner = halves[0][0].shape
+    count = early + halves[1][0].shape[1]
+    first_rows = early // parts
     pairs, _, layers, rows, chans = tiles.shape
     groups = bias.shape[0]
     heads = bias.shape[2] // 128
@@ -202,13 +255,14 @@
         )
         ordered = dot(block, order_ref[...])
         for s in range(batch):
-            for n in range(2):
-                at = n * half + (me ^ hop(b * batch + s, parts)) * cols
-                at = pl.ds(pl.multiple_of(at, cols), cols)
-                low = s * rows + n * cols
+            level = me ^ hop(b * batch + s, parts)
+            for low, high, base in ((0, first_rows, 0), (first_rows, rows, early)):
+                at = pl.multiple_of(base + level * (high - low), first_rows)
+                at = pl.ds(at, high - low)
+                some = slice(s * rows + low, s * rows + high)
                 for h in range(heads):
                     across = slice(h * 128, (h + 1) * 128)
-                    bias[g, at, across] = ordered[low : low + cols, across] + key_ref[at, :]
+                    bias[g, at, across] = ordered[some, across] + key_ref[at, :]
         return carry
 
     blocks = groups * (parts // batch)
@@ -217,48 +271,72 @@
     lane_head = over(lax.broadcasted_iota(jnp.int32, (1, inner), 1), head)
     odd = (col & 1) ^ side
 
-    def one_column(j, carry):
-        keys = jnp.concatenate([halves[0][1][j], halves[1][1][j]], axis=0)
-        vals = jnp.concatenate([halves[0][2][j], halves[1][2][j]], axis=0)
-
-        def one_group(g, inside):
-            places = [
-                pl.ds(pl.multiple_of((over(col, 2) ^ (g * group + t)) * cols, cols), cols)
-                for t in range(group)
-            ]
-
-            def gathered(n):
-                both = [
-                    jnp.concatenate([halves[k][n][j, at, :] for at in places], axis=0)
-                    for k in range(2)
-                ]
-                return jnp.where(odd == 1, both[1], both[0])
-
-            query = gathered(0)
-            gate = gathered(3)
-            blank = jnp.zeros_like(query)
-            attended = jnp.zeros((128, inner), F32)
-            for h in range(0, heads, 2):
-                some = jnp.concatenate(
-                    [jnp.where(lane_head == n, query, blank) for n in (h, h + 1)], axis=0
-                )
-                scores = dot_t(keys, some) + bias[g, :, h * 128 : (h + 2) * 128]
-                top = jnp.max(scores, axis=0, keepdims=True)
-                expo = jnp.exp(scores - top)
-                total = jnp.sum(expo, axis=0, keepdims=True)
-                weights = (expo * (1.0 / total)).astype(BF)
-                heard = dot_l(weights, vals)
-                attended = jnp.where(lane_head == h, heard[0:128], attended)
-                attended = jnp.where(lane_head == h + 1, heard[128:256], attended)
-            gated = (gate * attended.astype(BF).astype(F32)).astype(BF)
-            result = dot(gated, out_weight[...]) + out_bias[...]
-            update[pl.ds(g * 128 * width + j, 128, stride=width), :] = result
-            return inside
-
-        lax.fori_loop(0, groups, one_group, 0, unroll=groups == 1)
-        return carry
-
-    lax.fori_loop(0, width, one_column, 0, unroll=width if groups == 1 else 1)
+    def query_rows(j, g, n):
+        found = []
+        for t in range(group):
+            level = over(col, 2) ^ (g * group + t)
+            base = level * (rows - first_rows)
+            spots = (0, level * first_rows), (1, base + first_rows), (1, base + odd * 2 * first_rows)
+            upper, lower, last = (
+                halves[k][n][j, pl.ds(pl.multiple_of(at, first_rows), first_rows), :]
+                for k, at in spots
+            )
+            found += [jnp.where(odd == 1, lower, upper), last]
+        return jnp.concatenate(found, axis=0)
+
+    def key_rows(j, n):
+        return jnp.concatenate([halves[0][n][j], halves[1][n][j]], axis=0)
+
+    def scores_of(j, g, h):
+        query = query_rows(j, g, 0)
+        blank = jnp.zeros_like(query)
+        pair = [jnp.where(lane_head == n, query, blank) for n in (h, h + 1)]
+        product = dot_t(key_rows(j, 1), jnp.concatenate(pair, axis=0))
+        return product + bias[g, :, h * 128 : (h + 2) * 128]
+
+    def weights_of(scores):
+        top = jnp.max(scores, axis=0, keepdims=True)
+        expo = jnp.exp(scores - top)
+        total = jnp.sum(expo, axis=0, keepdims=True)
+        return (expo * (1.0 / total)).astype(BF)
+
+    def finish(j, g, heard):
+        attended = jnp.zeros((128, inner), F32)
+        for n in range(heads):
+            part = heard[n // 2][n % 2 * 128 : (n % 2 + 1) * 128]
+            attended = jnp.where(lane_head == n, part, attended)
+        gated = (query_rows(j, g, 3) * attended.astype(BF).astype(F32)).astype(BF)
+        result = dot(gated, out_weight[...]) + out_bias[...]
+        update[pl.ds(g * 128 * width + j, 128, stride=width), :] = result
+
+    def several(columns, g):
+        steps = [(j, h) for j in columns for h in range(0, heads, 2)]
+        scores = scores_of(steps[0][0], g, steps[0][1])
+        total_steps = len(steps)
+        scores, weights, heard = {}, {}, {}
+        for n in range(-3, total_steps + 2 + 2):
+            if 0 <= n + 3 < total_steps:
+                j, h = steps[n + 3]
+                scores[n + 3] = scores_of(j, g, h)
+            if 0 <= n < total_steps:
+                weights[n] = weights_of(scores.pop(n))
+            k = n - 2
+            if 0 <= k < total_steps:
+                heard[k] = dot_l(weights.pop(k), key_rows(steps[k][0], 2))
+            k = n - 2 - 2
+            if 0 <= k < total_steps and steps[k][1] == heads - 2:
+                first = k - heads // 2 + 1
+                finish(steps[k][0], g, [heard.pop(m) for m in range(first, k + 1)])
+
+    if groups == 1:
+        several(range(width), 0)
+    else:
+
+        def one(index, carry):
+            several([index // groups], index % groups)
+            return carry
+
+        lax.fori_loop(0, width * groups, one, 0)
     for s in range(parts):
         at = (hop(s, parts) ^ me ^ over(col, 2)) * (cols * width)
         at = pl.ds(pl.multiple_of(at, cols * width), cols * width)
@@ -271,16 +349,17 @@
     width = cols // parts
     me = lax.axis_index("row")
     odd = lax.axis_index("col") & 1
-    step = wide.shape[1]
+    step = min(rows // 2, 16)
 
     def body(index, carry):
+        low = pl.multiple_of(index * step, step)
         for side in range(2):
             for s in range(parts):
                 first = pl.multiple_of((me ^ hop(s, parts)) * width, width)
-                at = pl.ds(pl.multiple_of(index * step, step), step)
-                wide[side, :, pl.ds(first, width), :] = refs[side * parts + s][at].astype(F32)
-            at = pl.multiple_of((odd ^ side) * (rows // 2) + index * step, step)
-            out_ref[pl.ds(at, step)] = wide[side].astype(BF)
+                piece = refs[side * parts + s][pl.ds(low, step)]
+                wide[side, pl.ds(low, step), pl.ds(first, width), :] = piece.astype(F32)
+            at = pl.multiple_of((odd ^ side) * (rows // 2) + low, step)
+            out_ref[pl.ds(at, step)] = wide[side, pl.ds(low, step)].astype(BF)
         return carry
 
     lax.fori_loop(0, rows // 2 // step, body, 0, unroll=rows <= 64)
@@ -308,12 +387,11 @@
         return lax.ppermute(x, axis, [(i, i ^ offset) for i in range(size)])
 
     layers = lanes // chans
-    step = min(rows, 16)
-    half = rows // 2
+    first_rows = rows // 4
     parcels = pl.pallas_call(
         prep_kernel,
-        out_shape=[jax.ShapeDtypeStruct((half * width + rows * layers, chans), BF)] * parts
-        + [jax.ShapeDtypeStruct((half * width, chans), BF)] * parts,
+        out_shape=[jax.ShapeDtypeStruct((first_rows * width + rows * layers, chans), BF)] * parts
+        + [jax.ShapeDtypeStruct(((rows - first_rows) * width, chans), BF)] * parts,
         in_specs=[hbm] * 4,
         out_specs=[vmem] * (2 * parts),
         scratch_shapes=[
@@ -321,7 +399,7 @@
             pltpu.VMEM((1, chans), F32),
             pltpu.VMEM((1, chans), F32),
             pltpu.VMEM((heads, chans), BF),
-            pltpu.VMEM((step, cols, chans), F32),
+            pltpu.VMEM((rows, cols, chans), F32),
             pltpu.SemaphoreType.DMA((5,)),
         ],
         compiler_params=alone,
@@ -367,31 +445,33 @@
     shared, *waiting = lax.optimization_barrier((shared, *parcels[parts:]))
     late = back(waiting)
 
-    def project(pieces):
+    def project(pieces, size):
+        tokens = parts * size
+        batch = max(1, 256 // tokens)
         return pl.pallas_call(
-            functools.partial(project_kernel, parts, (inner // heads) ** (-0.5), half),
-            out_shape=[jax.ShapeDtypeStruct((width, count // 2, inner), BF)] * 3
-            + [jax.ShapeDtypeStruct((width, count // 2, inner), F32)],
+            functools.partial(project_kernel, parts, (inner // heads) ** (-0.5), size),
+            out_shape=[jax.ShapeDtypeStruct((width, tokens, inner), BF)] * 3
+            + [jax.ShapeDtypeStruct((width, tokens, inner), F32)],
             in_specs=[vmem] * (parts + 2),
             out_specs=[vmem] * 4,
             scratch_shapes=[
-                pltpu.VMEM((parts, half * width, chans), F32),
-                pltpu.VMEM((count, chans), BF),
+                pltpu.VMEM((parts, size * width, chans), F32),
+                pltpu.VMEM((width // batch, tokens * batch, chans), BF),
             ],
             cost_estimate=pl.CostEstimate(
-                flops=4 * width * count * chans * inner,
-                bytes_accessed=width * count * (chans + 5 * inner),
-                transcendentals=width * count * inner // 2,
+                flops=8 * width * tokens * chans * inner,
+                bytes_accessed=width * tokens * (2 * chans + 10 * inner),
+                transcendentals=width * tokens * inner,
             ),
             compiler_params=params,
             name="project",
         )(*pieces, weight, gate_row)
 
-    by_row = jnp.stack([p[half * width :].reshape(layers, rows, chans) for p in early])
+    by_row = jnp.stack([p[first_rows * width :].reshape(layers, rows, chans) for p in early])
     weight, gate_row, *shared = shared
     from_chips = [swap(by_row, "col", 2 * t) for t in range(1, col_count // 2)]
-    first = project(early)
-    second = project(late)
+    first = project(early, first_rows)
+    second = project(late, rows - first_rows)
     from_chips, second = lax.optimization_barrier((from_chips, second))
     by_chip = jnp.stack([by_row] + from_chips)
     other = swap(by_chip, "col", 1)
@@ -424,7 +504,7 @@
         out_shape=jax.ShapeDtypeStruct((rows, cols, chans), BF),
         in_specs=[vmem] * (2 * parts),
         out_specs=vmem,
-        scratch_shapes=[pltpu.VMEM((2, min(rows // 2, 16), cols, chans), F32)],
+        scratch_shapes=[pltpu.VMEM((2, rows // 2, cols, chans), F32)],
         compiler_params=params,
         name="place",
     )(*same, *crossed)

time: 50.1 us -> 43.1 us (0.86)
  Pallas kernels: 14.7 us -> 10.7 us
  waiting for transfers between devices: 10.4 us -> 7.29 us
    pallas_call x2, Pallas kernels: 8.44 us -> 4.99 us  [attend(): pl.pallas_call(functools.partial(attend_kernel, parts, side), out_shape=[...]
    ppermute x16, waiting for transfers between devices: 10.4 us -> 7.29 us  [swap(): return lax.ppermute(x, axis, [(i, i ^ offset) for i in range(size)])]
  transfers between devices with their start and end apart: 16 -> 16, of which waited for: 6 -> 3; matrix products, arithmetic and copies ran while one was open for 0% -> 0% of each run, Pallas kernels for 20% -> 15%
where the time goes in v4:
time: 43.1 us; the launch traced here: 42.9 us
  starting transfers between devices  24 us (56%)
  Pallas kernels  10.7 us (25%)
  waiting for transfers between devices  7.29 us (17%)
  local copies, waits for them, and re-layouts  0.69 us (2%)
    ppermute x16, starting transfers between devices, swap(): return lax.ppermute(x, axis, [(i, i ^ offset) for i in range(size)])  24 us
    ppermute x16, waiting for transfers between devices, swap(): return lax.ppermute(x, axis, [(i, i ^ offset) for i in range(size)])  7.29 us
    pallas_call x2, Pallas kernels, attend(): pl.pallas_call(functools.partial(attend_kernel, parts, side), out_shape=[...  4.99 us
    pallas_call x1, Pallas kernels, per_device(): pl.pallas_call(prep_kernel, out_shape=[jax.ShapeDtypeStruct((first_rows *...  3.25 us
    pallas_call x2, Pallas kernels, project(): pl.pallas_call(functools.partial(project_kernel, parts, (inner // heads)...  1.05 us
    pallas_call x1, Pallas kernels, per_device(): pl.pallas_call(functools.partial(place_kernel, parts), out_shape=jax.Shap...  1 us
  transfers between devices with their start and end apart: 16, of which 3 were waited for; matrix products, arithmetic and copies ran while one was open for 0% of the time, Pallas kernels for 15%

profile of v4, /device:TPU:0, one launch (start us, length us, event | category | flops | bytes accessed | tf_op | source)
XLA Modules:
  0.0 42.9 jit_solution(3353918920725409836)
XLA Ops:
  0.0 3.2 %prep.1 = (bf16[192,128]{1,0:T(8,128)(2,1)}, bf16[192,128]{1,0:T(8,128)(2,1)}, bf16[192,128]{1,0:T(8,128)(2,1)}, bf16[192,128]{1,0:T(8,128)(2,1)}, bf16[384,128]...) custom-call(bf16[64,32,128]{2,1,0:T(8,128)(2,1)} %pair_ref.1, ...), custom_call_target="tpu_custom_call" | custom-call | tf_op jit(solution)/shard_map/prep/pallas_call | solution.py:391
  3.3 5.1 %collective-permute-start = (bf16[192,128]{1,0:T(8,128)(2,1)}, bf16[192,128]{1,0:T(8,128)(2,1)S(1)}, u32[]{:S(2)}, u32[]{:S(2)}) collective-permute-start(bf16[192,128]{1,0:T(8,128)(2,1)} %get-tuple-element.53), channel_id=1, source_target_pairs={{0,24},{8,16},{16,8},{24,0},{1,25},{9,17},{17,9},{25,1},{2,26},{10... | collective-permute-start | bytes 147464 | tf_op jit(solution)/shard_map/ppermute | solution.py:387
  8.4 0.6 %collective-permute-start.2 = (bf16[192,128]{1,0:T(8,128)(2,1)}, bf16[192,128]{1,0:T(8,128)(2,1)S(1)}, u32[]{:S(2)}, u32[]{:S(2)}) collective-permute-start(bf16[192,128]{1,0:T(8,128)(2,1)} %get-tuple-element.55), channel_id=1, source_target_pairs={{0,8},{8,0},{16,24},{24,16},{1,9},{9,1},{17,25},{25,17},{2,10},{10... | collective-permute-start | bytes 147464 | tf_op jit(solution)/shard_map/ppermute | solution.py:387
  9.1 0.6 %copy-done.4 = s32[256]{0:T(256)S(1)} copy-done((s32[256]{0:T(256)S(1)}, s32[256]{0:T(256)}, u32[]{:S(2)}) %copy-start.4) | copy-done | bytes 1048
  9.7 0.4 constants.1
  10.1 3.8 %collective-permute-start.6 = (bf16[384,128]{1,0:T(8,128)(2,1)}, bf16[384,128]{1,0:T(8,128)(2,1)S(1)}, u32[]{:S(2)}, u32[]{:S(2)}) collective-permute-start(bf16[384,128]{1,0:T(8,128)(2,1)} %get-tuple-element.73), channel_id=1, source_target_pairs={{0,24},{8,16},{16,8},{24,0},{1,25},{9,17},{17,9},{25,1},{2,26},{10... | collective-permute-start | bytes 294920 | tf_op jit(solution)/shard_map/ppermute | solution.py:387
  14.0 0.7 %collective-permute-start.8 = (bf16[384,128]{1,0:T(8,128)(2,1)S(1)}, bf16[384,128]{1,0:T(8,128)(2,1)S(1)}, u32[]{:S(2)}, u32[]{:S(2)}) collective-permute-start(bf16[384,128]{1,0:T(8,128)(2,1)S(1)} %copy-done.8), channel_id=1, source_target_pairs={{0,8},{8,0},{16,24},{24,16},{1,9},{9,1},{17,25},{25,17},{2,10},{10... | collective-permute-start | bytes 294920 | tf_op jit(solution)/shard_map/ppermute | solution.py:387
  14.7 2.7 %collective-permute-start.5 = (bf16[4,1,64,128]{3,2,0,1:T(8,128)(2,1)S(1)}, bf16[4,1,64,128]{3,2,0,1:T(8,128)(2,1)S(1)}, u32[]{:S(2)}, u32[]{:S(2)}) collective-permute-start(bf16[4,1,64,128]{3,2,0,1:T(8,128)(2,1)S(1)} %get-tuple-element.100), channel_id=1, source_target_pairs={{0,6},{1,7},{2,4},{3,5},{4,2},{5,3},{6,0},{7,1},{8,14},{9,15},{10,... | collective-permute-start | bytes 196616 | tf_op jit(solution)/shard_map/ppermute | solution.py:387
  17.4 0.5 %collective-permute-start.4 = (bf16[4,1,64,128]{3,2,0,1:T(8,128)(2,1)S(1)}, bf16[4,1,64,128]{3,2,0,1:T(8,128)(2,1)S(1)}, u32[]{:S(2)}, u32[]{:S(2)}) collective-permute-start(bf16[4,1,64,128]{3,2,0,1:T(8,128)(2,1)S(1)} %get-tuple-element.100), channel_id=1, source_target_pairs={{0,4},{1,5},{2,6},{3,7},{4,0},{5,1},{6,2},{7,3},{8,12},{9,13},{10,... | collective-permute-start | bytes 196616 | tf_op jit(solution)/shard_map/ppermute | solution.py:387
  17.9 1.6 %collective-permute-start.3 = (bf16[4,1,64,128]{3,2,0,1:T(8,128)(2,1)S(1)}, bf16[4,1,64,128]{3,2,0,1:T(8,128)(2,1)S(1)}, u32[]{:S(2)}, u32[]{:S(2)}) collective-permute-start(bf16[4,1,64,128]{3,2,0,1:T(8,128)(2,1)S(1)} %get-tuple-element.100), channel_id=1, source_target_pairs={{0,2},{1,3},{2,0},{3,1},{4,6},{5,7},{6,4},{7,5},{8,10},{9,11},{10,... | collective-permute-start | bytes 196616 | tf_op jit(solution)/shard_map/ppermute | solution.py:387
  19.6 2.5 %collective-permute-done.7.refs_2_ = bf16[384,128]{1,0:T(8,128)(2,1)S(1)} collective-permute-done((bf16[384,128]{1,0:T(8,128)(2,1)}, bf16[384,128]{1,0:T(8,128)(2,1)S(1)}, u32[]{:S(2)}, u32[]{:S(2)}) %collective-permute-start.7) | collective-permute-done | bytes 98336 | tf_op jit(solution)/shard_map/ppermute | solution.py:387
  22.0 0.7 %project.3 = (bf16[8,192,128]{2,1,0:T(8,128)(2,1)S(1)}, bf16[8,192,128]{2,1,0:T(8,128)(2,1)S(1)}, bf16[8,192,128]{2,1,0:T(8,128)(2,1)S(1)}, f32[8,192,128]{2,1,0:T(8,128)S(1)}) custom-call(bf16[384,128]{1,0:T(8,128)(2,1)S(1)} %copy-done.7, bf16[384,128]{1,0:T(8,128)(2,1)S(1)} %collective-permute-done.6.refs_1_, ...), custom_call_target="tpu_custom_call" | custom-call | flops 201326592 | bytes 2359296 | tf_op jit(solution)/shard_map/project/pallas_call | solution.py:451
  22.8 0.1 collective-permute-start.12
  22.9 0.3 project.2
  23.2 2.5 %attend.2 = (bf16[32,8,128]{2,1,0:T(8,128)(2,1)S(1)}, bf16[32,8,128]{2,1,0:T(8,128)(2,1)S(1)}, bf16[32,8,128]{2,1,0:T(8,128)(2,1)S(1)}, bf16[32,8,128]{2,1,0:T(8,128)(2,1)S(1)}) custom-call(bf16[8,64,128]{2,1,0:T(8,128)(2,1)S(1)} %get-tuple-element.68.refs_0_, bf16[8,64,128]{2,1,0:T(8,128)(2,1)S(1)} %get-tuple-element.69.refs_1_, ...), custom_call_target="tpu_custom_call" | custom-call | flops 268435456 | bytes 2097152 | tf_op jit(solution)/shard_map/attend/pallas_call | solution.py:482
  25.7 3.2 %collective-permute-start.9 = (bf16[32,8,128]{2,1,0:T(8,128)(2,1)S(1)}, bf16[32,8,128]{2,1,0:T(8,128)(2,1)S(1)}, u32[]{:S(2)}, u32[]{:S(2)}) collective-permute-start(bf16[32,8,128]{2,1,0:T(8,128)(2,1)S(1)} %get-tuple-element.92), channel_id=1, source_target_pairs={{0,24},{8,16},{16,8},{24,0},{1,25},{9,17},{17,9},{25,1},{2,26},{10... | collective-permute-start | bytes 196616 | tf_op jit(solution)/shard_map/ppermute | solution.py:387
  29.0 1.0 %collective-permute-start.10 = (bf16[32,8,128]{2,1,0:T(8,128)(2,1)S(1)}, bf16[32,8,128]{2,1,0:T(8,128)(2,1)S(1)}, u32[]{:S(2)}, u32[]{:S(2)}) collective-permute-start(bf16[32,8,128]{2,1,0:T(8,128)(2,1)S(1)} %get-tuple-element.93), channel_id=1, source_target_pairs={{0,16},{8,24},{16,0},{24,8},{1,17},{9,25},{17,1},{25,9},{2,18},{10... | collective-permute-start | bytes 196616 | tf_op jit(solution)/shard_map/ppermute | solution.py:387
  29.9 0.3 collective-permute-start.11
  30.2 2.5 %attend.3 = (bf16[32,8,128]{2,1,0:T(8,128)(2,1)S(1)}, bf16[32,8,128]{2,1,0:T(8,128)(2,1)S(1)}, bf16[32,8,128]{2,1,0:T(8,128)(2,1)S(1)}, bf16[32,8,128]{2,1,0:T(8,128)(2,1)S(1)}) custom-call(bf16[8,64,128]{2,1,0:T(8,128)(2,1)S(1)} %get-tuple-element.68.refs_0_, bf16[8,64,128]{2,1,0:T(8,128)(2,1)S(1)} %get-tuple-element.69.refs_1_, ...), custom_call_target="tpu_custom_call" | custom-call | flops 268435456 | bytes 2097152 | tf_op jit(solution)/shard_map/attend/pallas_call | solution.py:482
  32.7 3.2 %collective-permute-start.13 = (bf16[32,8,128]{2,1,0:T(8,128)(2,1)S(1)}, bf16[32,8,128]{2,1,0:T(8,128)(2,1)S(1)}, u32[]{:S(2)}, u32[]{:S(2)}) collective-permute-start(bf16[32,8,128]{2,1,0:T(8,128)(2,1)S(1)} %get-tuple-element.96), channel_id=1, source_target_pairs={{0,24},{8,16},{16,8},{24,0},{1,25},{9,17},{17,9},{25,1},{2,26},{10... | collective-permute-start | bytes 196616 | tf_op jit(solution)/shard_map/ppermute | solution.py:387
  36.0 1.2 %collective-permute-start.15 = (bf16[32,8,128]{2,1,0:T(8,128)(2,1)S(1)}, bf16[32,8,128]{2,1,0:T(8,128)(2,1)S(1)}, u32[]{:S(2)}, u32[]{:S(2)}) collective-permute-start(bf16[32,8,128]{2,1,0:T(8,128)(2,1)S(1)} %get-tuple-element.98), channel_id=1, source_target_pairs={{0,8},{8,0},{16,24},{24,16},{1,9},{9,1},{17,25},{25,17},{2,10},{10... | collective-permute-start | bytes 196616 | tf_op jit(solution)/shard_map/ppermute | solution.py:387
  37.2 2.2 %collective-permute-done.13.refs_5_ = bf16[32,8,128]{2,1,0:T(8,128)(2,1)S(1)} collective-permute-done((bf16[32,8,128]{2,1,0:T(8,128)(2,1)S(1)}, bf16[32,8,128]{2,1,0:T(8,128)(2,1)S(1)}, u32[]{:S(2)}, u32[]{:S(2)}) %collective-permute-start.13) | collective-permute-done | bytes 65568 | tf_op jit(solution)/shard_map/ppermute | solution.py:387
  39.3 2.6 %collective-permute-done.14.refs_6_ = bf16[32,8,128]{2,1,0:T(8,128)(2,1)S(1)} collective-permute-done((bf16[32,8,128]{2,1,0:T(8,128)(2,1)S(1)}, bf16[32,8,128]{2,1,0:T(8,128)(2,1)S(1)}, u32[]{:S(2)}, u32[]{:S(2)}) %collective-permute-start.14) | collective-permute-done | bytes 65568 | tf_op jit(solution)/shard_map/ppermute | solution.py:387
  41.9 1.0 %place.1 = bf16[64,32,128]{2,1,0:T(8,128)(2,1)} custom-call(bf16[32,8,128]{2,1,0:T(8,128)(2,1)S(1)} %get-tuple-element.91.refs_0_, bf16[32,8,128]{2,1,0:T(8,128)(2,1)S(1)} %collective-permute-done.9.refs_1_, bf16[32,8,128]{2,1,0:T(8,128)(2,1)S(1)} %collective-permute-done.10.refs_2_, bf16[32,8,128]{2,1,0:T(8,128)(2,1)S(1)} %collective-permute-done.11.refs_3_, ...), custom_call_target="tpu_custom_call" | custom-call | tf_op jit(solution)/shard_map/place/pallas_call | solution.py:502
  (39 shorter events, 0.2 us)
Async XLA Ops:
  0.0 9.0 %copy-start = (bf16[128,384]{1,0:T(8,128)(2,1)S(1)}, bf16[128,384]{1,0:T(8,128)(2,1)}, u32[]{:S(2)}) copy-start(bf16[128,384]{1,0:T(8,128)(2,1)} %refs_1_.1) | copy-start | bytes 294916
  0.0 9.0 %copy-start.2 = (bf16[128,128]{1,0:T(8,128)(2,1)S(1)}, bf16[128,128]{1,0:T(8,128)(2,1)}, u32[]{:S(2)}) copy-start(bf16[128,128]{1,0:T(8,128)(2,1)} %refs_2_.1) | copy-start | bytes 98308
  0.0 9.0 %copy-start.3 = (bf16[128,128]{1,0:T(8,128)(2,1)S(1)}, bf16[128,128]{1,0:T(8,128)(2,1)}, u32[]{:S(2)}) copy-start(bf16[128,128]{1,0:T(8,128)(2,1)} %refs_4_.1) | copy-start | bytes 98308
  3.3 10.7 %collective-permute-start = (bf16[192,128]{1,0:T(8,128)(2,1)}, bf16[192,128]{1,0:T(8,128)(2,1)S(1)}, u32[]{:S(2)}, u32[]{:S(2)}) collective-permute-start(bf16[192,128]{1,0:T(8,128)(2,1)} %get-tuple-element.53), channel_id=1, source_target_pairs={{0,24},{8,16},{16,8},{24,0},{1,25},{9,17},{17,9},{25,1},{2,26},{10... | collective-permute-start | bytes 147464 | tf_op jit(solution)/shard_map/ppermute | solution.py:387
  8.4 6.3 %collective-permute-start.1 = (bf16[192,128]{1,0:T(8,128)(2,1)}, bf16[192,128]{1,0:T(8,128)(2,1)S(1)}, u32[]{:S(2)}, u32[]{:S(2)}) collective-permute-start(bf16[192,128]{1,0:T(8,128)(2,1)} %get-tuple-element.54), channel_id=1, source_target_pairs={{0,16},{8,24},{16,0},{24,8},{1,17},{9,25},{17,1},{25,9},{2,18},{10... | collective-permute-start | bytes 147464 | tf_op jit(solution)/shard_map/ppermute | solution.py:387
  8.4 6.3 %collective-permute-start.2 = (bf16[192,128]{1,0:T(8,128)(2,1)}, bf16[192,128]{1,0:T(8,128)(2,1)S(1)}, u32[]{:S(2)}, u32[]{:S(2)}) collective-permute-start(bf16[192,128]{1,0:T(8,128)(2,1)} %get-tuple-element.55), channel_id=1, source_target_pairs={{0,8},{8,0},{16,24},{24,16},{1,9},{9,1},{17,25},{25,17},{2,10},{10... | collective-permute-start | bytes 147464 | tf_op jit(solution)/shard_map/ppermute | solution.py:387
  9.0 0.7 %copy-start.4 = (s32[256]{0:T(256)S(1)}, s32[256]{0:T(256)}, u32[]{:S(2)}) copy-start(s32[256]{0:T(256)} %param.11) | copy-start | bytes 3076
  9.0 0.7 %copy-start.5 = (f32[128]{0:T(128)S(1)}, f32[128]{0:T(128)}, u32[]{:S(2)}) copy-start(f32[128]{0:T(128)} %param.17) | copy-start | bytes 1540
  9.7 4.2 %copy-start.1 = (bf16[192,128]{1,0:T(8,128)(2,1)S(1)}, bf16[192,128]{1,0:T(8,128)(2,1)}, u32[]{:S(2)}) copy-start(bf16[192,128]{1,0:T(8,128)(2,1)} %get-tuple-element.52.refs_0_) | copy-start | bytes 147460
  9.7 4.2 %copy-start.8 = (bf16[384,128]{1,0:T(8,128)(2,1)S(1)}, bf16[384,128]{1,0:T(8,128)(2,1)}, u32[]{:S(2)}) copy-start(bf16[384,128]{1,0:T(8,128)(2,1)} %get-tuple-element.75) | copy-start | bytes 294916
  10.1 7.8 %collective-permute-start.6 = (bf16[384,128]{1,0:T(8,128)(2,1)}, bf16[384,128]{1,0:T(8,128)(2,1)S(1)}, u32[]{:S(2)}, u32[]{:S(2)}) collective-permute-start(bf16[384,128]{1,0:T(8,128)(2,1)} %get-tuple-element.73), channel_id=1, source_target_pairs={{0,24},{8,16},{16,8},{24,0},{1,25},{9,17},{17,9},{25,1},{2,26},{10... | collective-permute-start | bytes 294920 | tf_op jit(solution)/shard_map/ppermute | solution.py:387
  13.9 8.1 %collective-permute-start.7 = (bf16[384,128]{1,0:T(8,128)(2,1)}, bf16[384,128]{1,0:T(8,128)(2,1)S(1)}, u32[]{:S(2)}, u32[]{:S(2)}) collective-permute-start(bf16[384,128]{1,0:T(8,128)(2,1)} %get-tuple-element.74), channel_id=1, source_target_pairs={{0,16},{8,24},{16,0},{24,8},{1,17},{9,25},{17,1},{25,9},{2,18},{10... | collective-permute-start | bytes 294920 | tf_op jit(solution)/shard_map/ppermute | solution.py:387
  14.0 8.1 %collective-permute-start.8 = (bf16[384,128]{1,0:T(8,128)(2,1)S(1)}, bf16[384,128]{1,0:T(8,128)(2,1)S(1)}, u32[]{:S(2)}, u32[]{:S(2)}) collective-permute-start(bf16[384,128]{1,0:T(8,128)(2,1)S(1)} %copy-done.8), channel_id=1, source_target_pairs={{0,8},{8,0},{16,24},{24,16},{1,9},{9,1},{17,25},{25,17},{2,10},{10... | collective-permute-start | bytes 294920 | tf_op jit(solution)/shard_map/ppermute | solution.py:387
  14.7 7.3 %copy-start.7 = (bf16[384,128]{1,0:T(8,128)(2,1)S(1)}, bf16[384,128]{1,0:T(8,128)(2,1)}, u32[]{:S(2)}) copy-start(bf16[384,128]{1,0:T(8,128)(2,1)} %get-tuple-element.72.refs_0_) | copy-start | bytes 294916
  14.7 8.0 %collective-permute-start.5 = (bf16[4,1,64,128]{3,2,0,1:T(8,128)(2,1)S(1)}, bf16[4,1,64,128]{3,2,0,1:T(8,128)(2,1)S(1)}, u32[]{:S(2)}, u32[]{:S(2)}) collective-permute-start(bf16[4,1,64,128]{3,2,0,1:T(8,128)(2,1)S(1)} %get-tuple-element.100), channel_id=1, source_target_pairs={{0,6},{1,7},{2,4},{3,5},{4,2},{5,3},{6,0},{7,1},{8,14},{9,15},{10,... | collective-permute-start | bytes 196616 | tf_op jit(solution)/shard_map/ppermute | solution.py:387
  17.4 5.4 %collective-permute-start.4 = (bf16[4,1,64,128]{3,2,0,1:T(8,128)(2,1)S(1)}, bf16[4,1,64,128]{3,2,0,1:T(8,128)(2,1)S(1)}, u32[]{:S(2)}, u32[]{:S(2)}) collective-permute-start(bf16[4,1,64,128]{3,2,0,1:T(8,128)(2,1)S(1)} %get-tuple-element.100), channel_id=1, source_target_pairs={{0,4},{1,5},{2,6},{3,7},{4,0},{5,1},{6,2},{7,3},{8,12},{9,13},{10,... | collective-permute-start | bytes 196616 | tf_op jit(solution)/shard_map/ppermute | solution.py:387
  17.9 4.8 %collective-permute-start.3 = (bf16[4,1,64,128]{3,2,0,1:T(8,128)(2,1)S(1)}, bf16[4,1,64,128]{3,2,0,1:T(8,128)(2,1)S(1)}, u32[]{:S(2)}, u32[]{:S(2)}) collective-permute-start(bf16[4,1,64,128]{3,2,0,1:T(8,128)(2,1)S(1)} %get-tuple-element.100), channel_id=1, source_target_pairs={{0,2},{1,3},{2,0},{3,1},{4,6},{5,7},{6,4},{7,5},{8,10},{9,11},{10,... | collective-permute-start | bytes 196616 | tf_op jit(solution)/shard_map/ppermute | solution.py:387
  22.8 7.4 %collective-permute-start.12 = (bf16[4,4,1,64,128]{4,3,2,1,0:T(8,128)(2,1)S(1)}, bf16[4,4,1,64,128]{4,3,2,1,0:T(8,128)(2,1)S(1)}, u32[]{:S(2)}, u32[]{:S(2)}) collective-permute-start(bf16[4,4,1,64,128]{4,3,2,1,0:T(8,128)(2,1)S(1)} %pad_maximum_fusion.refs_8_), channel_id=1, source_target_pairs={{0,1},{1,0},{2,3},{3,2},{4,5},{5,4},{6,7},{7,6},{8,9},{9,8},{10,11... | collective-permute-start | bytes 786440 | tf_op jit(solution)/shard_map/ppermute | solution.py:387
  25.7 10.3 %collective-permute-start.9 = (bf16[32,8,128]{2,1,0:T(8,128)(2,1)S(1)}, bf16[32,8,128]{2,1,0:T(8,128)(2,1)S(1)}, u32[]{:S(2)}, u32[]{:S(2)}) collective-permute-start(bf16[32,8,128]{2,1,0:T(8,128)(2,1)S(1)} %get-tuple-element.92), channel_id=1, source_target_pairs={{0,24},{8,16},{16,8},{24,0},{1,25},{9,17},{17,9},{25,1},{2,26},{10... | collective-permute-start | bytes 196616 | tf_op jit(solution)/shard_map/ppermute | solution.py:387
  29.0 8.2 %collective-permute-start.10 = (bf16[32,8,128]{2,1,0:T(8,128)(2,1)S(1)}, bf16[32,8,128]{2,1,0:T(8,128)(2,1)S(1)}, u32[]{:S(2)}, u32[]{:S(2)}) collective-permute-start(bf16[32,8,128]{2,1,0:T(8,128)(2,1)S(1)} %get-tuple-element.93), channel_id=1, source_target_pairs={{0,16},{8,24},{16,0},{24,8},{1,17},{9,25},{17,1},{25,9},{2,18},{10... | collective-permute-start | bytes 196616 | tf_op jit(solution)/shard_map/ppermute | solution.py:387
  29.9 7.2 %collective-permute-start.11 = (bf16[32,8,128]{2,1,0:T(8,128)(2,1)S(1)}, bf16[32,8,128]{2,1,0:T(8,128)(2,1)S(1)}, u32[]{:S(2)}, u32[]{:S(2)}) collective-permute-start(bf16[32,8,128]{2,1,0:T(8,128)(2,1)S(1)} %get-tuple-element.94), channel_id=1, source_target_pairs={{0,8},{8,0},{16,24},{24,16},{1,9},{9,1},{17,25},{25,17},{2,10},{10... | collective-permute-start | bytes 196616 | tf_op jit(solution)/shard_map/ppermute | solution.py:387
  32.7 6.6 %collective-permute-start.13 = (bf16[32,8,128]{2,1,0:T(8,128)(2,1)S(1)}, bf16[32,8,128]{2,1,0:T(8,128)(2,1)S(1)}, u32[]{:S(2)}, u32[]{:S(2)}) collective-permute-start(bf16[32,8,128]{2,1,0:T(8,128)(2,1)S(1)} %get-tuple-element.96), channel_id=1, source_target_pairs={{0,24},{8,16},{16,8},{24,0},{1,25},{9,17},{17,9},{25,1},{2,26},{10... | collective-permute-start | bytes 196616 | tf_op jit(solution)/shard_map/ppermute | solution.py:387
  35.9 6.0 %collective-permute-start.14 = (bf16[32,8,128]{2,1,0:T(8,128)(2,1)S(1)}, bf16[32,8,128]{2,1,0:T(8,128)(2,1)S(1)}, u32[]{:S(2)}, u32[]{:S(2)}) collective-permute-start(bf16[32,8,128]{2,1,0:T(8,128)(2,1)S(1)} %get-tuple-element.97), channel_id=1, source_target_pairs={{0,16},{8,24},{16,0},{24,8},{1,17},{9,25},{17,1},{25,9},{2,18},{10... | collective-permute-start | bytes 196616 | tf_op jit(solution)/shard_map/ppermute | solution.py:387
  36.0 5.9 %collective-permute-start.15 = (bf16[32,8,128]{2,1,0:T(8,128)(2,1)S(1)}, bf16[32,8,128]{2,1,0:T(8,128)(2,1)S(1)}, u32[]{:S(2)}, u32[]{:S(2)}) collective-permute-start(bf16[32,8,128]{2,1,0:T(8,128)(2,1)S(1)} %get-tuple-element.98), channel_id=1, source_target_pairs={{0,8},{8,0},{16,24},{24,16},{1,9},{9,1},{17,25},{25,17},{2,10},{10... | collective-permute-start | bytes 196616 | tf_op jit(solution)/shard_map/ppermute | solution.py:387
  (1 other events, 0.7 us)

commit v5 on v4

--- a/solution.py
+++ b/solution.py
@@ -34,7 +34,7 @@
 
 
 def hop(s, parts):
-    return (parts - s) % parts
+    return (parts - s) & (parts - 1)
 
 
 def column_of(row, width):
@@ -59,8 +59,9 @@
 
 
 def prep_kernel(pair_ref, gain_ref, shift_ref, wb_ref, *refs):
-    parcels, (raw, gain, shift, wbt, wide, sem) = refs[:-6], refs[-6:]
-    parts = len(parcels) // 2
+    outs, (raw, gain, shift, wbt, wide, early, late, sem, sent) = refs[:-9], refs[-9:]
+    parts = len(outs) // 2
+    parcels = [early.at[s] for s in range(parts)] + [late.at[s] for s in range(parts)]
     rows, cols, chans = pair_ref.shape
     heads = wb_ref.shape[0]
     lanes = heads * cols
@@ -118,6 +119,15 @@
                 parcels[s][pl.ds(row, step), :] = tile[:, layer * chans : (layer + 1) * chans]
         return ()
 
+    leaving = []
+
+    def leave(n, low, size):
+        for s in range(n * parts, (n + 1) * parts):
+            at = pl.ds(low, size)
+            copy = pltpu.make_async_copy(parcels[s].at[at], outs[s].at[at], sent.at[len(leaving)])
+            copy.start()
+            leaving.append(copy)
+
     if rows <= 64:
 
         def first_stage(n):
@@ -129,7 +139,10 @@
             return scale(n * step, centred, var)
 
         def third_stage(n, normed, every):
-            return store(n * step, int(n * step >= first_rows), normed, every)
+            which = int(n * step >= first_rows)
+            store(n * step, which, normed, every)
+            leave(which, (n * step - which * first_rows) * width, step * width)
+            return ()
 
         pipelined(rows // step, (first_stage, second_stage, third_stage), (0, 1, 2))
     else:
@@ -143,6 +156,10 @@
                 return carry
 
             lax.fori_loop(0, (high - low) // step, one, 0)
+            leave(which, 0, (high - low) * width)
+    leave(0, first_rows * width, rows * (lanes // chans))
+    for copy in leaving:
+        copy.wait()
 
 
 def project_kernel(parts, scale, size, *refs):
@@ -274,7 +291,7 @@
     def query_rows(j, g, n):
         found = []
         for t in range(group):
-            level = over(col, 2) ^ (g * group + t)
+            level = over(col, 2) ^ hop(g * group + t, parts)
             base = level * (rows - first_rows)
             spots = (0, level * first_rows), (1, base + first_rows), (1, base + odd * 2 * first_rows)
             upper, lower, last = (
@@ -338,31 +355,35 @@
 
         lax.fori_loop(0, width * groups, one, 0)
     for s in range(parts):
-        at = (hop(s, parts) ^ me ^ over(col, 2)) * (cols * width)
+        at = hop(hop(s, parts) ^ me ^ over(col, 2), parts) * (cols * width)
         at = pl.ds(pl.multiple_of(at, cols * width), cols * width)
         outs[s][...] = update[at, :].astype(BF).reshape(cols, width, chans)
 
 
 def place_kernel(parts, *refs):
-    out_ref, wide = refs[2 * parts :]
+    out_ref, wide, result, sem = refs[2 * parts :]
     rows, cols, chans = out_ref.shape
     width = cols // parts
     me = lax.axis_index("row")
     odd = lax.axis_index("col") & 1
     step = min(rows // 2, 16)
-
-    def body(index, carry):
-        low = pl.multiple_of(index * step, step)
-        for side in range(2):
+    copies = []
+    for side in range(2):
+        for low in range(0, rows // 2, step):
+            lines = slice(low, low + step)
             for s in range(parts):
                 first = pl.multiple_of((me ^ hop(s, parts)) * width, width)
-                piece = refs[side * parts + s][pl.ds(low, step)]
-                wide[side, pl.ds(low, step), pl.ds(first, width), :] = piece.astype(F32)
+                piece = refs[(1 - side) * parts + s][lines]
+                wide[side, lines, pl.ds(first, width), :] = piece.astype(F32)
+            result[side, lines] = wide[side, lines].astype(BF)
             at = pl.multiple_of((odd ^ side) * (rows // 2) + low, step)
-            out_ref[pl.ds(at, step)] = wide[side, pl.ds(low, step)].astype(BF)
-        return carry
-
-    lax.fori_loop(0, rows // 2 // step, body, 0, unroll=rows <= 64)
+            copy = pltpu.make_async_copy(
+                result.at[side, pl.ds(low, step)], out_ref.at[pl.ds(at, step)], sem.at[len(copies)]
+            )
+            copy.start()
+            copies.append(copy)
+    for copy in copies:
+        copy.wait()
 
 
 def per_device(
@@ -388,19 +409,24 @@
 
     layers = lanes // chans
     first_rows = rows // 4
+    early = first_rows * width + rows * layers, chans
+    late = (rows - first_rows) * width, chans
     parcels = pl.pallas_call(
         prep_kernel,
-        out_shape=[jax.ShapeDtypeStruct((first_rows * width + rows * layers, chans), BF)] * parts
-        + [jax.ShapeDtypeStruct(((rows - first_rows) * width, chans), BF)] * parts,
+        out_shape=[jax.ShapeDtypeStruct(early, BF)] * parts
+        + [jax.ShapeDtypeStruct(late, BF)] * parts,
         in_specs=[hbm] * 4,
-        out_specs=[vmem] * (2 * parts),
+        out_specs=[hbm] * (2 * parts),
         scratch_shapes=[
             pltpu.VMEM((rows, cols, chans), BF),
             pltpu.VMEM((1, chans), F32),
             pltpu.VMEM((1, chans), F32),
             pltpu.VMEM((heads, chans), BF),
             pltpu.VMEM((rows, cols, chans), F32),
+            pltpu.VMEM((parts, *early), BF),
+            pltpu.VMEM((parts, *late), BF),
             pltpu.SemaphoreType.DMA((5,)),
+            pltpu.SemaphoreType.DMA((parts * (rows // min(rows, 16) + 1),)),
         ],
         compiler_params=alone,
         name="prep",
@@ -469,8 +495,9 @@
 
     by_row = jnp.stack([p[first_rows * width :].reshape(layers, rows, chans) for p in early])
     weight, gate_row, *shared = shared
-    from_chips = [swap(by_row, "col", 2 * t) for t in range(1, col_count // 2)]
+    from_chips = [swap(by_row, "col", 2 * hop(t, parts)) for t in range(1, parts)]
     first = project(early, first_rows)
+    late[0], first = lax.optimization_barrier((late[0], first))
     second = project(late, rows - first_rows)
     from_chips, second = lax.optimization_barrier((from_chips, second))
     by_chip = jnp.stack([by_row] + from_chips)
@@ -503,11 +530,15 @@
         functools.partial(place_kernel, parts),
         out_shape=jax.ShapeDtypeStruct((rows, cols, chans), BF),
         in_specs=[vmem] * (2 * parts),
-        out_specs=vmem,
-        scratch_shapes=[pltpu.VMEM((2, rows // 2, cols, chans), F32)],
+        out_specs=hbm,
+        scratch_shapes=[
+            pltpu.VMEM((2, rows // 2, cols, chans), F32),
+            pltpu.VMEM((2, rows // 2, cols, chans), BF),
+            pltpu.SemaphoreType.DMA((2 * (rows // 2 // min(rows // 2, 16)),)),
+        ],
         compiler_params=params,
         name="place",
-    )(*same, *crossed)
+    )(*crossed, *same)
 
 
 def solution(mesh):

time: 43.1 us -> 42.7 us (level)
  no operation moved by 1% of the time
where the time goes in v5:
time: 42.7 us; the launch traced here: 42.5 us
  starting transfers between devices  24.1 us (56%)
  Pallas kernels  10.6 us (25%)
  waiting for transfers between devices  6.93 us (16%)
  local copies, waits for them, and re-layouts  0.69 us (2%)
    ppermute x16, starting transfers between devices, swap(): return lax.ppermute(x, axis, [(i, i ^ offset) for i in range(size)])  24.1 us
    ppermute x16, waiting for transfers between devices, swap(): return lax.ppermute(x, axis, [(i, i ^ offset) for i in range(size)])  6.93 us
    pallas_call x2, Pallas kernels, attend(): pl.pallas_call(functools.partial(attend_kernel, parts, side), out_shape=[...  4.98 us
    pallas_call x1, Pallas kernels, per_device(): pl.pallas_call(prep_kernel, out_shape=[jax.ShapeDtypeStruct(early, BF)] *...  3.35 us
    pallas_call x2, Pallas kernels, project(): pl.pallas_call(functools.partial(project_kernel, parts, (inner // heads)...  1.04 us
    pallas_call x1, Pallas kernels, per_device(): pl.pallas_call(functools.partial(place_kernel, parts), out_shape=jax.Shap...  0.87 us
  transfers between devices with their start and end apart: 16, of which 3 were waited for; matrix products, arithmetic and copies ran while one was open for 0% of the time, Pallas kernels for 15%

profile of v5, /device:TPU:0, one launch (start us, length us, event | category | flops | bytes accessed | tf_op | source)
XLA Modules:
  0.0 42.5 jit_solution(435708164796492421)
XLA Ops:
  0.0 3.3 %prep.1 = (bf16[192,128]{1,0:T(8,128)(2,1)}, bf16[192,128]{1,0:T(8,128)(2,1)}, bf16[192,128]{1,0:T(8,128)(2,1)}, bf16[192,128]{1,0:T(8,128)(2,1)}, bf16[384,128]...) custom-call(bf16[64,32,128]{2,1,0:T(8,128)(2,1)} %pair_ref.1, ...), custom_call_target="tpu_custom_call" | custom-call | tf_op jit(solution)/shard_map/prep/pallas_call | solution.py:414
  3.4 5.1 %collective-permute-start = (bf16[192,128]{1,0:T(8,128)(2,1)}, bf16[192,128]{1,0:T(8,128)(2,1)S(1)}, u32[]{:S(2)}, u32[]{:S(2)}) collective-permute-start(bf16[192,128]{1,0:T(8,128)(2,1)} %get-tuple-element.69), channel_id=1, source_target_pairs={{0,24},{8,16},{16,8},{24,0},{1,25},{9,17},{17,9},{25,1},{2,26},{10... | collective-permute-start | bytes 147464 | tf_op jit(solution)/shard_map/ppermute | solution.py:408
  8.5 0.6 %collective-permute-start.2 = (bf16[192,128]{1,0:T(8,128)(2,1)}, bf16[192,128]{1,0:T(8,128)(2,1)S(1)}, u32[]{:S(2)}, u32[]{:S(2)}) collective-permute-start(bf16[192,128]{1,0:T(8,128)(2,1)} %get-tuple-element.71), channel_id=1, source_target_pairs={{0,8},{8,0},{16,24},{24,16},{1,9},{9,1},{17,25},{25,17},{2,10},{10... | collective-permute-start | bytes 147464 | tf_op jit(solution)/shard_map/ppermute | solution.py:408
  9.2 0.6 %copy-done.4 = s32[256]{0:T(256)S(1)} copy-done((s32[256]{0:T(256)S(1)}, s32[256]{0:T(256)}, u32[]{:S(2)}) %copy-start.4) | copy-done | bytes 1048
  9.8 0.4 constants.1
  10.2 3.8 %collective-permute-start.6 = (bf16[384,128]{1,0:T(8,128)(2,1)}, bf16[384,128]{1,0:T(8,128)(2,1)S(1)}, u32[]{:S(2)}, u32[]{:S(2)}) collective-permute-start(bf16[384,128]{1,0:T(8,128)(2,1)} %get-tuple-element.83), channel_id=1, source_target_pairs={{0,24},{8,16},{16,8},{24,0},{1,25},{9,17},{17,9},{25,1},{2,26},{10... | collective-permute-start | bytes 294920 | tf_op jit(solution)/shard_map/ppermute | solution.py:408
  14.1 0.7 %collective-permute-start.8 = (bf16[384,128]{1,0:T(8,128)(2,1)S(1)}, bf16[384,128]{1,0:T(8,128)(2,1)S(1)}, u32[]{:S(2)}, u32[]{:S(2)}) collective-permute-start(bf16[384,128]{1,0:T(8,128)(2,1)S(1)} %copy-done.8), channel_id=1, source_target_pairs={{0,8},{8,0},{16,24},{24,16},{1,9},{9,1},{17,25},{25,17},{2,10},{10... | collective-permute-start | bytes 294920 | tf_op jit(solution)/shard_map/ppermute | solution.py:408
  14.8 2.7 %collective-permute-start.3 = (bf16[4,1,64,128]{3,2,0,1:T(8,128)(2,1)S(1)}, bf16[4,1,64,128]{3,2,0,1:T(8,128)(2,1)S(1)}, u32[]{:S(2)}, u32[]{:S(2)}) collective-permute-start(bf16[4,1,64,128]{3,2,0,1:T(8,128)(2,1)S(1)} %get-tuple-element.110), channel_id=1, source_target_pairs={{0,6},{1,7},{2,4},{3,5},{4,2},{5,3},{6,0},{7,1},{8,14},{9,15},{10,... | collective-permute-start | bytes 196616 | tf_op jit(solution)/shard_map/ppermute | solution.py:408
  17.5 0.5 %collective-permute-start.4 = (bf16[4,1,64,128]{3,2,0,1:T(8,128)(2,1)S(1)}, bf16[4,1,64,128]{3,2,0,1:T(8,128)(2,1)S(1)}, u32[]{:S(2)}, u32[]{:S(2)}) collective-permute-start(bf16[4,1,64,128]{3,2,0,1:T(8,128)(2,1)S(1)} %get-tuple-element.110), channel_id=1, source_target_pairs={{0,4},{1,5},{2,6},{3,7},{4,0},{5,1},{6,2},{7,3},{8,12},{9,13},{10,... | collective-permute-start | bytes 196616 | tf_op jit(solution)/shard_map/ppermute | solution.py:408
  18.0 1.6 %collective-permute-start.5 = (bf16[4,1,64,128]{3,2,0,1:T(8,128)(2,1)S(1)}, bf16[4,1,64,128]{3,2,0,1:T(8,128)(2,1)S(1)}, u32[]{:S(2)}, u32[]{:S(2)}) collective-permute-start(bf16[4,1,64,128]{3,2,0,1:T(8,128)(2,1)S(1)} %get-tuple-element.110), channel_id=1, source_target_pairs={{0,2},{1,3},{2,0},{3,1},{4,6},{5,7},{6,4},{7,5},{8,10},{9,11},{10,... | collective-permute-start | bytes 196616 | tf_op jit(solution)/shard_map/ppermute | solution.py:408
  19.7 0.3 project.2
  20.0 2.1 %collective-permute-done.7.refs_2_ = bf16[384,128]{1,0:T(8,128)(2,1)S(1)} collective-permute-done((bf16[384,128]{1,0:T(8,128)(2,1)}, bf16[384,128]{1,0:T(8,128)(2,1)S(1)}, u32[]{:S(2)}, u32[]{:S(2)}) %collective-permute-start.7) | collective-permute-done | bytes 98336 | tf_op jit(solution)/shard_map/ppermute | solution.py:408
  22.1 0.7 %project.3 = (bf16[8,192,128]{2,1,0:T(8,128)(2,1)S(1)}, bf16[8,192,128]{2,1,0:T(8,128)(2,1)S(1)}, bf16[8,192,128]{2,1,0:T(8,128)(2,1)S(1)}, f32[8,192,128]{2,1,0:T(8,128)S(1)}) custom-call(bf16[384,128]{1,0:T(8,128)(2,1)S(1)} %copy-done.7, bf16[384,128]{1,0:T(8,128)(2,1)S(1)} %collective-permute-done.6.refs_1_, ...), custom_call_target="tpu_custom_call" | custom-call | flops 201326592 | bytes 2359296 | tf_op jit(solution)/shard_map/project/pallas_call | solution.py:477
  23.0 2.5 %attend.3 = (bf16[32,8,128]{2,1,0:T(8,128)(2,1)S(1)}, bf16[32,8,128]{2,1,0:T(8,128)(2,1)S(1)}, bf16[32,8,128]{2,1,0:T(8,128)(2,1)S(1)}, bf16[32,8,128]{2,1,0:T(8,128)(2,1)S(1)}) custom-call(bf16[8,64,128]{2,1,0:T(8,128)(2,1)S(1)} %get-tuple-element.78.refs_0_, bf16[8,64,128]{2,1,0:T(8,128)(2,1)S(1)} %get-tuple-element.79.refs_1_, ...), custom_call_target="tpu_custom_call" | custom-call | flops 268435456 | bytes 2097152 | tf_op jit(solution)/shard_map/attend/pallas_call | solution.py:509
  25.5 3.2 %collective-permute-start.13 = (bf16[32,8,128]{2,1,0:T(8,128)(2,1)S(1)}, bf16[32,8,128]{2,1,0:T(8,128)(2,1)S(1)}, u32[]{:S(2)}, u32[]{:S(2)}) collective-permute-start(bf16[32,8,128]{2,1,0:T(8,128)(2,1)S(1)} %get-tuple-element.106), channel_id=1, source_target_pairs={{0,24},{8,16},{16,8},{24,0},{1,25},{9,17},{17,9},{25,1},{2,26},{10... | collective-permute-start | bytes 196616 | tf_op jit(solution)/shard_map/ppermute | solution.py:408
  28.7 1.0 %collective-permute-start.14 = (bf16[32,8,128]{2,1,0:T(8,128)(2,1)S(1)}, bf16[32,8,128]{2,1,0:T(8,128)(2,1)S(1)}, u32[]{:S(2)}, u32[]{:S(2)}) collective-permute-start(bf16[32,8,128]{2,1,0:T(8,128)(2,1)S(1)} %get-tuple-element.107), channel_id=1, source_target_pairs={{0,16},{8,24},{16,0},{24,8},{1,17},{9,25},{17,1},{25,9},{2,18},{10... | collective-permute-start | bytes 196616 | tf_op jit(solution)/shard_map/ppermute | solution.py:408
  29.7 0.3 collective-permute-start.15
  29.9 2.5 %attend.2 = (bf16[32,8,128]{2,1,0:T(8,128)(2,1)S(1)}, bf16[32,8,128]{2,1,0:T(8,128)(2,1)S(1)}, bf16[32,8,128]{2,1,0:T(8,128)(2,1)S(1)}, bf16[32,8,128]{2,1,0:T(8,128)(2,1)S(1)}) custom-call(bf16[8,64,128]{2,1,0:T(8,128)(2,1)S(1)} %get-tuple-element.78.refs_0_, bf16[8,64,128]{2,1,0:T(8,128)(2,1)S(1)} %get-tuple-element.79.refs_1_, ...), custom_call_target="tpu_custom_call" | custom-call | flops 268435456 | bytes 2097152 | tf_op jit(solution)/shard_map/attend/pallas_call | solution.py:509
  32.4 3.2 %collective-permute-start.10 = (bf16[32,8,128]{2,1,0:T(8,128)(2,1)S(1)}, bf16[32,8,128]{2,1,0:T(8,128)(2,1)S(1)}, u32[]{:S(2)}, u32[]{:S(2)}) collective-permute-start(bf16[32,8,128]{2,1,0:T(8,128)(2,1)S(1)} %get-tuple-element.102), channel_id=1, source_target_pairs={{0,24},{8,16},{16,8},{24,0},{1,25},{9,17},{17,9},{25,1},{2,26},{10... | collective-permute-start | bytes 196616 | tf_op jit(solution)/shard_map/ppermute | solution.py:408
  35.7 0.1 collective-permute-start.11
  35.7 1.2 %collective-permute-start.12 = (bf16[32,8,128]{2,1,0:T(8,128)(2,1)S(1)}, bf16[32,8,128]{2,1,0:T(8,128)(2,1)S(1)}, u32[]{:S(2)}, u32[]{:S(2)}) collective-permute-start(bf16[32,8,128]{2,1,0:T(8,128)(2,1)S(1)} %get-tuple-element.104), channel_id=1, source_target_pairs={{0,8},{8,0},{16,24},{24,16},{1,9},{9,1},{17,25},{25,17},{2,10},{10... | collective-permute-start | bytes 196616 | tf_op jit(solution)/shard_map/ppermute | solution.py:408
  36.9 2.2 %collective-permute-done.10.refs_1_ = bf16[32,8,128]{2,1,0:T(8,128)(2,1)S(1)} collective-permute-done((bf16[32,8,128]{2,1,0:T(8,128)(2,1)S(1)}, bf16[32,8,128]{2,1,0:T(8,128)(2,1)S(1)}, u32[]{:S(2)}, u32[]{:S(2)}) %collective-permute-start.10) | collective-permute-done | bytes 65568 | tf_op jit(solution)/shard_map/ppermute | solution.py:408
  39.1 2.6 %collective-permute-done.11.refs_2_ = bf16[32,8,128]{2,1,0:T(8,128)(2,1)S(1)} collective-permute-done((bf16[32,8,128]{2,1,0:T(8,128)(2,1)S(1)}, bf16[32,8,128]{2,1,0:T(8,128)(2,1)S(1)}, u32[]{:S(2)}, u32[]{:S(2)}) %collective-permute-start.11) | collective-permute-done | bytes 65568 | tf_op jit(solution)/shard_map/ppermute | solution.py:408
  41.7 0.9 %place.1 = bf16[64,32,128]{2,1,0:T(8,128)(2,1)} custom-call(bf16[32,8,128]{2,1,0:T(8,128)(2,1)S(1)} %get-tuple-element.101.refs_0_, bf16[32,8,128]{2,1,0:T(8,128)(2,1)S(1)} %collective-permute-done.10.refs_1_, bf16[32,8,128]{2,1,0:T(8,128)(2,1)S(1)} %collective-permute-done.11.refs_2_, bf16[32,8,128]{2,1,0:T(8,128)(2,1)S(1)} %collective-permute-done.12.refs_3_, ...), custom_call_target="tpu_custom_call" | custom-call | tf_op jit(solution)/shard_map/place/pallas_call | solution.py:529
  (39 shorter events, 0.2 us)
Async XLA Ops:
  0.0 9.1 %copy-start = (bf16[128,384]{1,0:T(8,128)(2,1)S(1)}, bf16[128,384]{1,0:T(8,128)(2,1)}, u32[]{:S(2)}) copy-start(bf16[128,384]{1,0:T(8,128)(2,1)} %refs_1_.1) | copy-start | bytes 294916
  0.0 9.1 %copy-start.2 = (bf16[128,128]{1,0:T(8,128)(2,1)S(1)}, bf16[128,128]{1,0:T(8,128)(2,1)}, u32[]{:S(2)}) copy-start(bf16[128,128]{1,0:T(8,128)(2,1)} %refs_2_.1) | copy-start | bytes 98308
  0.0 9.1 %copy-start.3 = (bf16[128,128]{1,0:T(8,128)(2,1)S(1)}, bf16[128,128]{1,0:T(8,128)(2,1)}, u32[]{:S(2)}) copy-start(bf16[128,128]{1,0:T(8,128)(2,1)} %refs_4_.1) | copy-start | bytes 98308
  3.4 11.4 %collective-permute-start = (bf16[192,128]{1,0:T(8,128)(2,1)}, bf16[192,128]{1,0:T(8,128)(2,1)S(1)}, u32[]{:S(2)}, u32[]{:S(2)}) collective-permute-start(bf16[192,128]{1,0:T(8,128)(2,1)} %get-tuple-element.69), channel_id=1, source_target_pairs={{0,24},{8,16},{16,8},{24,0},{1,25},{9,17},{17,9},{25,1},{2,26},{10... | collective-permute-start | bytes 147464 | tf_op jit(solution)/shard_map/ppermute | solution.py:408
  8.5 6.3 %collective-permute-start.1 = (bf16[192,128]{1,0:T(8,128)(2,1)}, bf16[192,128]{1,0:T(8,128)(2,1)S(1)}, u32[]{:S(2)}, u32[]{:S(2)}) collective-permute-start(bf16[192,128]{1,0:T(8,128)(2,1)} %get-tuple-element.70), channel_id=1, source_target_pairs={{0,16},{8,24},{16,0},{24,8},{1,17},{9,25},{17,1},{25,9},{2,18},{10... | collective-permute-start | bytes 147464 | tf_op jit(solution)/shard_map/ppermute | solution.py:408
  8.5 5.5 %collective-permute-start.2 = (bf16[192,128]{1,0:T(8,128)(2,1)}, bf16[192,128]{1,0:T(8,128)(2,1)S(1)}, u32[]{:S(2)}, u32[]{:S(2)}) collective-permute-start(bf16[192,128]{1,0:T(8,128)(2,1)} %get-tuple-element.71), channel_id=1, source_target_pairs={{0,8},{8,0},{16,24},{24,16},{1,9},{9,1},{17,25},{25,17},{2,10},{10... | collective-permute-start | bytes 147464 | tf_op jit(solution)/shard_map/ppermute | solution.py:408
  9.1 0.7 %copy-start.4 = (s32[256]{0:T(256)S(1)}, s32[256]{0:T(256)}, u32[]{:S(2)}) copy-start(s32[256]{0:T(256)} %param.11) | copy-start | bytes 3076
  9.1 0.7 %copy-start.5 = (f32[128]{0:T(128)S(1)}, f32[128]{0:T(128)}, u32[]{:S(2)}) copy-start(f32[128]{0:T(128)} %param.17) | copy-start | bytes 1540
  9.8 4.2 %copy-start.1 = (bf16[192,128]{1,0:T(8,128)(2,1)S(1)}, bf16[192,128]{1,0:T(8,128)(2,1)}, u32[]{:S(2)}) copy-start(bf16[192,128]{1,0:T(8,128)(2,1)} %get-tuple-element.68.refs_0_) | copy-start | bytes 147460
  9.8 4.2 %copy-start.8 = (bf16[384,128]{1,0:T(8,128)(2,1)S(1)}, bf16[384,128]{1,0:T(8,128)(2,1)}, u32[]{:S(2)}) copy-start(bf16[384,128]{1,0:T(8,128)(2,1)} %get-tuple-element.85) | copy-start | bytes 294916
  10.2 7.8 %collective-permute-start.6 = (bf16[384,128]{1,0:T(8,128)(2,1)}, bf16[384,128]{1,0:T(8,128)(2,1)S(1)}, u32[]{:S(2)}, u32[]{:S(2)}) collective-permute-start(bf16[384,128]{1,0:T(8,128)(2,1)} %get-tuple-element.83), channel_id=1, source_target_pairs={{0,24},{8,16},{16,8},{24,0},{1,25},{9,17},{17,9},{25,1},{2,26},{10... | collective-permute-start | bytes 294920 | tf_op jit(solution)/shard_map/ppermute | solution.py:408
  14.0 8.1 %collective-permute-start.7 = (bf16[384,128]{1,0:T(8,128)(2,1)}, bf16[384,128]{1,0:T(8,128)(2,1)S(1)}, u32[]{:S(2)}, u32[]{:S(2)}) collective-permute-start(bf16[384,128]{1,0:T(8,128)(2,1)} %get-tuple-element.84), channel_id=1, source_target_pairs={{0,16},{8,24},{16,0},{24,8},{1,17},{9,25},{17,1},{25,9},{2,18},{10... | collective-permute-start | bytes 294920 | tf_op jit(solution)/shard_map/ppermute | solution.py:408
  14.1 8.1 %collective-permute-start.8 = (bf16[384,128]{1,0:T(8,128)(2,1)S(1)}, bf16[384,128]{1,0:T(8,128)(2,1)S(1)}, u32[]{:S(2)}, u32[]{:S(2)}) collective-permute-start(bf16[384,128]{1,0:T(8,128)(2,1)S(1)} %copy-done.8), channel_id=1, source_target_pairs={{0,8},{8,0},{16,24},{24,16},{1,9},{9,1},{17,25},{25,17},{2,10},{10... | collective-permute-start | bytes 294920 | tf_op jit(solution)/shard_map/ppermute | solution.py:408
  14.8 7.3 %copy-start.7 = (bf16[384,128]{1,0:T(8,128)(2,1)S(1)}, bf16[384,128]{1,0:T(8,128)(2,1)}, u32[]{:S(2)}) copy-start(bf16[384,128]{1,0:T(8,128)(2,1)} %get-tuple-element.82.refs_0_) | copy-start | bytes 294916
  14.8 8.0 %collective-permute-start.3 = (bf16[4,1,64,128]{3,2,0,1:T(8,128)(2,1)S(1)}, bf16[4,1,64,128]{3,2,0,1:T(8,128)(2,1)S(1)}, u32[]{:S(2)}, u32[]{:S(2)}) collective-permute-start(bf16[4,1,64,128]{3,2,0,1:T(8,128)(2,1)S(1)} %get-tuple-element.110), channel_id=1, source_target_pairs={{0,6},{1,7},{2,4},{3,5},{4,2},{5,3},{6,0},{7,1},{8,14},{9,15},{10,... | collective-permute-start | bytes 196616 | tf_op jit(solution)/shard_map/ppermute | solution.py:408
  17.5 5.4 %collective-permute-start.4 = (bf16[4,1,64,128]{3,2,0,1:T(8,128)(2,1)S(1)}, bf16[4,1,64,128]{3,2,0,1:T(8,128)(2,1)S(1)}, u32[]{:S(2)}, u32[]{:S(2)}) collective-permute-start(bf16[4,1,64,128]{3,2,0,1:T(8,128)(2,1)S(1)} %get-tuple-element.110), channel_id=1, source_target_pairs={{0,4},{1,5},{2,6},{3,7},{4,0},{5,1},{6,2},{7,3},{8,12},{9,13},{10,... | collective-permute-start | bytes 196616 | tf_op jit(solution)/shard_map/ppermute | solution.py:408
  18.0 4.8 %collective-permute-start.5 = (bf16[4,1,64,128]{3,2,0,1:T(8,128)(2,1)S(1)}, bf16[4,1,64,128]{3,2,0,1:T(8,128)(2,1)S(1)}, u32[]{:S(2)}, u32[]{:S(2)}) collective-permute-start(bf16[4,1,64,128]{3,2,0,1:T(8,128)(2,1)S(1)} %get-tuple-element.110), channel_id=1, source_target_pairs={{0,2},{1,3},{2,0},{3,1},{4,6},{5,7},{6,4},{7,5},{8,10},{9,11},{10,... | collective-permute-start | bytes 196616 | tf_op jit(solution)/shard_map/ppermute | solution.py:408
  22.9 7.0 %collective-permute-start.9 = (bf16[4,4,1,64,128]{4,3,2,1,0:T(8,128)(2,1)S(1)}, bf16[4,4,1,64,128]{4,3,2,1,0:T(8,128)(2,1)S(1)}, u32[]{:S(2)}, u32[]{:S(2)}) collective-permute-start(bf16[4,4,1,64,128]{4,3,2,1,0:T(8,128)(2,1)S(1)} %pad_maximum_fusion.refs_8_), channel_id=1, source_target_pairs={{0,1},{1,0},{2,3},{3,2},{4,5},{5,4},{6,7},{7,6},{8,9},{9,8},{10,11... | collective-permute-start | bytes 786440 | tf_op jit(solution)/shard_map/ppermute | solution.py:408
  25.5 10.3 %collective-permute-start.13 = (bf16[32,8,128]{2,1,0:T(8,128)(2,1)S(1)}, bf16[32,8,128]{2,1,0:T(8,128)(2,1)S(1)}, u32[]{:S(2)}, u32[]{:S(2)}) collective-permute-start(bf16[32,8,128]{2,1,0:T(8,128)(2,1)S(1)} %get-tuple-element.106), channel_id=1, source_target_pairs={{0,24},{8,16},{16,8},{24,0},{1,25},{9,17},{17,9},{25,1},{2,26},{10... | collective-permute-start | bytes 196616 | tf_op jit(solution)/shard_map/ppermute | solution.py:408
  28.7 8.2 %collective-permute-start.14 = (bf16[32,8,128]{2,1,0:T(8,128)(2,1)S(1)}, bf16[32,8,128]{2,1,0:T(8,128)(2,1)S(1)}, u32[]{:S(2)}, u32[]{:S(2)}) collective-permute-start(bf16[32,8,128]{2,1,0:T(8,128)(2,1)S(1)} %get-tuple-element.107), channel_id=1, source_target_pairs={{0,16},{8,24},{16,0},{24,8},{1,17},{9,25},{17,1},{25,9},{2,18},{10... | collective-permute-start | bytes 196616 | tf_op jit(solution)/shard_map/ppermute | solution.py:408
  29.7 7.2 %collective-permute-start.15 = (bf16[32,8,128]{2,1,0:T(8,128)(2,1)S(1)}, bf16[32,8,128]{2,1,0:T(8,128)(2,1)S(1)}, u32[]{:S(2)}, u32[]{:S(2)}) collective-permute-start(bf16[32,8,128]{2,1,0:T(8,128)(2,1)S(1)} %get-tuple-element.108), channel_id=1, source_target_pairs={{0,8},{8,0},{16,24},{24,16},{1,9},{9,1},{17,25},{25,17},{2,10},{10... | collective-permute-start | bytes 196616 | tf_op jit(solution)/shard_map/ppermute | solution.py:408
  32.4 6.6 %collective-permute-start.10 = (bf16[32,8,128]{2,1,0:T(8,128)(2,1)S(1)}, bf16[32,8,128]{2,1,0:T(8,128)(2,1)S(1)}, u32[]{:S(2)}, u32[]{:S(2)}) collective-permute-start(bf16[32,8,128]{2,1,0:T(8,128)(2,1)S(1)} %get-tuple-element.102), channel_id=1, source_target_pairs={{0,24},{8,16},{16,8},{24,0},{1,25},{9,17},{17,9},{25,1},{2,26},{10... | collective-permute-start | bytes 196616 | tf_op jit(solution)/shard_map/ppermute | solution.py:408
  35.7 6.0 %collective-permute-start.11 = (bf16[32,8,128]{2,1,0:T(8,128)(2,1)S(1)}, bf16[32,8,128]{2,1,0:T(8,128)(2,1)S(1)}, u32[]{:S(2)}, u32[]{:S(2)}) collective-permute-start(bf16[32,8,128]{2,1,0:T(8,128)(2,1)S(1)} %get-tuple-element.103), channel_id=1, source_target_pairs={{0,16},{8,24},{16,0},{24,8},{1,17},{9,25},{17,1},{25,9},{2,18},{10... | collective-permute-start | bytes 196616 | tf_op jit(solution)/shard_map/ppermute | solution.py:408
  35.7 5.9 %collective-permute-start.12 = (bf16[32,8,128]{2,1,0:T(8,128)(2,1)S(1)}, bf16[32,8,128]{2,1,0:T(8,128)(2,1)S(1)}, u32[]{:S(2)}, u32[]{:S(2)}) collective-permute-start(bf16[32,8,128]{2,1,0:T(8,128)(2,1)S(1)} %get-tuple-element.104), channel_id=1, source_target_pairs={{0,8},{8,0},{16,24},{24,16},{1,9},{9,1},{17,25},{25,17},{2,10},{10... | collective-permute-start | bytes 196616 | tf_op jit(solution)/shard_map/ppermute | solution.py:408
  (1 other events, 0.7 us)

commit v6 on v5

--- a/solution.py
+++ b/solution.py
@@ -167,16 +167,14 @@
     weight, gate_bias, q_ref, k_ref, v_ref, gate_ref, wide, tokens = refs[parts:]
     width, count, inner = q_ref.shape
     batch = tokens.shape[1] // count
-    me = lax.axis_index("row")
     for s in range(parts):
         wide[s] = parcels[s][0 : size * width, :].astype(F32)
 
     def lay(j):
         for k in range(batch):
             for s in range(parts):
-                at = pl.multiple_of(k * count + (me ^ hop(s, parts)) * size, size)
                 line = wide[s, pl.ds(batch * j + k, size, stride=width), :]
-                tokens[j, pl.ds(at, size), :] = line.astype(BF)
+                tokens[j, pl.ds(k * count + s * size, size), :] = line.astype(BF)
         return ()
 
     def multiply(j):
@@ -272,14 +270,16 @@
         )
         ordered = dot(block, order_ref[...])
         for s in range(batch):
-            level = me ^ hop(b * batch + s, parts)
+            place = b * batch + s
+            level = me ^ hop(place, parts)
             for low, high, base in ((0, first_rows, 0), (first_rows, rows, early)):
-                at = pl.multiple_of(base + level * (high - low), first_rows)
-                at = pl.ds(at, high - low)
+                size = high - low
+                key = key_ref[pl.ds(pl.multiple_of(base + level * size, first_rows), size), :]
+                at = pl.ds(pl.multiple_of(base + place * size, first_rows), size)
                 some = slice(s * rows + low, s * rows + high)
                 for h in range(heads):
                     across = slice(h * 128, (h + 1) * 128)
-                    bias[g, at, across] = ordered[some, across] + key_ref[at, :]
+                    bias[g, at, across] = ordered[some, across] + key
         return carry
 
     blocks = groups * (parts // batch)
@@ -291,9 +291,9 @@
     def query_rows(j, g, n):
         found = []
         for t in range(group):
-            level = over(col, 2) ^ hop(g * group + t, parts)
-            base = level * (rows - first_rows)
-            spots = (0, level * first_rows), (1, base + first_rows), (1, base + odd * 2 * first_rows)
+            place = hop(me ^ over(col, 2) ^ hop(g * group + t, parts), parts)
+            base = place * (rows - first_rows)
+            spots = (0, place * first_rows), (1, base + first_rows), (1, base + odd * 2 * first_rows)
             upper, lower, last = (
                 halves[k][n][j, pl.ds(pl.multiple_of(at, first_rows), first_rows), :]
                 for k, at in spots

time: 42.7 us -> 42.6 us (level)
  no operation moved by 1% of the time
where the time goes in v6:
time: 42.6 us; the launch traced here: 42.5 us
  starting transfers between devices  24.1 us (57%)
  Pallas kernels  10.5 us (25%)
  waiting for transfers between devices  6.97 us (16%)
  local copies, waits for them, and re-layouts  0.69 us (2%)
    ppermute x16, starting transfers between devices, swap(): return lax.ppermute(x, axis, [(i, i ^ offset) for i in range(size)])  24.1 us
    ppermute x16, waiting for transfers between devices, swap(): return lax.ppermute(x, axis, [(i, i ^ offset) for i in range(size)])  6.97 us
    pallas_call x2, Pallas kernels, attend(): pl.pallas_call(functools.partial(attend_kernel, parts, side), out_shape=[...  5 us
    pallas_call x1, Pallas kernels, per_device(): pl.pallas_call(prep_kernel, out_shape=[jax.ShapeDtypeStruct(early, BF)] *...  3.35 us
    pallas_call x2, Pallas kernels, project(): pl.pallas_call(functools.partial(project_kernel, parts, (inner // heads)...  0.91 us
    pallas_call x1, Pallas kernels, per_device(): pl.pallas_call(functools.partial(place_kernel, parts), out_shape=jax.Shap...  0.87 us
  transfers between devices with their start and end apart: 16, of which 3 were waited for; matrix products, arithmetic and copies ran while one was open for 0% of the time, Pallas kernels for 15%

profile of v6, /device:TPU:0, one launch (start us, length us, event | category | flops | bytes accessed | tf_op | source)
XLA Modules:
  0.0 42.5 jit_solution(16044719537482619678)
XLA Ops:
  0.0 3.3 %prep.1 = (bf16[192,128]{1,0:T(8,128)(2,1)}, bf16[192,128]{1,0:T(8,128)(2,1)}, bf16[192,128]{1,0:T(8,128)(2,1)}, bf16[192,128]{1,0:T(8,128)(2,1)}, bf16[384,128]...) custom-call(bf16[64,32,128]{2,1,0:T(8,128)(2,1)} %pair_ref.1, ...), custom_call_target="tpu_custom_call" | custom-call | tf_op jit(solution)/shard_map/prep/pallas_call | solution.py:414
  3.4 5.1 %collective-permute-start = (bf16[192,128]{1,0:T(8,128)(2,1)}, bf16[192,128]{1,0:T(8,128)(2,1)S(1)}, u32[]{:S(2)}, u32[]{:S(2)}) collective-permute-start(bf16[192,128]{1,0:T(8,128)(2,1)} %get-tuple-element.69), channel_id=1, source_target_pairs={{0,24},{8,16},{16,8},{24,0},{1,25},{9,17},{17,9},{25,1},{2,26},{10... | collective-permute-start | bytes 147464 | tf_op jit(solution)/shard_map/ppermute | solution.py:408
  8.5 0.6 %collective-permute-start.2 = (bf16[192,128]{1,0:T(8,128)(2,1)}, bf16[192,128]{1,0:T(8,128)(2,1)S(1)}, u32[]{:S(2)}, u32[]{:S(2)}) collective-permute-start(bf16[192,128]{1,0:T(8,128)(2,1)} %get-tuple-element.71), channel_id=1, source_target_pairs={{0,8},{8,0},{16,24},{24,16},{1,9},{9,1},{17,25},{25,17},{2,10},{10... | collective-permute-start | bytes 147464 | tf_op jit(solution)/shard_map/ppermute | solution.py:408
  9.2 0.6 %copy-done.4 = s32[256]{0:T(256)S(1)} copy-done((s32[256]{0:T(256)S(1)}, s32[256]{0:T(256)}, u32[]{:S(2)}) %copy-start.4) | copy-done | bytes 1048
  9.8 0.4 constants.1
  10.2 3.8 %collective-permute-start.6 = (bf16[384,128]{1,0:T(8,128)(2,1)}, bf16[384,128]{1,0:T(8,128)(2,1)S(1)}, u32[]{:S(2)}, u32[]{:S(2)}) collective-permute-start(bf16[384,128]{1,0:T(8,128)(2,1)} %get-tuple-element.83), channel_id=1, source_target_pairs={{0,24},{8,16},{16,8},{24,0},{1,25},{9,17},{17,9},{25,1},{2,26},{10... | collective-permute-start | bytes 294920 | tf_op jit(solution)/shard_map/ppermute | solution.py:408
  14.1 0.7 %collective-permute-start.8 = (bf16[384,128]{1,0:T(8,128)(2,1)S(1)}, bf16[384,128]{1,0:T(8,128)(2,1)S(1)}, u32[]{:S(2)}, u32[]{:S(2)}) collective-permute-start(bf16[384,128]{1,0:T(8,128)(2,1)S(1)} %copy-done.8), channel_id=1, source_target_pairs={{0,8},{8,0},{16,24},{24,16},{1,9},{9,1},{17,25},{25,17},{2,10},{10... | collective-permute-start | bytes 294920 | tf_op jit(solution)/shard_map/ppermute | solution.py:408
  14.8 2.7 %collective-permute-start.3 = (bf16[4,1,64,128]{3,2,0,1:T(8,128)(2,1)S(1)}, bf16[4,1,64,128]{3,2,0,1:T(8,128)(2,1)S(1)}, u32[]{:S(2)}, u32[]{:S(2)}) collective-permute-start(bf16[4,1,64,128]{3,2,0,1:T(8,128)(2,1)S(1)} %get-tuple-element.110), channel_id=1, source_target_pairs={{0,6},{1,7},{2,4},{3,5},{4,2},{5,3},{6,0},{7,1},{8,14},{9,15},{10,... | collective-permute-start | bytes 196616 | tf_op jit(solution)/shard_map/ppermute | solution.py:408
  17.5 0.5 %collective-permute-start.4 = (bf16[4,1,64,128]{3,2,0,1:T(8,128)(2,1)S(1)}, bf16[4,1,64,128]{3,2,0,1:T(8,128)(2,1)S(1)}, u32[]{:S(2)}, u32[]{:S(2)}) collective-permute-start(bf16[4,1,64,128]{3,2,0,1:T(8,128)(2,1)S(1)} %get-tuple-element.110), channel_id=1, source_target_pairs={{0,4},{1,5},{2,6},{3,7},{4,0},{5,1},{6,2},{7,3},{8,12},{9,13},{10,... | collective-permute-start | bytes 196616 | tf_op jit(solution)/shard_map/ppermute | solution.py:408
  18.0 1.6 %collective-permute-start.5 = (bf16[4,1,64,128]{3,2,0,1:T(8,128)(2,1)S(1)}, bf16[4,1,64,128]{3,2,0,1:T(8,128)(2,1)S(1)}, u32[]{:S(2)}, u32[]{:S(2)}) collective-permute-start(bf16[4,1,64,128]{3,2,0,1:T(8,128)(2,1)S(1)} %get-tuple-element.110), channel_id=1, source_target_pairs={{0,2},{1,3},{2,0},{3,1},{4,6},{5,7},{6,4},{7,5},{8,10},{9,11},{10,... | collective-permute-start | bytes 196616 | tf_op jit(solution)/shard_map/ppermute | solution.py:408
  19.7 0.3 project.2
  20.0 2.1 %collective-permute-done.7.refs_2_ = bf16[384,128]{1,0:T(8,128)(2,1)S(1)} collective-permute-done((bf16[384,128]{1,0:T(8,128)(2,1)}, bf16[384,128]{1,0:T(8,128)(2,1)S(1)}, u32[]{:S(2)}, u32[]{:S(2)}) %collective-permute-start.7) | collective-permute-done | bytes 98336 | tf_op jit(solution)/shard_map/ppermute | solution.py:408
  22.1 0.6 %project.3 = (bf16[8,192,128]{2,1,0:T(8,128)(2,1)S(1)}, bf16[8,192,128]{2,1,0:T(8,128)(2,1)S(1)}, bf16[8,192,128]{2,1,0:T(8,128)(2,1)S(1)}, f32[8,192,128]{2,1,0:T(8,128)S(1)}) custom-call(bf16[384,128]{1,0:T(8,128)(2,1)S(1)} %copy-done.7, bf16[384,128]{1,0:T(8,128)(2,1)S(1)} %collective-permute-done.6.refs_1_, ...), custom_call_target="tpu_custom_call" | custom-call | flops 201326592 | bytes 2359296 | tf_op jit(solution)/shard_map/project/pallas_call | solution.py:477
  22.9 2.5 %attend.3 = (bf16[32,8,128]{2,1,0:T(8,128)(2,1)S(1)}, bf16[32,8,128]{2,1,0:T(8,128)(2,1)S(1)}, bf16[32,8,128]{2,1,0:T(8,128)(2,1)S(1)}, bf16[32,8,128]{2,1,0:T(8,128)(2,1)S(1)}) custom-call(bf16[8,64,128]{2,1,0:T(8,128)(2,1)S(1)} %get-tuple-element.78.refs_0_, bf16[8,64,128]{2,1,0:T(8,128)(2,1)S(1)} %get-tuple-element.79.refs_1_, ...), custom_call_target="tpu_custom_call" | custom-call | flops 268435456 | bytes 2097152 | tf_op jit(solution)/shard_map/attend/pallas_call | solution.py:509
  25.4 3.3 %collective-permute-start.13 = (bf16[32,8,128]{2,1,0:T(8,128)(2,1)S(1)}, bf16[32,8,128]{2,1,0:T(8,128)(2,1)S(1)}, u32[]{:S(2)}, u32[]{:S(2)}) collective-permute-start(bf16[32,8,128]{2,1,0:T(8,128)(2,1)S(1)} %get-tuple-element.106), channel_id=1, source_target_pairs={{0,24},{8,16},{16,8},{24,0},{1,25},{9,17},{17,9},{25,1},{2,26},{10... | collective-permute-start | bytes 196616 | tf_op jit(solution)/shard_map/ppermute | solution.py:408
  28.7 1.0 %collective-permute-start.14 = (bf16[32,8,128]{2,1,0:T(8,128)(2,1)S(1)}, bf16[32,8,128]{2,1,0:T(8,128)(2,1)S(1)}, u32[]{:S(2)}, u32[]{:S(2)}) collective-permute-start(bf16[32,8,128]{2,1,0:T(8,128)(2,1)S(1)} %get-tuple-element.107), channel_id=1, source_target_pairs={{0,16},{8,24},{16,0},{24,8},{1,17},{9,25},{17,1},{25,9},{2,18},{10... | collective-permute-start | bytes 196616 | tf_op jit(solution)/shard_map/ppermute | solution.py:408
  29.7 0.2 collective-permute-start.15
  29.9 2.5 %attend.2 = (bf16[32,8,128]{2,1,0:T(8,128)(2,1)S(1)}, bf16[32,8,128]{2,1,0:T(8,128)(2,1)S(1)}, bf16[32,8,128]{2,1,0:T(8,128)(2,1)S(1)}, bf16[32,8,128]{2,1,0:T(8,128)(2,1)S(1)}) custom-call(bf16[8,64,128]{2,1,0:T(8,128)(2,1)S(1)} %get-tuple-element.78.refs_0_, bf16[8,64,128]{2,1,0:T(8,128)(2,1)S(1)} %get-tuple-element.79.refs_1_, ...), custom_call_target="tpu_custom_call" | custom-call | flops 268435456 | bytes 2097152 | tf_op jit(solution)/shard_map/attend/pallas_call | solution.py:509
  32.4 3.3 %collective-permute-start.10 = (bf16[32,8,128]{2,1,0:T(8,128)(2,1)S(1)}, bf16[32,8,128]{2,1,0:T(8,128)(2,1)S(1)}, u32[]{:S(2)}, u32[]{:S(2)}) collective-permute-start(bf16[32,8,128]{2,1,0:T(8,128)(2,1)S(1)} %get-tuple-element.102), channel_id=1, source_target_pairs={{0,24},{8,16},{16,8},{24,0},{1,25},{9,17},{17,9},{25,1},{2,26},{10... | collective-permute-start | bytes 196616 | tf_op jit(solution)/shard_map/ppermute | solution.py:408
  35.7 0.1 collective-permute-start.11
  35.8 1.1 %collective-permute-start.12 = (bf16[32,8,128]{2,1,0:T(8,128)(2,1)S(1)}, bf16[32,8,128]{2,1,0:T(8,128)(2,1)S(1)}, u32[]{:S(2)}, u32[]{:S(2)}) collective-permute-start(bf16[32,8,128]{2,1,0:T(8,128)(2,1)S(1)} %get-tuple-element.104), channel_id=1, source_target_pairs={{0,8},{8,0},{16,24},{24,16},{1,9},{9,1},{17,25},{25,17},{2,10},{10... | collective-permute-start | bytes 196616 | tf_op jit(solution)/shard_map/ppermute | solution.py:408
  36.8 2.2 %collective-permute-done.10.refs_1_ = bf16[32,8,128]{2,1,0:T(8,128)(2,1)S(1)} collective-permute-done((bf16[32,8,128]{2,1,0:T(8,128)(2,1)S(1)}, bf16[32,8,128]{2,1,0:T(8,128)(2,1)S(1)}, u32[]{:S(2)}, u32[]{:S(2)}) %collective-permute-start.10) | collective-permute-done | bytes 65568 | tf_op jit(solution)/shard_map/ppermute | solution.py:408
  39.0 2.6 %collective-permute-done.11.refs_2_ = bf16[32,8,128]{2,1,0:T(8,128)(2,1)S(1)} collective-permute-done((bf16[32,8,128]{2,1,0:T(8,128)(2,1)S(1)}, bf16[32,8,128]{2,1,0:T(8,128)(2,1)S(1)}, u32[]{:S(2)}, u32[]{:S(2)}) %collective-permute-start.11) | collective-permute-done | bytes 65568 | tf_op jit(solution)/shard_map/ppermute | solution.py:408
  41.6 0.9 %place.1 = bf16[64,32,128]{2,1,0:T(8,128)(2,1)} custom-call(bf16[32,8,128]{2,1,0:T(8,128)(2,1)S(1)} %get-tuple-element.101.refs_0_, bf16[32,8,128]{2,1,0:T(8,128)(2,1)S(1)} %collective-permute-done.10.refs_1_, bf16[32,8,128]{2,1,0:T(8,128)(2,1)S(1)} %collective-permute-done.11.refs_2_, bf16[32,8,128]{2,1,0:T(8,128)(2,1)S(1)} %collective-permute-done.12.refs_3_, ...), custom_call_target="tpu_custom_call" | custom-call | tf_op jit(solution)/shard_map/place/pallas_call | solution.py:529
  (39 shorter events, 0.2 us)
Async XLA Ops:
  0.0 9.1 %copy-start = (bf16[128,384]{1,0:T(8,128)(2,1)S(1)}, bf16[128,384]{1,0:T(8,128)(2,1)}, u32[]{:S(2)}) copy-start(bf16[128,384]{1,0:T(8,128)(2,1)} %refs_1_.1) | copy-start | bytes 294916
  0.0 9.1 %copy-start.2 = (bf16[128,128]{1,0:T(8,128)(2,1)S(1)}, bf16[128,128]{1,0:T(8,128)(2,1)}, u32[]{:S(2)}) copy-start(bf16[128,128]{1,0:T(8,128)(2,1)} %refs_2_.1) | copy-start | bytes 98308
  0.0 9.1 %copy-start.3 = (bf16[128,128]{1,0:T(8,128)(2,1)S(1)}, bf16[128,128]{1,0:T(8,128)(2,1)}, u32[]{:S(2)}) copy-start(bf16[128,128]{1,0:T(8,128)(2,1)} %refs_4_.1) | copy-start | bytes 98308
  3.4 11.4 %collective-permute-start = (bf16[192,128]{1,0:T(8,128)(2,1)}, bf16[192,128]{1,0:T(8,128)(2,1)S(1)}, u32[]{:S(2)}, u32[]{:S(2)}) collective-permute-start(bf16[192,128]{1,0:T(8,128)(2,1)} %get-tuple-element.69), channel_id=1, source_target_pairs={{0,24},{8,16},{16,8},{24,0},{1,25},{9,17},{17,9},{25,1},{2,26},{10... | collective-permute-start | bytes 147464 | tf_op jit(solution)/shard_map/ppermute | solution.py:408
  8.5 6.3 %collective-permute-start.1 = (bf16[192,128]{1,0:T(8,128)(2,1)}, bf16[192,128]{1,0:T(8,128)(2,1)S(1)}, u32[]{:S(2)}, u32[]{:S(2)}) collective-permute-start(bf16[192,128]{1,0:T(8,128)(2,1)} %get-tuple-element.70), channel_id=1, source_target_pairs={{0,16},{8,24},{16,0},{24,8},{1,17},{9,25},{17,1},{25,9},{2,18},{10... | collective-permute-start | bytes 147464 | tf_op jit(solution)/shard_map/ppermute | solution.py:408
  8.5 5.5 %collective-permute-start.2 = (bf16[192,128]{1,0:T(8,128)(2,1)}, bf16[192,128]{1,0:T(8,128)(2,1)S(1)}, u32[]{:S(2)}, u32[]{:S(2)}) collective-permute-start(bf16[192,128]{1,0:T(8,128)(2,1)} %get-tuple-element.71), channel_id=1, source_target_pairs={{0,8},{8,0},{16,24},{24,16},{1,9},{9,1},{17,25},{25,17},{2,10},{10... | collective-permute-start | bytes 147464 | tf_op jit(solution)/shard_map/ppermute | solution.py:408
  9.1 0.7 %copy-start.4 = (s32[256]{0:T(256)S(1)}, s32[256]{0:T(256)}, u32[]{:S(2)}) copy-start(s32[256]{0:T(256)} %param.11) | copy-start | bytes 3076
  9.1 0.7 %copy-start.5 = (f32[128]{0:T(128)S(1)}, f32[128]{0:T(128)}, u32[]{:S(2)}) copy-start(f32[128]{0:T(128)} %param.17) | copy-start | bytes 1540
  9.8 4.2 %copy-start.1 = (bf16[192,128]{1,0:T(8,128)(2,1)S(1)}, bf16[192,128]{1,0:T(8,128)(2,1)}, u32[]{:S(2)}) copy-start(bf16[192,128]{1,0:T(8,128)(2,1)} %get-tuple-element.68.refs_0_) | copy-start | bytes 147460
  9.8 4.2 %copy-start.8 = (bf16[384,128]{1,0:T(8,128)(2,1)S(1)}, bf16[384,128]{1,0:T(8,128)(2,1)}, u32[]{:S(2)}) copy-start(bf16[384,128]{1,0:T(8,128)(2,1)} %get-tuple-element.85) | copy-start | bytes 294916
  10.2 7.8 %collective-permute-start.6 = (bf16[384,128]{1,0:T(8,128)(2,1)}, bf16[384,128]{1,0:T(8,128)(2,1)S(1)}, u32[]{:S(2)}, u32[]{:S(2)}) collective-permute-start(bf16[384,128]{1,0:T(8,128)(2,1)} %get-tuple-element.83), channel_id=1, source_target_pairs={{0,24},{8,16},{16,8},{24,0},{1,25},{9,17},{17,9},{25,1},{2,26},{10... | collective-permute-start | bytes 294920 | tf_op jit(solution)/shard_map/ppermute | solution.py:408
  14.0 8.1 %collective-permute-start.7 = (bf16[384,128]{1,0:T(8,128)(2,1)}, bf16[384,128]{1,0:T(8,128)(2,1)S(1)}, u32[]{:S(2)}, u32[]{:S(2)}) collective-permute-start(bf16[384,128]{1,0:T(8,128)(2,1)} %get-tuple-element.84), channel_id=1, source_target_pairs={{0,16},{8,24},{16,0},{24,8},{1,17},{9,25},{17,1},{25,9},{2,18},{10... | collective-permute-start | bytes 294920 | tf_op jit(solution)/shard_map/ppermute | solution.py:408
  14.1 8.1 %collective-permute-start.8 = (bf16[384,128]{1,0:T(8,128)(2,1)S(1)}, bf16[384,128]{1,0:T(8,128)(2,1)S(1)}, u32[]{:S(2)}, u32[]{:S(2)}) collective-permute-start(bf16[384,128]{1,0:T(8,128)(2,1)S(1)} %copy-done.8), channel_id=1, source_target_pairs={{0,8},{8,0},{16,24},{24,16},{1,9},{9,1},{17,25},{25,17},{2,10},{10... | collective-permute-start | bytes 294920 | tf_op jit(solution)/shard_map/ppermute | solution.py:408
  14.8 7.3 %copy-start.7 = (bf16[384,128]{1,0:T(8,128)(2,1)S(1)}, bf16[384,128]{1,0:T(8,128)(2,1)}, u32[]{:S(2)}) copy-start(bf16[384,128]{1,0:T(8,128)(2,1)} %get-tuple-element.82.refs_0_) | copy-start | bytes 294916
  14.8 7.9 %collective-permute-start.3 = (bf16[4,1,64,128]{3,2,0,1:T(8,128)(2,1)S(1)}, bf16[4,1,64,128]{3,2,0,1:T(8,128)(2,1)S(1)}, u32[]{:S(2)}, u32[]{:S(2)}) collective-permute-start(bf16[4,1,64,128]{3,2,0,1:T(8,128)(2,1)S(1)} %get-tuple-element.110), channel_id=1, source_target_pairs={{0,6},{1,7},{2,4},{3,5},{4,2},{5,3},{6,0},{7,1},{8,14},{9,15},{10,... | collective-permute-start | bytes 196616 | tf_op jit(solution)/shard_map/ppermute | solution.py:408
  17.5 5.3 %collective-permute-start.4 = (bf16[4,1,64,128]{3,2,0,1:T(8,128)(2,1)S(1)}, bf16[4,1,64,128]{3,2,0,1:T(8,128)(2,1)S(1)}, u32[]{:S(2)}, u32[]{:S(2)}) collective-permute-start(bf16[4,1,64,128]{3,2,0,1:T(8,128)(2,1)S(1)} %get-tuple-element.110), channel_id=1, source_target_pairs={{0,4},{1,5},{2,6},{3,7},{4,0},{5,1},{6,2},{7,3},{8,12},{9,13},{10,... | collective-permute-start | bytes 196616 | tf_op jit(solution)/shard_map/ppermute | solution.py:408
  18.0 4.7 %collective-permute-start.5 = (bf16[4,1,64,128]{3,2,0,1:T(8,128)(2,1)S(1)}, bf16[4,1,64,128]{3,2,0,1:T(8,128)(2,1)S(1)}, u32[]{:S(2)}, u32[]{:S(2)}) collective-permute-start(bf16[4,1,64,128]{3,2,0,1:T(8,128)(2,1)S(1)} %get-tuple-element.110), channel_id=1, source_target_pairs={{0,2},{1,3},{2,0},{3,1},{4,6},{5,7},{6,4},{7,5},{8,10},{9,11},{10,... | collective-permute-start | bytes 196616 | tf_op jit(solution)/shard_map/ppermute | solution.py:408
  22.8 7.0 %collective-permute-start.9 = (bf16[4,4,1,64,128]{4,3,2,1,0:T(8,128)(2,1)S(1)}, bf16[4,4,1,64,128]{4,3,2,1,0:T(8,128)(2,1)S(1)}, u32[]{:S(2)}, u32[]{:S(2)}) collective-permute-start(bf16[4,4,1,64,128]{4,3,2,1,0:T(8,128)(2,1)S(1)} %pad_maximum_fusion.refs_8_), channel_id=1, source_target_pairs={{0,1},{1,0},{2,3},{3,2},{4,5},{5,4},{6,7},{7,6},{8,9},{9,8},{10,11... | collective-permute-start | bytes 786440 | tf_op jit(solution)/shard_map/ppermute | solution.py:408
  25.4 10.4 %collective-permute-start.13 = (bf16[32,8,128]{2,1,0:T(8,128)(2,1)S(1)}, bf16[32,8,128]{2,1,0:T(8,128)(2,1)S(1)}, u32[]{:S(2)}, u32[]{:S(2)}) collective-permute-start(bf16[32,8,128]{2,1,0:T(8,128)(2,1)S(1)} %get-tuple-element.106), channel_id=1, source_target_pairs={{0,24},{8,16},{16,8},{24,0},{1,25},{9,17},{17,9},{25,1},{2,26},{10... | collective-permute-start | bytes 196616 | tf_op jit(solution)/shard_map/ppermute | solution.py:408
  28.7 8.1 %collective-permute-start.14 = (bf16[32,8,128]{2,1,0:T(8,128)(2,1)S(1)}, bf16[32,8,128]{2,1,0:T(8,128)(2,1)S(1)}, u32[]{:S(2)}, u32[]{:S(2)}) collective-permute-start(bf16[32,8,128]{2,1,0:T(8,128)(2,1)S(1)} %get-tuple-element.107), channel_id=1, source_target_pairs={{0,16},{8,24},{16,0},{24,8},{1,17},{9,25},{17,1},{25,9},{2,18},{10... | collective-permute-start | bytes 196616 | tf_op jit(solution)/shard_map/ppermute | solution.py:408
  29.7 7.1 %collective-permute-start.15 = (bf16[32,8,128]{2,1,0:T(8,128)(2,1)S(1)}, bf16[32,8,128]{2,1,0:T(8,128)(2,1)S(1)}, u32[]{:S(2)}, u32[]{:S(2)}) collective-permute-start(bf16[32,8,128]{2,1,0:T(8,128)(2,1)S(1)} %get-tuple-element.108), channel_id=1, source_target_pairs={{0,8},{8,0},{16,24},{24,16},{1,9},{9,1},{17,25},{25,17},{2,10},{10... | collective-permute-start | bytes 196616 | tf_op jit(solution)/shard_map/ppermute | solution.py:408
  32.4 6.6 %collective-permute-start.10 = (bf16[32,8,128]{2,1,0:T(8,128)(2,1)S(1)}, bf16[32,8,128]{2,1,0:T(8,128)(2,1)S(1)}, u32[]{:S(2)}, u32[]{:S(2)}) collective-permute-start(bf16[32,8,128]{2,1,0:T(8,128)(2,1)S(1)} %get-tuple-element.102), channel_id=1, source_target_pairs={{0,24},{8,16},{16,8},{24,0},{1,25},{9,17},{17,9},{25,1},{2,26},{10... | collective-permute-start | bytes 196616 | tf_op jit(solution)/shard_map/ppermute | solution.py:408
  35.7 5.9 %collective-permute-start.11 = (bf16[32,8,128]{2,1,0:T(8,128)(2,1)S(1)}, bf16[32,8,128]{2,1,0:T(8,128)(2,1)S(1)}, u32[]{:S(2)}, u32[]{:S(2)}) collective-permute-start(bf16[32,8,128]{2,1,0:T(8,128)(2,1)S(1)} %get-tuple-element.103), channel_id=1, source_target_pairs={{0,16},{8,24},{16,0},{24,8},{1,17},{9,25},{17,1},{25,9},{2,18},{10... | collective-permute-start | bytes 196616 | tf_op jit(solution)/shard_map/ppermute | solution.py:408
  35.8 5.8 %collective-permute-start.12 = (bf16[32,8,128]{2,1,0:T(8,128)(2,1)S(1)}, bf16[32,8,128]{2,1,0:T(8,128)(2,1)S(1)}, u32[]{:S(2)}, u32[]{:S(2)}) collective-permute-start(bf16[32,8,128]{2,1,0:T(8,128)(2,1)S(1)} %get-tuple-element.104), channel_id=1, source_target_pairs={{0,8},{8,0},{16,24},{24,16},{1,9},{9,1},{17,25},{25,17},{2,10},{10... | collective-permute-start | bytes 196616 | tf_op jit(solution)/shard_map/ppermute | solution.py:408
  (1 other events, 0.7 us)

commit v7 on v6

--- a/solution.py
+++ b/solution.py
@@ -131,8 +131,9 @@
     if rows <= 64:
 
         def first_stage(n):
-            if n * step in (0, half):
-                fetches[n * step // half].wait()
+            if n == 0:
+                for copy in fetches:
+                    copy.wait()
             return centre(n * step)
 
         def second_stage(n, centred, var):
@@ -331,10 +332,10 @@
         scores = scores_of(steps[0][0], g, steps[0][1])
         total_steps = len(steps)
         scores, weights, heard = {}, {}, {}
-        for n in range(-3, total_steps + 2 + 2):
-            if 0 <= n + 3 < total_steps:
-                j, h = steps[n + 3]
-                scores[n + 3] = scores_of(j, g, h)
+        for n in range(-2, total_steps + 2 + 2):
+            if 0 <= n + 2 < total_steps:
+                j, h = steps[n + 2]
+                scores[n + 2] = scores_of(j, g, h)
             if 0 <= n < total_steps:
                 weights[n] = weights_of(scores.pop(n))
             k = n - 2

time: 42.6 us -> 42.5 us (level)
  no operation moved by 1% of the time
where the time goes in v7:
time: 42.5 us; the launch traced here: 42.3 us
  starting transfers between devices  24.1 us (57%)
  Pallas kernels  10.3 us (24%)
  waiting for transfers between devices  7.02 us (17%)
  local copies, waits for them, and re-layouts  0.69 us (2%)
    ppermute x16, starting transfers between devices, swap(): return lax.ppermute(x, axis, [(i, i ^ offset) for i in range(size)])  24.1 us
    ppermute x16, waiting for transfers between devices, swap(): return lax.ppermute(x, axis, [(i, i ^ offset) for i in range(size)])  7.02 us
    pallas_call x2, Pallas kernels, attend(): pl.pallas_call(functools.partial(attend_kernel, parts, side), out_shape=[...  4.89 us
    pallas_call x1, Pallas kernels, per_device(): pl.pallas_call(prep_kernel, out_shape=[jax.ShapeDtypeStruct(early, BF)] *...  3.28 us
    pallas_call x2, Pallas kernels, project(): pl.pallas_call(functools.partial(project_kernel, parts, (inner // heads)...  0.91 us
    pallas_call x1, Pallas kernels, per_device(): pl.pallas_call(functools.partial(place_kernel, parts), out_shape=jax.Shap...  0.87 us
  transfers between devices with their start and end apart: 16, of which 3 were waited for; matrix products, arithmetic and copies ran while one was open for 0% of the time, Pallas kernels for 15%

profile of v7, /device:TPU:0, one launch (start us, length us, event | category | flops | bytes accessed | tf_op | source)
XLA Modules:
  0.0 42.3 jit_solution(17910136662662204532)
XLA Ops:
  0.0 3.3 %prep.1 = (bf16[192,128]{1,0:T(8,128)(2,1)}, bf16[192,128]{1,0:T(8,128)(2,1)}, bf16[192,128]{1,0:T(8,128)(2,1)}, bf16[192,128]{1,0:T(8,128)(2,1)}, bf16[384,128]...) custom-call(bf16[64,32,128]{2,1,0:T(8,128)(2,1)} %pair_ref.1, ...), custom_call_target="tpu_custom_call" | custom-call | tf_op jit(solution)/shard_map/prep/pallas_call | solution.py:415
  3.3 5.1 %collective-permute-start = (bf16[192,128]{1,0:T(8,128)(2,1)}, bf16[192,128]{1,0:T(8,128)(2,1)S(1)}, u32[]{:S(2)}, u32[]{:S(2)}) collective-permute-start(bf16[192,128]{1,0:T(8,128)(2,1)} %get-tuple-element.69), channel_id=1, source_target_pairs={{0,24},{8,16},{16,8},{24,0},{1,25},{9,17},{17,9},{25,1},{2,26},{10... | collective-permute-start | bytes 147464 | tf_op jit(solution)/shard_map/ppermute | solution.py:409
  8.4 0.6 %collective-permute-start.2 = (bf16[192,128]{1,0:T(8,128)(2,1)}, bf16[192,128]{1,0:T(8,128)(2,1)S(1)}, u32[]{:S(2)}, u32[]{:S(2)}) collective-permute-start(bf16[192,128]{1,0:T(8,128)(2,1)} %get-tuple-element.71), channel_id=1, source_target_pairs={{0,8},{8,0},{16,24},{24,16},{1,9},{9,1},{17,25},{25,17},{2,10},{10... | collective-permute-start | bytes 147464 | tf_op jit(solution)/shard_map/ppermute | solution.py:409
  9.1 0.6 %copy-done.4 = s32[256]{0:T(256)S(1)} copy-done((s32[256]{0:T(256)S(1)}, s32[256]{0:T(256)}, u32[]{:S(2)}) %copy-start.4) | copy-done | bytes 1048
  9.7 0.4 constants.1
  10.1 3.8 %collective-permute-start.6 = (bf16[384,128]{1,0:T(8,128)(2,1)}, bf16[384,128]{1,0:T(8,128)(2,1)S(1)}, u32[]{:S(2)}, u32[]{:S(2)}) collective-permute-start(bf16[384,128]{1,0:T(8,128)(2,1)} %get-tuple-element.83), channel_id=1, source_target_pairs={{0,24},{8,16},{16,8},{24,0},{1,25},{9,17},{17,9},{25,1},{2,26},{10... | collective-permute-start | bytes 294920 | tf_op jit(solution)/shard_map/ppermute | solution.py:409
  14.0 0.7 %collective-permute-start.8 = (bf16[384,128]{1,0:T(8,128)(2,1)S(1)}, bf16[384,128]{1,0:T(8,128)(2,1)S(1)}, u32[]{:S(2)}, u32[]{:S(2)}) collective-permute-start(bf16[384,128]{1,0:T(8,128)(2,1)S(1)} %copy-done.8), channel_id=1, source_target_pairs={{0,8},{8,0},{16,24},{24,16},{1,9},{9,1},{17,25},{25,17},{2,10},{10... | collective-permute-start | bytes 294920 | tf_op jit(solution)/shard_map/ppermute | solution.py:409
  14.8 2.7 %collective-permute-start.3 = (bf16[4,1,64,128]{3,2,0,1:T(8,128)(2,1)S(1)}, bf16[4,1,64,128]{3,2,0,1:T(8,128)(2,1)S(1)}, u32[]{:S(2)}, u32[]{:S(2)}) collective-permute-start(bf16[4,1,64,128]{3,2,0,1:T(8,128)(2,1)S(1)} %get-tuple-element.110), channel_id=1, source_target_pairs={{0,6},{1,7},{2,4},{3,5},{4,2},{5,3},{6,0},{7,1},{8,14},{9,15},{10,... | collective-permute-start | bytes 196616 | tf_op jit(solution)/shard_map/ppermute | solution.py:409
  17.4 0.5 %collective-permute-start.4 = (bf16[4,1,64,128]{3,2,0,1:T(8,128)(2,1)S(1)}, bf16[4,1,64,128]{3,2,0,1:T(8,128)(2,1)S(1)}, u32[]{:S(2)}, u32[]{:S(2)}) collective-permute-start(bf16[4,1,64,128]{3,2,0,1:T(8,128)(2,1)S(1)} %get-tuple-element.110), channel_id=1, source_target_pairs={{0,4},{1,5},{2,6},{3,7},{4,0},{5,1},{6,2},{7,3},{8,12},{9,13},{10,... | collective-permute-start | bytes 196616 | tf_op jit(solution)/shard_map/ppermute | solution.py:409
  18.0 1.6 %collective-permute-start.5 = (bf16[4,1,64,128]{3,2,0,1:T(8,128)(2,1)S(1)}, bf16[4,1,64,128]{3,2,0,1:T(8,128)(2,1)S(1)}, u32[]{:S(2)}, u32[]{:S(2)}) collective-permute-start(bf16[4,1,64,128]{3,2,0,1:T(8,128)(2,1)S(1)} %get-tuple-element.110), channel_id=1, source_target_pairs={{0,2},{1,3},{2,0},{3,1},{4,6},{5,7},{6,4},{7,5},{8,10},{9,11},{10,... | collective-permute-start | bytes 196616 | tf_op jit(solution)/shard_map/ppermute | solution.py:409
  19.6 0.3 project.2
  19.9 2.1 %collective-permute-done.7.refs_2_ = bf16[384,128]{1,0:T(8,128)(2,1)S(1)} collective-permute-done((bf16[384,128]{1,0:T(8,128)(2,1)}, bf16[384,128]{1,0:T(8,128)(2,1)S(1)}, u32[]{:S(2)}, u32[]{:S(2)}) %collective-permute-start.7) | collective-permute-done | bytes 98336 | tf_op jit(solution)/shard_map/ppermute | solution.py:409
  22.1 0.6 %project.3 = (bf16[8,192,128]{2,1,0:T(8,128)(2,1)S(1)}, bf16[8,192,128]{2,1,0:T(8,128)(2,1)S(1)}, bf16[8,192,128]{2,1,0:T(8,128)(2,1)S(1)}, f32[8,192,128]{2,1,0:T(8,128)S(1)}) custom-call(bf16[384,128]{1,0:T(8,128)(2,1)S(1)} %copy-done.7, bf16[384,128]{1,0:T(8,128)(2,1)S(1)} %collective-permute-done.6.refs_1_, ...), custom_call_target="tpu_custom_call" | custom-call | flops 201326592 | bytes 2359296 | tf_op jit(solution)/shard_map/project/pallas_call | solution.py:478
  22.7 0.1 collective-permute-start.9
  22.8 2.4 %attend.3 = (bf16[32,8,128]{2,1,0:T(8,128)(2,1)S(1)}, bf16[32,8,128]{2,1,0:T(8,128)(2,1)S(1)}, bf16[32,8,128]{2,1,0:T(8,128)(2,1)S(1)}, bf16[32,8,128]{2,1,0:T(8,128)(2,1)S(1)}) custom-call(bf16[8,64,128]{2,1,0:T(8,128)(2,1)S(1)} %get-tuple-element.78.refs_0_, bf16[8,64,128]{2,1,0:T(8,128)(2,1)S(1)} %get-tuple-element.79.refs_1_, ...), custom_call_target="tpu_custom_call" | custom-call | flops 268435456 | bytes 2097152 | tf_op jit(solution)/shard_map/attend/pallas_call | solution.py:510
  25.3 3.3 %collective-permute-start.13 = (bf16[32,8,128]{2,1,0:T(8,128)(2,1)S(1)}, bf16[32,8,128]{2,1,0:T(8,128)(2,1)S(1)}, u32[]{:S(2)}, u32[]{:S(2)}) collective-permute-start(bf16[32,8,128]{2,1,0:T(8,128)(2,1)S(1)} %get-tuple-element.106), channel_id=1, source_target_pairs={{0,24},{8,16},{16,8},{24,0},{1,25},{9,17},{17,9},{25,1},{2,26},{10... | collective-permute-start | bytes 196616 | tf_op jit(solution)/shard_map/ppermute | solution.py:409
  28.6 1.0 %collective-permute-start.14 = (bf16[32,8,128]{2,1,0:T(8,128)(2,1)S(1)}, bf16[32,8,128]{2,1,0:T(8,128)(2,1)S(1)}, u32[]{:S(2)}, u32[]{:S(2)}) collective-permute-start(bf16[32,8,128]{2,1,0:T(8,128)(2,1)S(1)} %get-tuple-element.107), channel_id=1, source_target_pairs={{0,16},{8,24},{16,0},{24,8},{1,17},{9,25},{17,1},{25,9},{2,18},{10... | collective-permute-start | bytes 196616 | tf_op jit(solution)/shard_map/ppermute | solution.py:409
  29.6 0.2 collective-permute-start.15
  29.7 2.4 %attend.2 = (bf16[32,8,128]{2,1,0:T(8,128)(2,1)S(1)}, bf16[32,8,128]{2,1,0:T(8,128)(2,1)S(1)}, bf16[32,8,128]{2,1,0:T(8,128)(2,1)S(1)}, bf16[32,8,128]{2,1,0:T(8,128)(2,1)S(1)}) custom-call(bf16[8,64,128]{2,1,0:T(8,128)(2,1)S(1)} %get-tuple-element.78.refs_0_, bf16[8,64,128]{2,1,0:T(8,128)(2,1)S(1)} %get-tuple-element.79.refs_1_, ...), custom_call_target="tpu_custom_call" | custom-call | flops 268435456 | bytes 2097152 | tf_op jit(solution)/shard_map/attend/pallas_call | solution.py:510
  32.2 3.3 %collective-permute-start.10 = (bf16[32,8,128]{2,1,0:T(8,128)(2,1)S(1)}, bf16[32,8,128]{2,1,0:T(8,128)(2,1)S(1)}, u32[]{:S(2)}, u32[]{:S(2)}) collective-permute-start(bf16[32,8,128]{2,1,0:T(8,128)(2,1)S(1)} %get-tuple-element.102), channel_id=1, source_target_pairs={{0,24},{8,16},{16,8},{24,0},{1,25},{9,17},{17,9},{25,1},{2,26},{10... | collective-permute-start | bytes 196616 | tf_op jit(solution)/shard_map/ppermute | solution.py:409
  35.6 1.0 %collective-permute-start.12 = (bf16[32,8,128]{2,1,0:T(8,128)(2,1)S(1)}, bf16[32,8,128]{2,1,0:T(8,128)(2,1)S(1)}, u32[]{:S(2)}, u32[]{:S(2)}) collective-permute-start(bf16[32,8,128]{2,1,0:T(8,128)(2,1)S(1)} %get-tuple-element.104), channel_id=1, source_target_pairs={{0,8},{8,0},{16,24},{24,16},{1,9},{9,1},{17,25},{25,17},{2,10},{10... | collective-permute-start | bytes 196616 | tf_op jit(solution)/shard_map/ppermute | solution.py:409
  36.6 2.1 %collective-permute-done.10.refs_1_ = bf16[32,8,128]{2,1,0:T(8,128)(2,1)S(1)} collective-permute-done((bf16[32,8,128]{2,1,0:T(8,128)(2,1)S(1)}, bf16[32,8,128]{2,1,0:T(8,128)(2,1)S(1)}, u32[]{:S(2)}, u32[]{:S(2)}) %collective-permute-start.10) | collective-permute-done | bytes 65568 | tf_op jit(solution)/shard_map/ppermute | solution.py:409
  38.8 2.7 %collective-permute-done.11.refs_2_ = bf16[32,8,128]{2,1,0:T(8,128)(2,1)S(1)} collective-permute-done((bf16[32,8,128]{2,1,0:T(8,128)(2,1)S(1)}, bf16[32,8,128]{2,1,0:T(8,128)(2,1)S(1)}, u32[]{:S(2)}, u32[]{:S(2)}) %collective-permute-start.11) | collective-permute-done | bytes 65568 | tf_op jit(solution)/shard_map/ppermute | solution.py:409
  41.5 0.9 %place.1 = bf16[64,32,128]{2,1,0:T(8,128)(2,1)} custom-call(bf16[32,8,128]{2,1,0:T(8,128)(2,1)S(1)} %get-tuple-element.101.refs_0_, bf16[32,8,128]{2,1,0:T(8,128)(2,1)S(1)} %collective-permute-done.10.refs_1_, bf16[32,8,128]{2,1,0:T(8,128)(2,1)S(1)} %collective-permute-done.11.refs_2_, bf16[32,8,128]{2,1,0:T(8,128)(2,1)S(1)} %collective-permute-done.12.refs_3_, ...), custom_call_target="tpu_custom_call" | custom-call | tf_op jit(solution)/shard_map/place/pallas_call | solution.py:530
  (39 shorter events, 0.2 us)
Async XLA Ops:
  0.0 9.1 %copy-start = (bf16[128,384]{1,0:T(8,128)(2,1)S(1)}, bf16[128,384]{1,0:T(8,128)(2,1)}, u32[]{:S(2)}) copy-start(bf16[128,384]{1,0:T(8,128)(2,1)} %refs_1_.1) | copy-start | bytes 294916
  0.0 9.1 %copy-start.2 = (bf16[128,128]{1,0:T(8,128)(2,1)S(1)}, bf16[128,128]{1,0:T(8,128)(2,1)}, u32[]{:S(2)}) copy-start(bf16[128,128]{1,0:T(8,128)(2,1)} %refs_2_.1) | copy-start | bytes 98308
  0.0 9.1 %copy-start.3 = (bf16[128,128]{1,0:T(8,128)(2,1)S(1)}, bf16[128,128]{1,0:T(8,128)(2,1)}, u32[]{:S(2)}) copy-start(bf16[128,128]{1,0:T(8,128)(2,1)} %refs_4_.1) | copy-start | bytes 98308
  3.3 11.4 %collective-permute-start = (bf16[192,128]{1,0:T(8,128)(2,1)}, bf16[192,128]{1,0:T(8,128)(2,1)S(1)}, u32[]{:S(2)}, u32[]{:S(2)}) collective-permute-start(bf16[192,128]{1,0:T(8,128)(2,1)} %get-tuple-element.69), channel_id=1, source_target_pairs={{0,24},{8,16},{16,8},{24,0},{1,25},{9,17},{17,9},{25,1},{2,26},{10... | collective-permute-start | bytes 147464 | tf_op jit(solution)/shard_map/ppermute | solution.py:409
  8.4 6.3 %collective-permute-start.1 = (bf16[192,128]{1,0:T(8,128)(2,1)}, bf16[192,128]{1,0:T(8,128)(2,1)S(1)}, u32[]{:S(2)}, u32[]{:S(2)}) collective-permute-start(bf16[192,128]{1,0:T(8,128)(2,1)} %get-tuple-element.70), channel_id=1, source_target_pairs={{0,16},{8,24},{16,0},{24,8},{1,17},{9,25},{17,1},{25,9},{2,18},{10... | collective-permute-start | bytes 147464 | tf_op jit(solution)/shard_map/ppermute | solution.py:409
  8.4 5.5 %collective-permute-start.2 = (bf16[192,128]{1,0:T(8,128)(2,1)}, bf16[192,128]{1,0:T(8,128)(2,1)S(1)}, u32[]{:S(2)}, u32[]{:S(2)}) collective-permute-start(bf16[192,128]{1,0:T(8,128)(2,1)} %get-tuple-element.71), channel_id=1, source_target_pairs={{0,8},{8,0},{16,24},{24,16},{1,9},{9,1},{17,25},{25,17},{2,10},{10... | collective-permute-start | bytes 147464 | tf_op jit(solution)/shard_map/ppermute | solution.py:409
  9.1 0.7 %copy-start.4 = (s32[256]{0:T(256)S(1)}, s32[256]{0:T(256)}, u32[]{:S(2)}) copy-start(s32[256]{0:T(256)} %param.11) | copy-start | bytes 3076
  9.1 0.7 %copy-start.5 = (f32[128]{0:T(128)S(1)}, f32[128]{0:T(128)}, u32[]{:S(2)}) copy-start(f32[128]{0:T(128)} %param.17) | copy-start | bytes 1540
  9.7 4.2 %copy-start.1 = (bf16[192,128]{1,0:T(8,128)(2,1)S(1)}, bf16[192,128]{1,0:T(8,128)(2,1)}, u32[]{:S(2)}) copy-start(bf16[192,128]{1,0:T(8,128)(2,1)} %get-tuple-element.68.refs_0_) | copy-start | bytes 147460
  9.7 4.2 %copy-start.8 = (bf16[384,128]{1,0:T(8,128)(2,1)S(1)}, bf16[384,128]{1,0:T(8,128)(2,1)}, u32[]{:S(2)}) copy-start(bf16[384,128]{1,0:T(8,128)(2,1)} %get-tuple-element.85) | copy-start | bytes 294916
  10.1 7.8 %collective-permute-start.6 = (bf16[384,128]{1,0:T(8,128)(2,1)}, bf16[384,128]{1,0:T(8,128)(2,1)S(1)}, u32[]{:S(2)}, u32[]{:S(2)}) collective-permute-start(bf16[384,128]{1,0:T(8,128)(2,1)} %get-tuple-element.83), channel_id=1, source_target_pairs={{0,24},{8,16},{16,8},{24,0},{1,25},{9,17},{17,9},{25,1},{2,26},{10... | collective-permute-start | bytes 294920 | tf_op jit(solution)/shard_map/ppermute | solution.py:409
  14.0 8.1 %collective-permute-start.7 = (bf16[384,128]{1,0:T(8,128)(2,1)}, bf16[384,128]{1,0:T(8,128)(2,1)S(1)}, u32[]{:S(2)}, u32[]{:S(2)}) collective-permute-start(bf16[384,128]{1,0:T(8,128)(2,1)} %get-tuple-element.84), channel_id=1, source_target_pairs={{0,16},{8,24},{16,0},{24,8},{1,17},{9,25},{17,1},{25,9},{2,18},{10... | collective-permute-start | bytes 294920 | tf_op jit(solution)/shard_map/ppermute | solution.py:409
  14.0 8.1 %collective-permute-start.8 = (bf16[384,128]{1,0:T(8,128)(2,1)S(1)}, bf16[384,128]{1,0:T(8,128)(2,1)S(1)}, u32[]{:S(2)}, u32[]{:S(2)}) collective-permute-start(bf16[384,128]{1,0:T(8,128)(2,1)S(1)} %copy-done.8), channel_id=1, source_target_pairs={{0,8},{8,0},{16,24},{24,16},{1,9},{9,1},{17,25},{25,17},{2,10},{10... | collective-permute-start | bytes 294920 | tf_op jit(solution)/shard_map/ppermute | solution.py:409
  14.7 7.3 %copy-start.7 = (bf16[384,128]{1,0:T(8,128)(2,1)S(1)}, bf16[384,128]{1,0:T(8,128)(2,1)}, u32[]{:S(2)}) copy-start(bf16[384,128]{1,0:T(8,128)(2,1)} %get-tuple-element.82.refs_0_) | copy-start | bytes 294916
  14.8 7.9 %collective-permute-start.3 = (bf16[4,1,64,128]{3,2,0,1:T(8,128)(2,1)S(1)}, bf16[4,1,64,128]{3,2,0,1:T(8,128)(2,1)S(1)}, u32[]{:S(2)}, u32[]{:S(2)}) collective-permute-start(bf16[4,1,64,128]{3,2,0,1:T(8,128)(2,1)S(1)} %get-tuple-element.110), channel_id=1, source_target_pairs={{0,6},{1,7},{2,4},{3,5},{4,2},{5,3},{6,0},{7,1},{8,14},{9,15},{10,... | collective-permute-start | bytes 196616 | tf_op jit(solution)/shard_map/ppermute | solution.py:409
  17.4 5.3 %collective-permute-start.4 = (bf16[4,1,64,128]{3,2,0,1:T(8,128)(2,1)S(1)}, bf16[4,1,64,128]{3,2,0,1:T(8,128)(2,1)S(1)}, u32[]{:S(2)}, u32[]{:S(2)}) collective-permute-start(bf16[4,1,64,128]{3,2,0,1:T(8,128)(2,1)S(1)} %get-tuple-element.110), channel_id=1, source_target_pairs={{0,4},{1,5},{2,6},{3,7},{4,0},{5,1},{6,2},{7,3},{8,12},{9,13},{10,... | collective-permute-start | bytes 196616 | tf_op jit(solution)/shard_map/ppermute | solution.py:409
  18.0 4.7 %collective-permute-start.5 = (bf16[4,1,64,128]{3,2,0,1:T(8,128)(2,1)S(1)}, bf16[4,1,64,128]{3,2,0,1:T(8,128)(2,1)S(1)}, u32[]{:S(2)}, u32[]{:S(2)}) collective-permute-start(bf16[4,1,64,128]{3,2,0,1:T(8,128)(2,1)S(1)} %get-tuple-element.110), channel_id=1, source_target_pairs={{0,2},{1,3},{2,0},{3,1},{4,6},{5,7},{6,4},{7,5},{8,10},{9,11},{10,... | collective-permute-start | bytes 196616 | tf_op jit(solution)/shard_map/ppermute | solution.py:409
  22.7 7.0 %collective-permute-start.9 = (bf16[4,4,1,64,128]{4,3,2,1,0:T(8,128)(2,1)S(1)}, bf16[4,4,1,64,128]{4,3,2,1,0:T(8,128)(2,1)S(1)}, u32[]{:S(2)}, u32[]{:S(2)}) collective-permute-start(bf16[4,4,1,64,128]{4,3,2,1,0:T(8,128)(2,1)S(1)} %pad_maximum_fusion.refs_8_), channel_id=1, source_target_pairs={{0,1},{1,0},{2,3},{3,2},{4,5},{5,4},{6,7},{7,6},{8,9},{9,8},{10,11... | collective-permute-start | bytes 786440 | tf_op jit(solution)/shard_map/ppermute | solution.py:409
  25.3 10.3 %collective-permute-start.13 = (bf16[32,8,128]{2,1,0:T(8,128)(2,1)S(1)}, bf16[32,8,128]{2,1,0:T(8,128)(2,1)S(1)}, u32[]{:S(2)}, u32[]{:S(2)}) collective-permute-start(bf16[32,8,128]{2,1,0:T(8,128)(2,1)S(1)} %get-tuple-element.106), channel_id=1, source_target_pairs={{0,24},{8,16},{16,8},{24,0},{1,25},{9,17},{17,9},{25,1},{2,26},{10... | collective-permute-start | bytes 196616 | tf_op jit(solution)/shard_map/ppermute | solution.py:409
  28.6 8.0 %collective-permute-start.14 = (bf16[32,8,128]{2,1,0:T(8,128)(2,1)S(1)}, bf16[32,8,128]{2,1,0:T(8,128)(2,1)S(1)}, u32[]{:S(2)}, u32[]{:S(2)}) collective-permute-start(bf16[32,8,128]{2,1,0:T(8,128)(2,1)S(1)} %get-tuple-element.107), channel_id=1, source_target_pairs={{0,16},{8,24},{16,0},{24,8},{1,17},{9,25},{17,1},{25,9},{2,18},{10... | collective-permute-start | bytes 196616 | tf_op jit(solution)/shard_map/ppermute | solution.py:409
  29.6 7.1 %collective-permute-start.15 = (bf16[32,8,128]{2,1,0:T(8,128)(2,1)S(1)}, bf16[32,8,128]{2,1,0:T(8,128)(2,1)S(1)}, u32[]{:S(2)}, u32[]{:S(2)}) collective-permute-start(bf16[32,8,128]{2,1,0:T(8,128)(2,1)S(1)} %get-tuple-element.108), channel_id=1, source_target_pairs={{0,8},{8,0},{16,24},{24,16},{1,9},{9,1},{17,25},{25,17},{2,10},{10... | collective-permute-start | bytes 196616 | tf_op jit(solution)/shard_map/ppermute | solution.py:409
  32.2 6.6 %collective-permute-start.10 = (bf16[32,8,128]{2,1,0:T(8,128)(2,1)S(1)}, bf16[32,8,128]{2,1,0:T(8,128)(2,1)S(1)}, u32[]{:S(2)}, u32[]{:S(2)}) collective-permute-start(bf16[32,8,128]{2,1,0:T(8,128)(2,1)S(1)} %get-tuple-element.102), channel_id=1, source_target_pairs={{0,24},{8,16},{16,8},{24,0},{1,25},{9,17},{17,9},{25,1},{2,26},{10... | collective-permute-start | bytes 196616 | tf_op jit(solution)/shard_map/ppermute | solution.py:409
  35.5 5.9 %collective-permute-start.11 = (bf16[32,8,128]{2,1,0:T(8,128)(2,1)S(1)}, bf16[32,8,128]{2,1,0:T(8,128)(2,1)S(1)}, u32[]{:S(2)}, u32[]{:S(2)}) collective-permute-start(bf16[32,8,128]{2,1,0:T(8,128)(2,1)S(1)} %get-tuple-element.103), channel_id=1, source_target_pairs={{0,16},{8,24},{16,0},{24,8},{1,17},{9,25},{17,1},{25,9},{2,18},{10... | collective-permute-start | bytes 196616 | tf_op jit(solution)/shard_map/ppermute | solution.py:409
  35.6 5.9 %collective-permute-start.12 = (bf16[32,8,128]{2,1,0:T(8,128)(2,1)S(1)}, bf16[32,8,128]{2,1,0:T(8,128)(2,1)S(1)}, u32[]{:S(2)}, u32[]{:S(2)}) collective-permute-start(bf16[32,8,128]{2,1,0:T(8,128)(2,1)S(1)} %get-tuple-element.104), channel_id=1, source_target_pairs={{0,8},{8,0},{16,24},{24,16},{1,9},{9,1},{17,25},{25,17},{2,10},{10... | collective-permute-start | bytes 196616 | tf_op jit(solution)/shard_map/ppermute | solution.py:409
  (1 other events, 0.7 us)

commit v8 on v6

--- a/solution.py
+++ b/solution.py
@@ -366,7 +366,7 @@
     width = cols // parts
     me = lax.axis_index("row")
     odd = lax.axis_index("col") & 1
-    step = min(rows // 2, 16)
+    step = min(rows // 2, 8)
     copies = []
     for side in range(2):
         for low in range(0, rows // 2, step):
@@ -534,7 +534,7 @@
         scratch_shapes=[
             pltpu.VMEM((2, rows // 2, cols, chans), F32),
             pltpu.VMEM((2, rows // 2, cols, chans), BF),
-            pltpu.SemaphoreType.DMA((2 * (rows // 2 // min(rows // 2, 16)),)),
+            pltpu.SemaphoreType.DMA((2 * (rows // 2 // min(rows // 2, 8)),)),
         ],
         compiler_params=params,
         name="place",

time: 42.6 us -> 42.6 us (level)
  no operation moved by 1% of the time
where the time goes in v8:
time: 42.6 us; the launch traced here: 42.5 us
  starting transfers between devices  24.1 us (57%)
  Pallas kernels  10.5 us (25%)
  waiting for transfers between devices  6.97 us (16%)
  local copies, waits for them, and re-layouts  0.69 us (2%)
    ppermute x16, starting transfers between devices, swap(): return lax.ppermute(x, axis, [(i, i ^ offset) for i in range(size)])  24.1 us
    ppermute x16, waiting for transfers between devices, swap(): return lax.ppermute(x, axis, [(i, i ^ offset) for i in range(size)])  6.97 us
    pallas_call x2, Pallas kernels, attend(): pl.pallas_call(functools.partial(attend_kernel, parts, side), out_shape=[...  5 us
    pallas_call x1, Pallas kernels, per_device(): pl.pallas_call(prep_kernel, out_shape=[jax.ShapeDtypeStruct(early, BF)] *...  3.35 us
    pallas_call x2, Pallas kernels, project(): pl.pallas_call(functools.partial(project_kernel, parts, (inner // heads)...  0.91 us
    pallas_call x1, Pallas kernels, per_device(): pl.pallas_call(functools.partial(place_kernel, parts), out_shape=jax.Shap...  0.87 us
  transfers between devices with their start and end apart: 16, of which 3 were waited for; matrix products, arithmetic and copies ran while one was open for 0% of the time, Pallas kernels for 15%

profile of v8, /device:TPU:0, one launch (start us, length us, event | category | flops | bytes accessed | tf_op | source)
XLA Modules:
  0.0 42.5 jit_solution(17472563692411121740)
XLA Ops:
  0.0 3.3 %prep.1 = (bf16[192,128]{1,0:T(8,128)(2,1)}, bf16[192,128]{1,0:T(8,128)(2,1)}, bf16[192,128]{1,0:T(8,128)(2,1)}, bf16[192,128]{1,0:T(8,128)(2,1)}, bf16[384,128]...) custom-call(bf16[64,32,128]{2,1,0:T(8,128)(2,1)} %pair_ref.1, ...), custom_call_target="tpu_custom_call" | custom-call | tf_op jit(solution)/shard_map/prep/pallas_call | solution.py:414
  3.4 5.1 %collective-permute-start = (bf16[192,128]{1,0:T(8,128)(2,1)}, bf16[192,128]{1,0:T(8,128)(2,1)S(1)}, u32[]{:S(2)}, u32[]{:S(2)}) collective-permute-start(bf16[192,128]{1,0:T(8,128)(2,1)} %get-tuple-element.69), channel_id=1, source_target_pairs={{0,24},{8,16},{16,8},{24,0},{1,25},{9,17},{17,9},{25,1},{2,26},{10... | collective-permute-start | bytes 147464 | tf_op jit(solution)/shard_map/ppermute | solution.py:408
  8.5 0.6 %collective-permute-start.2 = (bf16[192,128]{1,0:T(8,128)(2,1)}, bf16[192,128]{1,0:T(8,128)(2,1)S(1)}, u32[]{:S(2)}, u32[]{:S(2)}) collective-permute-start(bf16[192,128]{1,0:T(8,128)(2,1)} %get-tuple-element.71), channel_id=1, source_target_pairs={{0,8},{8,0},{16,24},{24,16},{1,9},{9,1},{17,25},{25,17},{2,10},{10... | collective-permute-start | bytes 147464 | tf_op jit(solution)/shard_map/ppermute | solution.py:408
  9.2 0.6 %copy-done.4 = s32[256]{0:T(256)S(1)} copy-done((s32[256]{0:T(256)S(1)}, s32[256]{0:T(256)}, u32[]{:S(2)}) %copy-start.4) | copy-done | bytes 1048
  9.8 0.4 constants.1
  10.2 3.8 %collective-permute-start.6 = (bf16[384,128]{1,0:T(8,128)(2,1)}, bf16[384,128]{1,0:T(8,128)(2,1)S(1)}, u32[]{:S(2)}, u32[]{:S(2)}) collective-permute-start(bf16[384,128]{1,0:T(8,128)(2,1)} %get-tuple-element.83), channel_id=1, source_target_pairs={{0,24},{8,16},{16,8},{24,0},{1,25},{9,17},{17,9},{25,1},{2,26},{10... | collective-permute-start | bytes 294920 | tf_op jit(solution)/shard_map/ppermute | solution.py:408
  14.1 0.7 %collective-permute-start.8 = (bf16[384,128]{1,0:T(8,128)(2,1)S(1)}, bf16[384,128]{1,0:T(8,128)(2,1)S(1)}, u32[]{:S(2)}, u32[]{:S(2)}) collective-permute-start(bf16[384,128]{1,0:T(8,128)(2,1)S(1)} %copy-done.8), channel_id=1, source_target_pairs={{0,8},{8,0},{16,24},{24,16},{1,9},{9,1},{17,25},{25,17},{2,10},{10... | collective-permute-start | bytes 294920 | tf_op jit(solution)/shard_map/ppermute | solution.py:408
  14.8 2.7 %collective-permute-start.3 = (bf16[4,1,64,128]{3,2,0,1:T(8,128)(2,1)S(1)}, bf16[4,1,64,128]{3,2,0,1:T(8,128)(2,1)S(1)}, u32[]{:S(2)}, u32[]{:S(2)}) collective-permute-start(bf16[4,1,64,128]{3,2,0,1:T(8,128)(2,1)S(1)} %get-tuple-element.110), channel_id=1, source_target_pairs={{0,6},{1,7},{2,4},{3,5},{4,2},{5,3},{6,0},{7,1},{8,14},{9,15},{10,... | collective-permute-start | bytes 196616 | tf_op jit(solution)/shard_map/ppermute | solution.py:408
  17.5 0.5 %collective-permute-start.4 = (bf16[4,1,64,128]{3,2,0,1:T(8,128)(2,1)S(1)}, bf16[4,1,64,128]{3,2,0,1:T(8,128)(2,1)S(1)}, u32[]{:S(2)}, u32[]{:S(2)}) collective-permute-start(bf16[4,1,64,128]{3,2,0,1:T(8,128)(2,1)S(1)} %get-tuple-element.110), channel_id=1, source_target_pairs={{0,4},{1,5},{2,6},{3,7},{4,0},{5,1},{6,2},{7,3},{8,12},{9,13},{10,... | collective-permute-start | bytes 196616 | tf_op jit(solution)/shard_map/ppermute | solution.py:408
  18.0 1.6 %collective-permute-start.5 = (bf16[4,1,64,128]{3,2,0,1:T(8,128)(2,1)S(1)}, bf16[4,1,64,128]{3,2,0,1:T(8,128)(2,1)S(1)}, u32[]{:S(2)}, u32[]{:S(2)}) collective-permute-start(bf16[4,1,64,128]{3,2,0,1:T(8,128)(2,1)S(1)} %get-tuple-element.110), channel_id=1, source_target_pairs={{0,2},{1,3},{2,0},{3,1},{4,6},{5,7},{6,4},{7,5},{8,10},{9,11},{10,... | collective-permute-start | bytes 196616 | tf_op jit(solution)/shard_map/ppermute | solution.py:408
  19.7 0.3 project.2
  20.0 2.1 %collective-permute-done.7.refs_2_ = bf16[384,128]{1,0:T(8,128)(2,1)S(1)} collective-permute-done((bf16[384,128]{1,0:T(8,128)(2,1)}, bf16[384,128]{1,0:T(8,128)(2,1)S(1)}, u32[]{:S(2)}, u32[]{:S(2)}) %collective-permute-start.7) | collective-permute-done | bytes 98336 | tf_op jit(solution)/shard_map/ppermute | solution.py:408
  22.1 0.6 %project.3 = (bf16[8,192,128]{2,1,0:T(8,128)(2,1)S(1)}, bf16[8,192,128]{2,1,0:T(8,128)(2,1)S(1)}, bf16[8,192,128]{2,1,0:T(8,128)(2,1)S(1)}, f32[8,192,128]{2,1,0:T(8,128)S(1)}) custom-call(bf16[384,128]{1,0:T(8,128)(2,1)S(1)} %copy-done.7, bf16[384,128]{1,0:T(8,128)(2,1)S(1)} %collective-permute-done.6.refs_1_, ...), custom_call_target="tpu_custom_call" | custom-call | flops 201326592 | bytes 2359296 | tf_op jit(solution)/shard_map/project/pallas_call | solution.py:477
  22.9 2.5 %attend.3 = (bf16[32,8,128]{2,1,0:T(8,128)(2,1)S(1)}, bf16[32,8,128]{2,1,0:T(8,128)(2,1)S(1)}, bf16[32,8,128]{2,1,0:T(8,128)(2,1)S(1)}, bf16[32,8,128]{2,1,0:T(8,128)(2,1)S(1)}) custom-call(bf16[8,64,128]{2,1,0:T(8,128)(2,1)S(1)} %get-tuple-element.78.refs_0_, bf16[8,64,128]{2,1,0:T(8,128)(2,1)S(1)} %get-tuple-element.79.refs_1_, ...), custom_call_target="tpu_custom_call" | custom-call | flops 268435456 | bytes 2097152 | tf_op jit(solution)/shard_map/attend/pallas_call | solution.py:509
  25.4 3.3 %collective-permute-start.13 = (bf16[32,8,128]{2,1,0:T(8,128)(2,1)S(1)}, bf16[32,8,128]{2,1,0:T(8,128)(2,1)S(1)}, u32[]{:S(2)}, u32[]{:S(2)}) collective-permute-start(bf16[32,8,128]{2,1,0:T(8,128)(2,1)S(1)} %get-tuple-element.106), channel_id=1, source_target_pairs={{0,24},{8,16},{16,8},{24,0},{1,25},{9,17},{17,9},{25,1},{2,26},{10... | collective-permute-start | bytes 196616 | tf_op jit(solution)/shard_map/ppermute | solution.py:408
  28.7 1.0 %collective-permute-start.14 = (bf16[32,8,128]{2,1,0:T(8,128)(2,1)S(1)}, bf16[32,8,128]{2,1,0:T(8,128)(2,1)S(1)}, u32[]{:S(2)}, u32[]{:S(2)}) collective-permute-start(bf16[32,8,128]{2,1,0:T(8,128)(2,1)S(1)} %get-tuple-element.107), channel_id=1, source_target_pairs={{0,16},{8,24},{16,0},{24,8},{1,17},{9,25},{17,1},{25,9},{2,18},{10... | collective-permute-start | bytes 196616 | tf_op jit(solution)/shard_map/ppermute | solution.py:408
  29.7 0.2 collective-permute-start.15
  29.9 2.5 %attend.2 = (bf16[32,8,128]{2,1,0:T(8,128)(2,1)S(1)}, bf16[32,8,128]{2,1,0:T(8,128)(2,1)S(1)}, bf16[32,8,128]{2,1,0:T(8,128)(2,1)S(1)}, bf16[32,8,128]{2,1,0:T(8,128)(2,1)S(1)}) custom-call(bf16[8,64,128]{2,1,0:T(8,128)(2,1)S(1)} %get-tuple-element.78.refs_0_, bf16[8,64,128]{2,1,0:T(8,128)(2,1)S(1)} %get-tuple-element.79.refs_1_, ...), custom_call_target="tpu_custom_call" | custom-call | flops 268435456 | bytes 2097152 | tf_op jit(solution)/shard_map/attend/pallas_call | solution.py:509
  32.4 3.3 %collective-permute-start.10 = (bf16[32,8,128]{2,1,0:T(8,128)(2,1)S(1)}, bf16[32,8,128]{2,1,0:T(8,128)(2,1)S(1)}, u32[]{:S(2)}, u32[]{:S(2)}) collective-permute-start(bf16[32,8,128]{2,1,0:T(8,128)(2,1)S(1)} %get-tuple-element.102), channel_id=1, source_target_pairs={{0,24},{8,16},{16,8},{24,0},{1,25},{9,17},{17,9},{25,1},{2,26},{10... | collective-permute-start | bytes 196616 | tf_op jit(solution)/shard_map/ppermute | solution.py:408
  35.7 0.1 collective-permute-start.11
  35.8 1.1 %collective-permute-start.12 = (bf16[32,8,128]{2,1,0:T(8,128)(2,1)S(1)}, bf16[32,8,128]{2,1,0:T(8,128)(2,1)S(1)}, u32[]{:S(2)}, u32[]{:S(2)}) collective-permute-start(bf16[32,8,128]{2,1,0:T(8,128)(2,1)S(1)} %get-tuple-element.104), channel_id=1, source_target_pairs={{0,8},{8,0},{16,24},{24,16},{1,9},{9,1},{17,25},{25,17},{2,10},{10... | collective-permute-start | bytes 196616 | tf_op jit(solution)/shard_map/ppermute | solution.py:408
  36.8 2.2 %collective-permute-done.10.refs_1_ = bf16[32,8,128]{2,1,0:T(8,128)(2,1)S(1)} collective-permute-done((bf16[32,8,128]{2,1,0:T(8,128)(2,1)S(1)}, bf16[32,8,128]{2,1,0:T(8,128)(2,1)S(1)}, u32[]{:S(2)}, u32[]{:S(2)}) %collective-permute-start.10) | collective-permute-done | bytes 65568 | tf_op jit(solution)/shard_map/ppermute | solution.py:408
  39.0 2.6 %collective-permute-done.11.refs_2_ = bf16[32,8,128]{2,1,0:T(8,128)(2,1)S(1)} collective-permute-done((bf16[32,8,128]{2,1,0:T(8,128)(2,1)S(1)}, bf16[32,8,128]{2,1,0:T(8,128)(2,1)S(1)}, u32[]{:S(2)}, u32[]{:S(2)}) %collective-permute-start.11) | collective-permute-done | bytes 65568 | tf_op jit(solution)/shard_map/ppermute | solution.py:408
  41.6 0.9 %place.1 = bf16[64,32,128]{2,1,0:T(8,128)(2,1)} custom-call(bf16[32,8,128]{2,1,0:T(8,128)(2,1)S(1)} %get-tuple-element.101.refs_0_, bf16[32,8,128]{2,1,0:T(8,128)(2,1)S(1)} %collective-permute-done.10.refs_1_, bf16[32,8,128]{2,1,0:T(8,128)(2,1)S(1)} %collective-permute-done.11.refs_2_, bf16[32,8,128]{2,1,0:T(8,128)(2,1)S(1)} %collective-permute-done.12.refs_3_, ...), custom_call_target="tpu_custom_call" | custom-call | tf_op jit(solution)/shard_map/place/pallas_call | solution.py:529
  (39 shorter events, 0.2 us)
Async XLA Ops:
  0.0 9.1 %copy-start = (bf16[128,384]{1,0:T(8,128)(2,1)S(1)}, bf16[128,384]{1,0:T(8,128)(2,1)}, u32[]{:S(2)}) copy-start(bf16[128,384]{1,0:T(8,128)(2,1)} %refs_1_.1) | copy-start | bytes 294916
  0.0 9.1 %copy-start.2 = (bf16[128,128]{1,0:T(8,128)(2,1)S(1)}, bf16[128,128]{1,0:T(8,128)(2,1)}, u32[]{:S(2)}) copy-start(bf16[128,128]{1,0:T(8,128)(2,1)} %refs_2_.1) | copy-start | bytes 98308
  0.0 9.1 %copy-start.3 = (bf16[128,128]{1,0:T(8,128)(2,1)S(1)}, bf16[128,128]{1,0:T(8,128)(2,1)}, u32[]{:S(2)}) copy-start(bf16[128,128]{1,0:T(8,128)(2,1)} %refs_4_.1) | copy-start | bytes 98308
  3.4 11.4 %collective-permute-start = (bf16[192,128]{1,0:T(8,128)(2,1)}, bf16[192,128]{1,0:T(8,128)(2,1)S(1)}, u32[]{:S(2)}, u32[]{:S(2)}) collective-permute-start(bf16[192,128]{1,0:T(8,128)(2,1)} %get-tuple-element.69), channel_id=1, source_target_pairs={{0,24},{8,16},{16,8},{24,0},{1,25},{9,17},{17,9},{25,1},{2,26},{10... | collective-permute-start | bytes 147464 | tf_op jit(solution)/shard_map/ppermute | solution.py:408
  8.5 6.3 %collective-permute-start.1 = (bf16[192,128]{1,0:T(8,128)(2,1)}, bf16[192,128]{1,0:T(8,128)(2,1)S(1)}, u32[]{:S(2)}, u32[]{:S(2)}) collective-permute-start(bf16[192,128]{1,0:T(8,128)(2,1)} %get-tuple-element.70), channel_id=1, source_target_pairs={{0,16},{8,24},{16,0},{24,8},{1,17},{9,25},{17,1},{25,9},{2,18},{10... | collective-permute-start | bytes 147464 | tf_op jit(solution)/shard_map/ppermute | solution.py:408
  8.5 5.5 %collective-permute-start.2 = (bf16[192,128]{1,0:T(8,128)(2,1)}, bf16[192,128]{1,0:T(8,128)(2,1)S(1)}, u32[]{:S(2)}, u32[]{:S(2)}) collective-permute-start(bf16[192,128]{1,0:T(8,128)(2,1)} %get-tuple-element.71), channel_id=1, source_target_pairs={{0,8},{8,0},{16,24},{24,16},{1,9},{9,1},{17,25},{25,17},{2,10},{10... | collective-permute-start | bytes 147464 | tf_op jit(solution)/shard_map/ppermute | solution.py:408
  9.1 0.7 %copy-start.4 = (s32[256]{0:T(256)S(1)}, s32[256]{0:T(256)}, u32[]{:S(2)}) copy-start(s32[256]{0:T(256)} %param.11) | copy-start | bytes 3076
  9.1 0.7 %copy-start.5 = (f32[128]{0:T(128)S(1)}, f32[128]{0:T(128)}, u32[]{:S(2)}) copy-start(f32[128]{0:T(128)} %param.17) | copy-start | bytes 1540
  9.8 4.2 %copy-start.1 = (bf16[192,128]{1,0:T(8,128)(2,1)S(1)}, bf16[192,128]{1,0:T(8,128)(2,1)}, u32[]{:S(2)}) copy-start(bf16[192,128]{1,0:T(8,128)(2,1)} %get-tuple-element.68.refs_0_) | copy-start | bytes 147460
  9.8 4.2 %copy-start.8 = (bf16[384,128]{1,0:T(8,128)(2,1)S(1)}, bf16[384,128]{1,0:T(8,128)(2,1)}, u32[]{:S(2)}) copy-start(bf16[384,128]{1,0:T(8,128)(2,1)} %get-tuple-element.85) | copy-start | bytes 294916
  10.2 7.8 %collective-permute-start.6 = (bf16[384,128]{1,0:T(8,128)(2,1)}, bf16[384,128]{1,0:T(8,128)(2,1)S(1)}, u32[]{:S(2)}, u32[]{:S(2)}) collective-permute-start(bf16[384,128]{1,0:T(8,128)(2,1)} %get-tuple-element.83), channel_id=1, source_target_pairs={{0,24},{8,16},{16,8},{24,0},{1,25},{9,17},{17,9},{25,1},{2,26},{10... | collective-permute-start | bytes 294920 | tf_op jit(solution)/shard_map/ppermute | solution.py:408
  14.0 8.1 %collective-permute-start.7 = (bf16[384,128]{1,0:T(8,128)(2,1)}, bf16[384,128]{1,0:T(8,128)(2,1)S(1)}, u32[]{:S(2)}, u32[]{:S(2)}) collective-permute-start(bf16[384,128]{1,0:T(8,128)(2,1)} %get-tuple-element.84), channel_id=1, source_target_pairs={{0,16},{8,24},{16,0},{24,8},{1,17},{9,25},{17,1},{25,9},{2,18},{10... | collective-permute-start | bytes 294920 | tf_op jit(solution)/shard_map/ppermute | solution.py:408
  14.1 8.1 %collective-permute-start.8 = (bf16[384,128]{1,0:T(8,128)(2,1)S(1)}, bf16[384,128]{1,0:T(8,128)(2,1)S(1)}, u32[]{:S(2)}, u32[]{:S(2)}) collective-permute-start(bf16[384,128]{1,0:T(8,128)(2,1)S(1)} %copy-done.8), channel_id=1, source_target_pairs={{0,8},{8,0},{16,24},{24,16},{1,9},{9,1},{17,25},{25,17},{2,10},{10... | collective-permute-start | bytes 294920 | tf_op jit(solution)/shard_map/ppermute | solution.py:408
  14.8 7.3 %copy-start.7 = (bf16[384,128]{1,0:T(8,128)(2,1)S(1)}, bf16[384,128]{1,0:T(8,128)(2,1)}, u32[]{:S(2)}) copy-start(bf16[384,128]{1,0:T(8,128)(2,1)} %get-tuple-element.82.refs_0_) | copy-start | bytes 294916
  14.8 7.9 %collective-permute-start.3 = (bf16[4,1,64,128]{3,2,0,1:T(8,128)(2,1)S(1)}, bf16[4,1,64,128]{3,2,0,1:T(8,128)(2,1)S(1)}, u32[]{:S(2)}, u32[]{:S(2)}) collective-permute-start(bf16[4,1,64,128]{3,2,0,1:T(8,128)(2,1)S(1)} %get-tuple-element.110), channel_id=1, source_target_pairs={{0,6},{1,7},{2,4},{3,5},{4,2},{5,3},{6,0},{7,1},{8,14},{9,15},{10,... | collective-permute-start | bytes 196616 | tf_op jit(solution)/shard_map/ppermute | solution.py:408
  17.5 5.3 %collective-permute-start.4 = (bf16[4,1,64,128]{3,2,0,1:T(8,128)(2,1)S(1)}, bf16[4,1,64,128]{3,2,0,1:T(8,128)(2,1)S(1)}, u32[]{:S(2)}, u32[]{:S(2)}) collective-permute-start(bf16[4,1,64,128]{3,2,0,1:T(8,128)(2,1)S(1)} %get-tuple-element.110), channel_id=1, source_target_pairs={{0,4},{1,5},{2,6},{3,7},{4,0},{5,1},{6,2},{7,3},{8,12},{9,13},{10,... | collective-permute-start | bytes 196616 | tf_op jit(solution)/shard_map/ppermute | solution.py:408
  18.0 4.7 %collective-permute-start.5 = (bf16[4,1,64,128]{3,2,0,1:T(8,128)(2,1)S(1)}, bf16[4,1,64,128]{3,2,0,1:T(8,128)(2,1)S(1)}, u32[]{:S(2)}, u32[]{:S(2)}) collective-permute-start(bf16[4,1,64,128]{3,2,0,1:T(8,128)(2,1)S(1)} %get-tuple-element.110), channel_id=1, source_target_pairs={{0,2},{1,3},{2,0},{3,1},{4,6},{5,7},{6,4},{7,5},{8,10},{9,11},{10,... | collective-permute-start | bytes 196616 | tf_op jit(solution)/shard_map/ppermute | solution.py:408
  22.8 7.0 %collective-permute-start.9 = (bf16[4,4,1,64,128]{4,3,2,1,0:T(8,128)(2,1)S(1)}, bf16[4,4,1,64,128]{4,3,2,1,0:T(8,128)(2,1)S(1)}, u32[]{:S(2)}, u32[]{:S(2)}) collective-permute-start(bf16[4,4,1,64,128]{4,3,2,1,0:T(8,128)(2,1)S(1)} %pad_maximum_fusion.refs_8_), channel_id=1, source_target_pairs={{0,1},{1,0},{2,3},{3,2},{4,5},{5,4},{6,7},{7,6},{8,9},{9,8},{10,11... | collective-permute-start | bytes 786440 | tf_op jit(solution)/shard_map/ppermute | solution.py:408
  25.4 10.4 %collective-permute-start.13 = (bf16[32,8,128]{2,1,0:T(8,128)(2,1)S(1)}, bf16[32,8,128]{2,1,0:T(8,128)(2,1)S(1)}, u32[]{:S(2)}, u32[]{:S(2)}) collective-permute-start(bf16[32,8,128]{2,1,0:T(8,128)(2,1)S(1)} %get-tuple-element.106), channel_id=1, source_target_pairs={{0,24},{8,16},{16,8},{24,0},{1,25},{9,17},{17,9},{25,1},{2,26},{10... | collective-permute-start | bytes 196616 | tf_op jit(solution)/shard_map/ppermute | solution.py:408
  28.7 8.1 %collective-permute-start.14 = (bf16[32,8,128]{2,1,0:T(8,128)(2,1)S(1)}, bf16[32,8,128]{2,1,0:T(8,128)(2,1)S(1)}, u32[]{:S(2)}, u32[]{:S(2)}) collective-permute-start(bf16[32,8,128]{2,1,0:T(8,128)(2,1)S(1)} %get-tuple-element.107), channel_id=1, source_target_pairs={{0,16},{8,24},{16,0},{24,8},{1,17},{9,25},{17,1},{25,9},{2,18},{10... | collective-permute-start | bytes 196616 | tf_op jit(solution)/shard_map/ppermute | solution.py:408
  29.7 7.1 %collective-permute-start.15 = (bf16[32,8,128]{2,1,0:T(8,128)(2,1)S(1)}, bf16[32,8,128]{2,1,0:T(8,128)(2,1)S(1)}, u32[]{:S(2)}, u32[]{:S(2)}) collective-permute-start(bf16[32,8,128]{2,1,0:T(8,128)(2,1)S(1)} %get-tuple-element.108), channel_id=1, source_target_pairs={{0,8},{8,0},{16,24},{24,16},{1,9},{9,1},{17,25},{25,17},{2,10},{10... | collective-permute-start | bytes 196616 | tf_op jit(solution)/shard_map/ppermute | solution.py:408
  32.4 6.6 %collective-permute-start.10 = (bf16[32,8,128]{2,1,0:T(8,128)(2,1)S(1)}, bf16[32,8,128]{2,1,0:T(8,128)(2,1)S(1)}, u32[]{:S(2)}, u32[]{:S(2)}) collective-permute-start(bf16[32,8,128]{2,1,0:T(8,128)(2,1)S(1)} %get-tuple-element.102), channel_id=1, source_target_pairs={{0,24},{8,16},{16,8},{24,0},{1,25},{9,17},{17,9},{25,1},{2,26},{10... | collective-permute-start | bytes 196616 | tf_op jit(solution)/shard_map/ppermute | solution.py:408
  35.7 5.9 %collective-permute-start.11 = (bf16[32,8,128]{2,1,0:T(8,128)(2,1)S(1)}, bf16[32,8,128]{2,1,0:T(8,128)(2,1)S(1)}, u32[]{:S(2)}, u32[]{:S(2)}) collective-permute-start(bf16[32,8,128]{2,1,0:T(8,128)(2,1)S(1)} %get-tuple-element.103), channel_id=1, source_target_pairs={{0,16},{8,24},{16,0},{24,8},{1,17},{9,25},{17,1},{25,9},{2,18},{10... | collective-permute-start | bytes 196616 | tf_op jit(solution)/shard_map/ppermute | solution.py:408
  35.8 5.8 %collective-permute-start.12 = (bf16[32,8,128]{2,1,0:T(8,128)(2,1)S(1)}, bf16[32,8,128]{2,1,0:T(8,128)(2,1)S(1)}, u32[]{:S(2)}, u32[]{:S(2)}) collective-permute-start(bf16[32,8,128]{2,1,0:T(8,128)(2,1)S(1)} %get-tuple-element.104), channel_id=1, source_target_pairs={{0,8},{8,0},{16,24},{24,16},{1,9},{9,1},{17,25},{25,17},{2,10},{10... | collective-permute-start | bytes 196616 | tf_op jit(solution)/shard_map/ppermute | solution.py:408
  (1 other events, 0.7 us)
